TPU v7x, 32 devices: a whole 2x2x4 slice. The times are simulated.
32 devices in a mesh: aisle: 4 (over x, core), row: 8 (over z, y).
Axes of the slice: x: 2, y: 2, z: 4, core: 2. Of those that a mesh axis runs over, the one named last changes fastest.
Arguments:
- source: float32 [8, 128, 512], P(None, 'row', 'aisle'), may hold values from -6 to 6
- conduct: float32 [8, 128, 512], P(None, 'row', 'aisle'), may hold values from 1 to 10
- solid: int32 [8, 128, 512], P(None, 'row', 'aisle'), may hold values 0 or 1
Outputs:
- correction: float32 [8, 128, 512], P(None, 'row', 'aisle')
All inputs are finite; a program needn't handle non-finite values. No bound on the sum of `solid` on one device may be relied on, other than what follows from the above.
Results may differ from a plain program's by a relative error of at most 0.0003.
Values sent between devices are 32-bit elements; how exact they have to be, the bound alone decides.
No kernel may reach another device: no remote copies, remote signals or barrier semaphores. Data moves between devices by JAX's collectives and lax.ppermute only.
A program may use at most 64 MiB of HBM per device.

v0:
```python
import jax
import jax.numpy as jnp
from jax import lax
from jax.sharding import PartitionSpec as P

OV = 2
SWEEPS = 6


lower_end = 0.2
upper_end = 2.0


def shifted(block, axis, distance):
    devices = range(lax.axis_size(axis))
    route = [((i - distance) % len(devices), i) for i in devices]
    return lax.ppermute(block, axis, route)


def from_behind(shard, axis, by):
    count = lax.axis_size(axis)
    pairs = [(i, i + by) for i in range(count) if 0 <= i + by < count]
    return lax.ppermute(shard, axis, pairs)


def extended_2(block, sides, width):
    for axis, dim in sides:
        count = lax.axis_size(axis)
        forward = [(i, i + 1) for i in range(count - 1)]
        forward.append((count - 1, 0))
        backward = [(target, source) for source, target in forward]
        low = lax.ppermute(
            lax.slice_in_dim(block, block.shape[dim] - width, None, axis=dim), axis, forward
        )
        high = lax.ppermute(lax.slice_in_dim(block, 0, width, axis=dim), axis, backward)
        block = jnp.concatenate([low, block, high], axis=dim)
    return block


def padded(values):
    return jnp.pad(values, [(0, 0)] * (values.ndim - 3) + [(1, 1)] * 3)


def beside(padded_values):
    return [
        padded_values[..., 2:, 1:-1, 1:-1],
        padded_values[..., :-2, 1:-1, 1:-1],
        padded_values[..., 1:-1, 2:, 1:-1],
        padded_values[..., 1:-1, :-2, 1:-1],
        padded_values[..., 1:-1, 1:-1, 2:],
        padded_values[..., 1:-1, 1:-1, :-2],
    ]


def coupling(padded_cond, shift_term):
    centre = padded_cond[..., 1:-1, 1:-1, 1:-1]
    weights = [0.5 * (centre + other) for other in beside(padded_cond)]
    diagonal = shift_term
    for weight in weights:
        diagonal = diagonal + weight
    return (weights, diagonal)


def operate(padded_values, weights, diagonal):
    others = beside(padded_values)
    summed = weights[0] * others[0]
    for number in range(1, 6):
        summed = summed + weights[number] * others[number]
    return diagonal * padded_values[..., 1:-1, 1:-1, 1:-1] - summed


def smooth_local(source_ext, weights, diagonal):
    middle = 0.5 * (upper_end + lower_end)
    spread = 0.5 * (upper_end - lower_end)
    ratio_now = spread / middle
    inverse = 1.0 / diagonal
    update = inverse * source_ext / middle
    estimate = update
    for sweep_no in range(SWEEPS):
        remain = source_ext - operate(padded(estimate), weights, diagonal)
        ratio_next = 1.0 / (2.0 * middle / spread - ratio_now)
        update = ratio_next * ratio_now * update + 2.0 * ratio_next / spread * inverse * remain
        estimate = estimate + update
        ratio_now = ratio_next
    return estimate


def aisle_pass(slab, offset):
    return shifted(slab, "aisle", offset)


def row_pass(slab, offset):
    return from_behind(slab, "row", offset)


def fold_aisle(result):
    inner = result[..., OV:-OV]
    from_lower = aisle_pass(result[..., -OV:], 1)
    from_upper = aisle_pass(result[..., :OV], -1)
    return jnp.concatenate(
        [inner[..., :OV] + from_lower, inner[..., OV:-OV], inner[..., -OV:] + from_upper], axis=2
    )


def fold_row(result):
    inner = result[:, OV:-OV, :]
    from_lower = row_pass(result[:, -OV:, :], 1)
    from_upper = row_pass(result[:, :OV, :], -1)
    return jnp.concatenate(
        [inner[:, :OV, :] + from_lower, inner[:, OV:-OV, :], inner[:, -OV:, :] + from_upper], axis=1
    )


def schwarz_apply(source_core, weights, diagonal):
    source_ext = jnp.pad(source_core, ((0, 0), (OV, OV), (OV, OV)))
    result = smooth_local(source_ext, weights, diagonal)
    return fold_row(fold_aisle(result))


def body(source, conduct, solid):
    rows_here = source.shape[1]
    cols_here = source.shape[2]
    row_count = lax.axis_size("row")
    row_place = lax.axis_index("row")
    shift_term = 0.05 + 20.0 * solid.astype(jnp.float32)
    stacked = jnp.stack([conduct, shift_term])
    extended = extended_2(stacked, (("aisle", 3), ("row", 2)), OV)
    global_row = row_place * rows_here - OV + lax.iota(jnp.int32, rows_here + 2 * OV)
    outside = ((global_row < 0) | (global_row >= rows_here * row_count))[None, :, None]
    cond_ext = jnp.where(outside, 0.0, extended[0])
    shift_ext = jnp.where(outside, 1.0, extended[1])
    weights, diagonal = coupling(padded(cond_ext), shift_ext)
    first = schwarz_apply(source, weights, diagonal)
    cond_near = cond_ext[:, OV - 1 : OV + rows_here + 1, OV - 1 : OV + cols_here + 1]
    near_weights, near_diag = coupling(jnp.pad(cond_near, ((1, 1), (0, 0), (0, 0))), shift_term)
    beside_all = extended_2(first, (("aisle", 2), ("row", 1)), 1)
    near_row = row_place * rows_here - 1 + lax.iota(jnp.int32, rows_here + 2)
    near_out = ((near_row < 0) | (near_row >= rows_here * row_count))[None, :, None]
    beside_all = jnp.where(near_out, 0.0, beside_all)
    remain = source - operate(
        jnp.pad(beside_all, ((1, 1), (0, 0), (0, 0))), near_weights, near_diag
    )
    return first + schwarz_apply(remain, weights, diagonal)


def solution(mesh):
    return jax.shard_map(
        body,
        mesh=mesh,
        in_specs=(P(None, "row", "aisle"), P(None, "row", "aisle"), P(None, "row", "aisle")),
        out_specs=P(None, "row", "aisle"),
        check_vma=False,
    )
```

profile of v0, /device:TPU:8, one launch (start us, length us, event | category | flops | bytes accessed | tf_op | source)
XLA Modules:
  0.0 65.9 jit_solution(14664144267187588983)
XLA Ops:
  0.0 0.9 %fusion.193 = f32[1,8,16,128]{3,2,1,0:T(8,128)S(1)} fusion(s32[8,16,128]{2,1,0:T(8,128)} %param.5), kind=kLoop, calls=%fused_computation.329 | loop fusion | flops 49152 | bytes 131072 | tf_op jit(solution)/shard_map/stack | solution.py:126
  1.1 1.7 %collective-permute-start.1 = (f32[2,8,16,2]{3,2,1,0:T(8,128)S(1)}, f32[2,8,16,2]{3,2,1,0:T(8,128)S(1)}, u32[]{:S(2)}, u32[]{:S(2)}) collective-permute-start(f32[2,8,16,2]{3,2,1,0:T(8,128)S(1)} %get-tuple-element.46), channel_id=1, source_target_pairs={{8,0},{16,8},{24,16},{0,24},{9,1},{17,9},{25,17},{1,25},{10,2},{18... | collective-permute-start | bytes 6152 | tf_op jit(solution)/shard_map/ppermute | solution.py:35
  2.8 2.6 %collective-permute-done = f32[2,8,16,2]{3,2,1,0:T(8,128)S(1)} collective-permute-done((f32[2,8,16,2]{3,2,1,0:T(8,128)S(1)}, f32[2,8,16,2]{3,2,1,0:T(8,128)S(1)}, u32[]{:S(2)}, u32[]{:S(2)}) %collective-permute-start) | collective-permute-done | bytes 2080 | tf_op jit(solution)/shard_map/ppermute | solution.py:32
  6.0 1.6 %collective-permute-start.2 = (f32[2,8,2,132]{3,2,1,0:T(2,128)S(1)}, f32[2,8,2,132]{3,2,1,0:T(2,128)S(1)}, u32[]{:S(2)}, u32[]{:S(2)}) collective-permute-start(f32[2,8,2,132]{3,2,1,0:T(2,128)S(1)} %get-tuple-element.33), channel_id=1, source_target_pairs={{0,1},{1,2},{2,3},{3,4},{4,5},{5,6},{6,7},{7,0},{8,9},{9,10},{10,1... | collective-permute-start | bytes 50696 | tf_op jit(solution)/shard_map/ppermute | solution.py:32
  7.6 1.4 %collective-permute-start.3 = (f32[2,8,2,132]{3,2,1,0:T(2,128)S(1)}, f32[2,8,2,132]{3,2,1,0:T(2,128)S(1)}, u32[]{:S(2)}, u32[]{:S(2)}) collective-permute-start(f32[2,8,2,132]{3,2,1,0:T(2,128)S(1)} %get-tuple-element.34), channel_id=1, source_target_pairs={{1,0},{2,1},{3,2},{4,3},{5,4},{6,5},{7,6},{0,7},{9,8},{10,9},{11,1... | collective-permute-start | bytes 50696 | tf_op jit(solution)/shard_map/ppermute | solution.py:35
  9.0 2.0 %collective-permute-done.2 = f32[2,8,2,132]{3,2,1,0:T(2,128)S(1)} collective-permute-done((f32[2,8,2,132]{3,2,1,0:T(2,128)S(1)}, f32[2,8,2,132]{3,2,1,0:T(2,128)S(1)}, u32[]{:S(2)}, u32[]{:S(2)}) %collective-permute-start.2) | collective-permute-done | bytes 16928 | tf_op jit(solution)/shard_map/ppermute | solution.py:32
  11.0 0.9 %collective-permute-done.3 = f32[2,8,2,132]{3,2,1,0:T(2,128)S(1)} collective-permute-done((f32[2,8,2,132]{3,2,1,0:T(2,128)S(1)}, f32[2,8,2,132]{3,2,1,0:T(2,128)S(1)}, u32[]{:S(2)}, u32[]{:S(2)}) %collective-permute-start.3) | collective-permute-done | bytes 16928 | tf_op jit(solution)/shard_map/ppermute | solution.py:35
  15.4 3.9 %collective-permute-done.4 = f32[8,20,2]{2,1,0:T(8,128)S(1)} collective-permute-done((f32[8,20,2]{2,1,0:T(8,128)S(1)}, f32[8,20,2]{2,1,0:T(8,128)S(1)}, u32[]{:S(2)}, u32[]{:S(2)}) %collective-permute-start.4) | collective-permute-done | bytes 1312 | tf_op jit(solution)/shard_map/ppermute | solution.py:17
  19.6 2.1 %collective-permute-done.5 = f32[8,20,2]{2,1,0:T(8,128)S(1)} collective-permute-done((f32[8,20,2]{2,1,0:T(8,128)S(1)}, f32[8,20,2]{2,1,0:T(8,128)S(1)}, u32[]{:S(2)}, u32[]{:S(2)}) %collective-permute-start.5) | collective-permute-done | bytes 1312 | tf_op jit(solution)/shard_map/ppermute | solution.py:17
  21.8 4.2 %collective-permute-start.6 = (f32[8,2,128]{2,1,0:T(2,128)S(1)}, f32[8,2,128]{2,1,0:T(2,128)S(1)}, u32[]{:S(2)}, u32[]{:S(2)}) collective-permute-start(f32[8,2,128]{2,1,0:T(2,128)S(1)} %pad_maximum_fusion.17), channel_id=1, source_target_pairs={{0,1},{1,2},{2,3},{3,4},{4,5},{5,6},{6,7},{8,9},{9,10},{10,11},{11... | collective-permute-start | bytes 24584 | tf_op jit(solution)/shard_map/ppermute | solution.py:23
  26.0 2.2 %collective-permute-done.6 = f32[8,2,128]{2,1,0:T(2,128)S(1)} collective-permute-done((f32[8,2,128]{2,1,0:T(2,128)S(1)}, f32[8,2,128]{2,1,0:T(2,128)S(1)}, u32[]{:S(2)}, u32[]{:S(2)}) %collective-permute-start.6) | collective-permute-done | bytes 8224 | tf_op jit(solution)/shard_map/ppermute | solution.py:23
  28.3 3.2 %collective-permute-start.7 = (f32[8,2,128]{2,1,0:T(2,128)S(1)}, f32[8,2,128]{2,1,0:T(2,128)S(1)}, u32[]{:S(2)}, u32[]{:S(2)}) collective-permute-start(f32[8,2,128]{2,1,0:T(2,128)S(1)} %get-tuple-element.38), channel_id=1, source_target_pairs={{1,0},{2,1},{3,2},{4,3},{5,4},{6,5},{7,6},{9,8},{10,9},{11,10},{12... | collective-permute-start | bytes 24584 | tf_op jit(solution)/shard_map/ppermute | solution.py:23
  31.7 2.2 %collective-permute-done.7 = f32[8,2,128]{2,1,0:T(2,128)S(1)} collective-permute-done((f32[8,2,128]{2,1,0:T(2,128)S(1)}, f32[8,2,128]{2,1,0:T(2,128)S(1)}, u32[]{:S(2)}, u32[]{:S(2)}) %collective-permute-start.7) | collective-permute-done | bytes 8224 | tf_op jit(solution)/shard_map/ppermute | solution.py:23
  34.1 1.7 %collective-permute-start.9 = (f32[8,16,1]{2,1,0:T(8,128)S(1)}, f32[8,16,1]{2,1,0:T(8,128)S(1)}, u32[]{:S(2)}, u32[]{:S(2)}) collective-permute-start(f32[8,16,1]{2,1,0:T(8,128)S(1)} %get-tuple-element.48), channel_id=1, source_target_pairs={{8,0},{16,8},{24,16},{0,24},{9,1},{17,9},{25,17},{1,25},{10,2},{18... | collective-permute-start | bytes 1544 | tf_op jit(solution)/shard_map/ppermute | solution.py:35
  35.9 1.9 %collective-permute-done.8 = f32[8,16,1]{2,1,0:T(8,128)S(1)} collective-permute-done((f32[8,16,1]{2,1,0:T(8,128)S(1)}, f32[8,16,1]{2,1,0:T(8,128)S(1)}, u32[]{:S(2)}, u32[]{:S(2)}) %collective-permute-start.8) | collective-permute-done | bytes 544 | tf_op jit(solution)/shard_map/ppermute | solution.py:32
  38.0 2.3 %collective-permute-start.10 = (f32[8,1,130]{2,1,0:T(1,128)S(1)}, f32[8,1,130]{2,1,0:T(1,128)S(1)}, u32[]{:S(2)}, u32[]{:S(2)}) collective-permute-start(f32[8,1,130]{2,1,0:T(1,128)S(1)} %get-tuple-element.39), channel_id=1, source_target_pairs={{0,1},{1,2},{2,3},{3,4},{4,5},{5,6},{6,7},{7,0},{8,9},{9,10},{10,1... | collective-permute-start | bytes 12488 | tf_op jit(solution)/shard_map/ppermute | solution.py:32
  41.1 1.5 %collective-permute-done.10 = f32[8,1,130]{2,1,0:T(1,128)S(1)} collective-permute-done((f32[8,1,130]{2,1,0:T(1,128)S(1)}, f32[8,1,130]{2,1,0:T(1,128)S(1)}, u32[]{:S(2)}, u32[]{:S(2)}) %collective-permute-start.10) | collective-permute-done | bytes 4192 | tf_op jit(solution)/shard_map/ppermute | solution.py:32
  42.6 1.4 %collective-permute-done.11 = f32[8,1,130]{2,1,0:T(1,128)S(1)} collective-permute-done((f32[8,1,130]{2,1,0:T(1,128)S(1)}, f32[8,1,130]{2,1,0:T(1,128)S(1)}, u32[]{:S(2)}, u32[]{:S(2)}) %collective-permute-start.11) | collective-permute-done | bytes 4192 | tf_op jit(solution)/shard_map/ppermute | solution.py:35
  46.6 3.9 %collective-permute-done.12 = f32[8,20,2]{2,1,0:T(8,128)S(1)} collective-permute-done((f32[8,20,2]{2,1,0:T(8,128)S(1)}, f32[8,20,2]{2,1,0:T(8,128)S(1)}, u32[]{:S(2)}, u32[]{:S(2)}) %collective-permute-start.12) | collective-permute-done | bytes 1312 | tf_op jit(solution)/shard_map/ppermute | solution.py:17
  50.8 2.1 %collective-permute-done.13 = f32[8,20,2]{2,1,0:T(8,128)S(1)} collective-permute-done((f32[8,20,2]{2,1,0:T(8,128)S(1)}, f32[8,20,2]{2,1,0:T(8,128)S(1)}, u32[]{:S(2)}, u32[]{:S(2)}) %collective-permute-start.13) | collective-permute-done | bytes 1312 | tf_op jit(solution)/shard_map/ppermute | solution.py:17
  53.0 3.6 %collective-permute-start.14 = (f32[8,2,128]{2,1,0:T(2,128)S(1)}, f32[8,2,128]{2,1,0:T(2,128)S(1)}, u32[]{:S(2)}, u32[]{:S(2)}) collective-permute-start(f32[8,2,128]{2,1,0:T(2,128)S(1)} %pad_maximum_fusion.10), channel_id=1, source_target_pairs={{0,1},{1,2},{2,3},{3,4},{4,5},{5,6},{6,7},{8,9},{9,10},{10,11},{11... | collective-permute-start | bytes 24584 | tf_op jit(solution)/shard_map/ppermute | solution.py:23
  56.6 2.8 %collective-permute-done.14 = f32[8,2,128]{2,1,0:T(2,128)S(1)} collective-permute-done((f32[8,2,128]{2,1,0:T(2,128)S(1)}, f32[8,2,128]{2,1,0:T(2,128)S(1)}, u32[]{:S(2)}, u32[]{:S(2)}) %collective-permute-start.14) | collective-permute-done | bytes 8224 | tf_op jit(solution)/shard_map/ppermute | solution.py:23
  59.6 2.6 %collective-permute-start.15 = (f32[8,2,128]{2,1,0:T(2,128)S(1)}, f32[8,2,128]{2,1,0:T(2,128)S(1)}, u32[]{:S(2)}, u32[]{:S(2)}) collective-permute-start(f32[8,2,128]{2,1,0:T(2,128)S(1)} %get-tuple-element.36), channel_id=1, source_target_pairs={{1,0},{2,1},{3,2},{4,3},{5,4},{6,5},{7,6},{9,8},{10,9},{11,10},{12... | collective-permute-start | bytes 24584 | tf_op jit(solution)/shard_map/ppermute | solution.py:23
  62.3 2.8 %collective-permute-done.15 = f32[8,2,128]{2,1,0:T(2,128)S(1)} collective-permute-done((f32[8,2,128]{2,1,0:T(2,128)S(1)}, f32[8,2,128]{2,1,0:T(2,128)S(1)}, u32[]{:S(2)}, u32[]{:S(2)}) %collective-permute-start.15) | collective-permute-done | bytes 8224 | tf_op jit(solution)/shard_map/ppermute | solution.py:23
  (60 shorter events, 9.8 us)
Async XLA Ops:
  0.0 0.9 %copy-start.1 = (f32[8,16,128]{2,1,0:T(8,128)S(1)}, f32[8,16,128]{2,1,0:T(8,128)}, u32[]{:S(2)}) copy-start(f32[8,16,128]{2,1,0:T(8,128)} %param.4) | copy-start | bytes 196612
  1.0 4.4 %collective-permute-start = (f32[2,8,16,2]{3,2,1,0:T(8,128)S(1)}, f32[2,8,16,2]{3,2,1,0:T(8,128)S(1)}, u32[]{:S(2)}, u32[]{:S(2)}) collective-permute-start(f32[2,8,16,2]{3,2,1,0:T(8,128)S(1)} %get-tuple-element.45), channel_id=1, source_target_pairs={{0,8},{8,16},{16,24},{24,0},{1,9},{9,17},{17,25},{25,1},{2,10},{10... | collective-permute-start | bytes 6152 | tf_op jit(solution)/shard_map/ppermute | solution.py:32
  1.1 4.8 %collective-permute-start.1 = (f32[2,8,16,2]{3,2,1,0:T(8,128)S(1)}, f32[2,8,16,2]{3,2,1,0:T(8,128)S(1)}, u32[]{:S(2)}, u32[]{:S(2)}) collective-permute-start(f32[2,8,16,2]{3,2,1,0:T(8,128)S(1)} %get-tuple-element.46), channel_id=1, source_target_pairs={{8,0},{16,8},{24,16},{0,24},{9,1},{17,9},{25,17},{1,25},{10,2},{18... | collective-permute-start | bytes 6152 | tf_op jit(solution)/shard_map/ppermute | solution.py:35
  6.0 5.0 %collective-permute-start.2 = (f32[2,8,2,132]{3,2,1,0:T(2,128)S(1)}, f32[2,8,2,132]{3,2,1,0:T(2,128)S(1)}, u32[]{:S(2)}, u32[]{:S(2)}) collective-permute-start(f32[2,8,2,132]{3,2,1,0:T(2,128)S(1)} %get-tuple-element.33), channel_id=1, source_target_pairs={{0,1},{1,2},{2,3},{3,4},{4,5},{5,6},{6,7},{7,0},{8,9},{9,10},{10,1... | collective-permute-start | bytes 50696 | tf_op jit(solution)/shard_map/ppermute | solution.py:32
  7.6 4.3 %collective-permute-start.3 = (f32[2,8,2,132]{3,2,1,0:T(2,128)S(1)}, f32[2,8,2,132]{3,2,1,0:T(2,128)S(1)}, u32[]{:S(2)}, u32[]{:S(2)}) collective-permute-start(f32[2,8,2,132]{3,2,1,0:T(2,128)S(1)} %get-tuple-element.34), channel_id=1, source_target_pairs={{1,0},{2,1},{3,2},{4,3},{5,4},{6,5},{7,6},{0,7},{9,8},{10,9},{11,1... | collective-permute-start | bytes 50696 | tf_op jit(solution)/shard_map/ppermute | solution.py:35
  12.2 0.8 %copy-start = (f32[8,16,128]{2,1,0:T(8,128)S(1)}, f32[8,16,128]{2,1,0:T(8,128)}, u32[]{:S(2)}) copy-start(f32[8,16,128]{2,1,0:T(8,128)} %param.3) | copy-start | bytes 196612
  15.2 4.1 %collective-permute-start.4 = (f32[8,20,2]{2,1,0:T(8,128)S(1)}, f32[8,20,2]{2,1,0:T(8,128)S(1)}, u32[]{:S(2)}, u32[]{:S(2)}) collective-permute-start(f32[8,20,2]{2,1,0:T(8,128)S(1)} %slice.541), channel_id=1, source_target_pairs={{24,0},{0,8},{8,16},{16,24},{25,1},{1,9},{9,17},{17,25},{26,2},{2,... | collective-permute-start | bytes 3848 | tf_op jit(solution)/shard_map/ppermute | solution.py:17
  19.4 2.3 %collective-permute-start.5 = (f32[8,20,2]{2,1,0:T(8,128)S(1)}, f32[8,20,2]{2,1,0:T(8,128)S(1)}, u32[]{:S(2)}, u32[]{:S(2)}) collective-permute-start(f32[8,20,2]{2,1,0:T(8,128)S(1)} %get-tuple-element.44), channel_id=1, source_target_pairs={{8,0},{16,8},{24,16},{0,24},{9,1},{17,9},{25,17},{1,25},{10,2},{18... | collective-permute-start | bytes 3848 | tf_op jit(solution)/shard_map/ppermute | solution.py:17
  21.8 6.4 %collective-permute-start.6 = (f32[8,2,128]{2,1,0:T(2,128)S(1)}, f32[8,2,128]{2,1,0:T(2,128)S(1)}, u32[]{:S(2)}, u32[]{:S(2)}) collective-permute-start(f32[8,2,128]{2,1,0:T(2,128)S(1)} %pad_maximum_fusion.17), channel_id=1, source_target_pairs={{0,1},{1,2},{2,3},{3,4},{4,5},{5,6},{6,7},{8,9},{9,10},{10,11},{11... | collective-permute-start | bytes 24584 | tf_op jit(solution)/shard_map/ppermute | solution.py:23
  28.3 5.6 %collective-permute-start.7 = (f32[8,2,128]{2,1,0:T(2,128)S(1)}, f32[8,2,128]{2,1,0:T(2,128)S(1)}, u32[]{:S(2)}, u32[]{:S(2)}) collective-permute-start(f32[8,2,128]{2,1,0:T(2,128)S(1)} %get-tuple-element.38), channel_id=1, source_target_pairs={{1,0},{2,1},{3,2},{4,3},{5,4},{6,5},{7,6},{9,8},{10,9},{11,10},{12... | collective-permute-start | bytes 24584 | tf_op jit(solution)/shard_map/ppermute | solution.py:23
  34.1 3.7 %collective-permute-start.8 = (f32[8,16,1]{2,1,0:T(8,128)S(1)}, f32[8,16,1]{2,1,0:T(8,128)S(1)}, u32[]{:S(2)}, u32[]{:S(2)}) collective-permute-start(f32[8,16,1]{2,1,0:T(8,128)S(1)} %get-tuple-element.47), channel_id=1, source_target_pairs={{0,8},{8,16},{16,24},{24,0},{1,9},{9,17},{17,25},{25,1},{2,10},{10... | collective-permute-start | bytes 1544 | tf_op jit(solution)/shard_map/ppermute | solution.py:32
  34.1 3.7 %collective-permute-start.9 = (f32[8,16,1]{2,1,0:T(8,128)S(1)}, f32[8,16,1]{2,1,0:T(8,128)S(1)}, u32[]{:S(2)}, u32[]{:S(2)}) collective-permute-start(f32[8,16,1]{2,1,0:T(8,128)S(1)} %get-tuple-element.48), channel_id=1, source_target_pairs={{8,0},{16,8},{24,16},{0,24},{9,1},{17,9},{25,17},{1,25},{10,2},{18... | collective-permute-start | bytes 1544 | tf_op jit(solution)/shard_map/ppermute | solution.py:35
  38.0 4.6 %collective-permute-start.10 = (f32[8,1,130]{2,1,0:T(1,128)S(1)}, f32[8,1,130]{2,1,0:T(1,128)S(1)}, u32[]{:S(2)}, u32[]{:S(2)}) collective-permute-start(f32[8,1,130]{2,1,0:T(1,128)S(1)} %get-tuple-element.39), channel_id=1, source_target_pairs={{0,1},{1,2},{2,3},{3,4},{4,5},{5,6},{6,7},{7,0},{8,9},{9,10},{10,1... | collective-permute-start | bytes 12488 | tf_op jit(solution)/shard_map/ppermute | solution.py:32
  40.3 3.7 %collective-permute-start.11 = (f32[8,1,130]{2,1,0:T(1,128)S(1)}, f32[8,1,130]{2,1,0:T(1,128)S(1)}, u32[]{:S(2)}, u32[]{:S(2)}) collective-permute-start(f32[8,1,130]{2,1,0:T(1,128)S(1)} %get-tuple-element.40), channel_id=1, source_target_pairs={{1,0},{2,1},{3,2},{4,3},{5,4},{6,5},{7,6},{0,7},{9,8},{10,9},{11,1... | collective-permute-start | bytes 12488 | tf_op jit(solution)/shard_map/ppermute | solution.py:35
  41.1 3.1 %copy-start.2 = (s32[8,16,128]{2,1,0:T(8,128)S(1)}, s32[8,16,128]{2,1,0:T(8,128)}, u32[]{:S(2)}) copy-start(s32[8,16,128]{2,1,0:T(8,128)} %param.5) | copy-start | bytes 196612
  46.5 4.1 %collective-permute-start.12 = (f32[8,20,2]{2,1,0:T(8,128)S(1)}, f32[8,20,2]{2,1,0:T(8,128)S(1)}, u32[]{:S(2)}, u32[]{:S(2)}) collective-permute-start(f32[8,20,2]{2,1,0:T(8,128)S(1)} %slice.560), channel_id=1, source_target_pairs={{24,0},{0,8},{8,16},{16,24},{25,1},{1,9},{9,17},{17,25},{26,2},{2,... | collective-permute-start | bytes 3848 | tf_op jit(solution)/shard_map/ppermute | solution.py:17
  50.7 2.3 %collective-permute-start.13 = (f32[8,20,2]{2,1,0:T(8,128)S(1)}, f32[8,20,2]{2,1,0:T(8,128)S(1)}, u32[]{:S(2)}, u32[]{:S(2)}) collective-permute-start(f32[8,20,2]{2,1,0:T(8,128)S(1)} %get-tuple-element.42), channel_id=1, source_target_pairs={{8,0},{16,8},{24,16},{0,24},{9,1},{17,9},{25,17},{1,25},{10,2},{18... | collective-permute-start | bytes 3848 | tf_op jit(solution)/shard_map/ppermute | solution.py:17
  53.0 6.4 %collective-permute-start.14 = (f32[8,2,128]{2,1,0:T(2,128)S(1)}, f32[8,2,128]{2,1,0:T(2,128)S(1)}, u32[]{:S(2)}, u32[]{:S(2)}) collective-permute-start(f32[8,2,128]{2,1,0:T(2,128)S(1)} %pad_maximum_fusion.10), channel_id=1, source_target_pairs={{0,1},{1,2},{2,3},{3,4},{4,5},{5,6},{6,7},{8,9},{9,10},{10,11},{11... | collective-permute-start | bytes 24584 | tf_op jit(solution)/shard_map/ppermute | solution.py:23
  59.6 5.5 %collective-permute-start.15 = (f32[8,2,128]{2,1,0:T(2,128)S(1)}, f32[8,2,128]{2,1,0:T(2,128)S(1)}, u32[]{:S(2)}, u32[]{:S(2)}) collective-permute-start(f32[8,2,128]{2,1,0:T(2,128)S(1)} %get-tuple-element.36), channel_id=1, source_target_pairs={{1,0},{2,1},{3,2},{4,3},{5,4},{6,5},{7,6},{9,8},{10,9},{11,10},{12... | collective-permute-start | bytes 24584 | tf_op jit(solution)/shard_map/ppermute | solution.py:23
where the time goes:
time: 66.5 us; the launch traced here: 65.9 us
  waiting for transfers between devices  33 us (50%)
  starting transfers between devices  23.5 us (35%)
  other arithmetic  7.77 us (12%)
  local copies, waits for them, and re-layouts  1.29 us (2%)
    ppermute x4, starting transfers between devices, from_behind(): return lax.ppermute(shard, axis, pairs)  13.5 us
    ppermute x4, waiting for transfers between devices, shifted(): return lax.ppermute(block, axis, route)  12.1 us
    ppermute x4, waiting for transfers between devices, from_behind(): return lax.ppermute(shard, axis, pairs)  10.1 us
    ppermute x4, waiting for transfers between devices, extended_2(): lax.ppermute(lax.slice_in_dim(block, block.shape[dim] - width, None, axis...  8.08 us
    ppermute x4, starting transfers between devices, extended_2(): lax.ppermute(lax.slice_in_dim(block, 0, width, axis=dim), axis, backward)  5.53 us
    ppermute x4, starting transfers between devices, extended_2(): lax.ppermute(lax.slice_in_dim(block, block.shape[dim] - width, None, axis...  3.97 us
    add x12, other arithmetic, smooth_local(): estimate = estimate + update  3.61 us
    ppermute x4, waiting for transfers between devices, extended_2(): lax.ppermute(lax.slice_in_dim(block, 0, width, axis=dim), axis, backward)  2.71 us
  transfers between devices with their start and end apart: 16, of which 15 were waited for; matrix products, arithmetic and copies ran while one was open for 1% of the time, Pallas kernels for 0%

commit v1 on v0

v1 whole, which is shorter than its diff:
```python
import jax
import jax.numpy as jnp
from jax import lax
from jax.experimental import pallas as pl
from jax.experimental.pallas import tpu as pltpu
from jax.sharding import PartitionSpec as P

OV = 2
SWEEPS = 6
LOWER_END = 0.2
UPPER_END = 2.0
MIDDLE = 0.5 * (UPPER_END + LOWER_END)
SPREAD = 0.5 * (UPPER_END - LOWER_END)

NZ = 8
CR = 16
CA = 128
DG = 2 * SWEEPS + 1
DK = DG + 1
UP = DG + OV
OWN = CR + 2 * OV
ROWS = UP + OWN + UP
OWN0 = UP
DOWN0 = UP + OWN
WIDE = 2 * CA
TWIN = 5
STRIP = 14
PERIOD = 40
TILES = 2 * DG + 2 * DK


def chebyshev():
    ratio = SPREAD / MIDDLE
    steps = []
    for _ in range(SWEEPS):
        ratio_next = 1.0 / (2.0 * MIDDLE / SPREAD - ratio)
        steps.append((ratio_next * ratio, 2.0 * ratio_next / SPREAD))
        ratio = ratio_next
    return steps


def lanes(width=CA):
    return lax.broadcasted_iota(jnp.int32, (NZ, width), 1)


def turn(value, by, axis=1):
    return pltpu.roll(value, by % value.shape[axis], axis)


def any_of(lane, *spans):
    mask = None
    for low, high in spans:
        here = (lane >= low) & (lane < high)
        mask = here if mask is None else mask | here
    return mask


def pack_edges(source, conduct, solid, main, to_left, to_right):
    odd = lax.rem(lax.axis_index("row"), 2)
    lane = lanes()
    lefts, rights = [], []
    for row in range(CR):
        at = pl.ds(odd * (CR - 1 - 2 * row) + row, NZ, stride=CR)
        fields = [source[at, :], conduct[at, :], 0.05 + 20.0 * solid[at, :].astype(jnp.float32)]
        left = right = jnp.zeros((NZ, CA), jnp.float32)
        for number, field in enumerate(fields):
            main[number, row] = field
            base = PERIOD * number
            left = jnp.where(any_of(lane, (base + 24, base + 38)), turn(field, base + 24), left)
            right = jnp.where(any_of(lane, (base, base + STRIP)), turn(field, base + STRIP), right)
        lefts.append(left)
        rights.append(right)
    half = CR // 2
    for row in range(half):
        to_left[row] = lefts[row] + turn(lefts[row + half], -16)
        to_right[row] = rights[row] + turn(rights[row + half], 16)


def pack_rows(main, from_right, from_left, strips, to_far, to_near):
    lane = lanes()
    in_right = any_of(lane, *[(PERIOD * n + 24, PERIOD * n + 38) for n in range(3)])
    half = CR // 2
    for row in range(half):
        strips[row] = jnp.where(in_right, from_right[row], from_left[row])
        strips[row + half] = jnp.where(in_right, turn(from_right[row], 16), turn(from_left[row], -16))
    for out, place in ((to_far, lambda q: q), (to_near, lambda q: CR - 1 - q)):
        for q in range(DG):
            out[q] = main[0, place(q)]
            out[DG + DK + q] = main[2, place(q)]
        for q in range(DK):
            out[DG + q] = main[1, place(q)]
            out[2 * DG + DK + q] = strips[place(q)]


def beside_block(block, strip, number, lane, fill):
    boxes = jnp.where(any_of(lane, (5, 19), (109, 123)), turn(strip, -19 - PERIOD * number), 0.0)
    if not fill:
        return boxes
    mixed = jnp.where(any_of(lane, (5, 7), (121, 123)), boxes, block)
    low = any_of(lane, (0, 2), (123, 125))
    high = any_of(lane, (3, 5), (126, 128))
    return jnp.where(low, turn(mixed, -TWIN), jnp.where(high, turn(mixed, TWIN), boxes))


def loop_rows(low, high, unroll, body, carry=None):
    count = (high - low) // unroll

    def chunk(number, carry):
        for k in range(unroll):
            carry = body(low + number * unroll + k, carry)
        return carry

    if count > 0:
        carry = lax.fori_loop(0, count, chunk, carry)
    for row in range(low + count * unroll, high):
        carry = body(row, carry)
    return carry


def solve_all(main, strips, far, near, out, cond, shift, face_x, face_z, face_r, inverse, diag, rhs, est, upd, total):
    row_at = lax.axis_index("row")
    rows_all = lax.axis_size("row")
    odd = lax.rem(row_at, 2)
    far_there = jnp.where(odd == 0, row_at > 0, row_at < rows_all - 1)
    far_here = jnp.full((NZ, CA), far_there.astype(jnp.float32)) > 0.5
    far_wide = jnp.full((NZ, WIDE), far_there.astype(jnp.float32)) > 0.5
    lane = lanes()
    wide = lanes(WIDE)
    level = lax.broadcasted_iota(jnp.int32, (NZ, WIDE), 0)
    zeros = jnp.zeros((NZ, WIDE), jnp.float32)

    def put(block, strip, number, fill):
        return jnp.concatenate([block, beside_block(block, strip, number, lane, fill)], axis=1)

    def unpack_own(row, carry):
        strip = strips[row]
        rhs[OWN0 + OV + row] = put(main[0, row], strip, 0, False)
        cond[DK + row] = put(main[1, row], strip, 1, True)
        shift[DG + row] = put(main[2, row], strip, 2, True)
        return carry

    loop_rows(0, CR, 4, unpack_own)

    def unpack_sides(q, carry):
        strip = far[2 * DG + DK + q]
        rhs[DG - 1 - q] = put(far[q], strip, 0, False)
        cond[DK - 1 - q] = put(far[DG + q], strip, 1, True)
        shift[DG - 1 - q] = jnp.where(far_wide, put(far[DG + DK + q], strip, 2, True), 1.0)
        strip = near[2 * DG + DK + q]
        rhs[DOWN0 + OV + q] = put(near[q], strip, 0, False)
        cond[DK + CR + q] = put(near[DG + q], strip, 1, True)
        shift[DG + CR + q] = put(near[DG + DK + q], strip, 2, True)
        return carry

    loop_rows(0, DG, 3, unpack_sides)
    last = DK - 1
    cond[0] = put(far[DG + last], far[2 * DG + DK + last], 1, True)
    cond[DK + CR + last] = put(near[DG + last], near[2 * DG + DK + last], 1, True)
    for row in (UP - 2, UP - 1, OWN0, OWN0 + 1, DOWN0 - 2, DOWN0 - 1, DOWN0, DOWN0 + 1):
        rhs[row] = zeros

    in_box = any_of(wide, (0, 130), (131, 147), (237, 253), (254, 256))
    core = any_of(wide, (0, 128), (133, 147), (237, 251))
    top = level == NZ - 1
    bottom = level == 0

    def weights(row, place, low_end=False, high_end=False):
        here = cond[place + DK]
        below = zeros if low_end else cond[place + DK - 1]
        above = zeros if high_end else cond[place + DK + 1]
        z_up = jnp.where(top, 0.0, turn(here, -1, 0))
        z_down = jnp.where(bottom, 0.0, turn(here, 1, 0))
        x_up = turn(here, -1)
        x_down = turn(here, 1)
        diagonal = shift[place + DG] + 3.0 * here + 0.5 * (z_up + z_down + x_up + x_down + below + above)
        diag[row] = diagonal
        inverse[row] = jnp.where(in_box, 1.0 / diagonal, 0.0)
        face_x[row] = 0.5 * (here + x_up)
        face_z[row] = jnp.where(top, 0.0, 0.5 * (here + z_up))
        face_r[row] = zeros if low_end else 0.5 * (here + below)

    def span(first, count, place):
        def body(row, carry):
            weights(row, row + (place - first))
            return carry

        loop_rows(first, first + count, 4, body)

    span(0, UP - 1, -DG)
    weights(UP - 1, OV - 1, high_end=True)
    weights(OWN0, -OV, low_end=True)
    span(OWN0 + 1, OWN - 2, 1 - OV)
    weights(DOWN0 - 1, CR + OV - 1, high_end=True)
    weights(DOWN0, CR - OV, low_end=True)
    span(DOWN0 + 1, UP - 1, CR - OV + 1)
    face_r[ROWS] = zeros
    est[0] = zeros
    est[ROWS + 1] = zeros

    def around(row, here, below, above):
        fx = face_x[row]
        fz = face_z[row]
        summed = face_r[row] * below + face_r[row + 1] * above
        summed += fx * turn(here, -1) + turn(fx * here, 1)
        return summed + (fz * turn(here, -1, 0) + turn(fz * here, 1, 0))

    def solve(low, high):
        def begin(row, carry):
            first = inverse[row] * rhs[row] * (1.0 / MIDDLE)
            est[row + 1] = first
            upd[row] = first
            return carry

        loop_rows(low, high, 4, begin)
        for number, (keep, gain) in enumerate(chebyshev()):
            def sweep(row, carry):
                below, here = carry
                above = est[row + 2]
                summed = rhs[row] + around(row, here, below, above)
                step = keep * upd[row] + gain * (inverse[row] * summed - here)
                upd[row] = step
                est[row + 1] = here + step
                return here, above

            start = low + number + 1
            loop_rows(start, high - number - 1, 4, sweep, (est[start], est[start + 1]))

    solve(0, ROWS)

    reach = SWEEPS + 1
    to_low = any_of(wide, (126, 130), (249, 253))
    to_high = any_of(wide, (131, 135), (254, 256), (0, 2))

    def joined(value):
        other = jnp.where(to_low, turn(value, -TWIN), jnp.where(to_high, turn(value, TWIN), 0.0))
        return value + other

    for place in range(-reach, CR + reach):
        parts = []
        if place < OV:
            parts.append(est[place + DG + 1])
        if -OV <= place < CR + OV:
            parts.append(est[OWN0 + OV + place + 1])
        if place >= CR - OV:
            parts.append(est[DOWN0 + OV - CR + place + 1])
        value = joined(sum(parts[1:], parts[0]))
        if place < 0:
            value = jnp.where(far_wide, value, 0.0)
        total[place + reach] = value

    def remainder(row, place):
        at = place + reach
        here = total[at]
        summed = around(row, here, total[at - 1], total[at + 1])
        return jnp.where(core, rhs[row] - (diag[row] * here - summed), 0.0)

    def remain_own(row, carry):
        rhs[row] = remainder(row, row - (OWN0 + OV))
        return carry

    loop_rows(OWN0 + OV, OWN0 + OV + CR, 4, remain_own)
    for layer in range(SWEEPS):
        row = DG - 1 - layer
        rhs[row] = jnp.where(far_wide, remainder(row, -1 - layer), 0.0)
        row = DOWN0 + OV + layer
        rhs[row] = remainder(row, CR + layer)

    cut = DG - SWEEPS
    solve(cut, ROWS - cut)

    for place in range(CR):
        value = est[OWN0 + OV + place + 1]
        if place < OV:
            value = value + est[place + DG + 1]
        if place >= CR - OV:
            value = value + est[DOWN0 + OV - CR + place + 1]
        value = total[place + reach] + joined(value)
        out[pl.ds(odd * (CR - 1 - 2 * place) + place, NZ, stride=CR), :] = value[:, :CA]


def body(source, conduct, solid):
    aisles = lax.axis_size("aisle")
    rows = lax.axis_size("row")
    flat = (NZ * CR, CA)
    tile = lambda *lead: jax.ShapeDtypeStruct(lead + (NZ, CA), jnp.float32)
    main, to_left, to_right = pl.pallas_call(
        pack_edges, out_shape=(tile(3, CR), tile(CR // 2), tile(CR // 2)), name="pack_edges"
    )(source.reshape(flat), conduct.reshape(flat), solid.reshape(flat))
    up = [(i, (i + 1) % aisles) for i in range(aisles)]
    from_left = lax.ppermute(to_right, "aisle", up)
    from_right = lax.ppermute(to_left, "aisle", [(b, a) for a, b in up])
    strips, to_far, to_near = pl.pallas_call(
        pack_rows, out_shape=(tile(CR), tile(TILES), tile(TILES)), name="pack_rows"
    )(main, from_right, from_left)
    far_pairs = [(i, i + 1) for i in range(1, rows - 1, 2)]
    far = lax.ppermute(to_far, "row", far_pairs + [(b, a) for a, b in far_pairs])
    near = lax.ppermute(to_near, "row", [(i, i ^ 1) for i in range(rows)])
    rowbuf = lambda count: pltpu.VMEM((count, NZ, WIDE), jnp.float32)
    result = pl.pallas_call(
        solve_all,
        out_shape=jax.ShapeDtypeStruct(flat, jnp.float32),
        scratch_shapes=[
            rowbuf(CR + 2 * DK), rowbuf(CR + 2 * DG), rowbuf(ROWS), rowbuf(ROWS), rowbuf(ROWS + 1), rowbuf(ROWS),
            rowbuf(ROWS), rowbuf(ROWS), rowbuf(ROWS + 2), rowbuf(ROWS), rowbuf(CR + 2 * SWEEPS + 2),
        ],
        compiler_params=pltpu.CompilerParams(vmem_limit_bytes=16 * 1024 * 1024),
        name="solve_all",
    )(main, strips, far, near)
    return result.reshape(NZ, CR, CA)


def solution(mesh):
    spec = P(None, "row", "aisle")
    return jax.shard_map(body, mesh=mesh, in_specs=(spec, spec, spec), out_specs=spec, check_vma=False)
```

time: 66.5 us -> 39.3 us (0.59)
  the two profiles are of different devices: /device:TPU:8 before, /device:TPU:19 now
where the time goes in v1:
time: 39.3 us; the launch traced here: 39.1 us
  Pallas kernels  18.4 us (47%)
  waiting for transfers between devices  13.1 us (33%)
  starting transfers between devices  6.19 us (16%)
  local copies, waits for them, and re-layouts  1.46 us (4%)
    pallas_call x1, Pallas kernels, body(): pl.pallas_call(solve_all, out_shape=jax.ShapeDtypeStruct(flat, jnp.float3...  14.8 us
    ppermute x1, waiting for transfers between devices, body(): near = lax.ppermute(to_near, 'row', [(i, i ^ 1) for i in range(rows)])  5.41 us
    ppermute x1, waiting for transfers between devices, body(): lax.ppermute(to_far, 'row', far_pairs + [(b, a) for a, b in far_pairs])  5.22 us
    ppermute x1, starting transfers between devices, body(): lax.ppermute(to_far, 'row', far_pairs + [(b, a) for a, b in far_pairs])  3.01 us
    ppermute x1, waiting for transfers between devices, body(): from_right = lax.ppermute(to_left, 'aisle', [(b, a) for a, b in up])  2.44 us
    pallas_call x1, Pallas kernels, body(): pl.pallas_call(pack_rows, out_shape=(tile(CR), tile(TILES), tile(TILES)),...  1.81 us
    pallas_call x1, Pallas kernels, body(): pl.pallas_call(pack_edges, out_shape=(tile(3, CR), tile(CR // 2), tile(CR...  1.75 us
    unnamed x8, local copies, waits for them, and re-layouts  1.46 us
  transfers between devices with their start and end apart: 4, of which 3 were waited for; matrix products, arithmetic and copies ran while one was open for 0% of the time, Pallas kernels for 0%

profile of v1, /device:TPU:19, one launch (start us, length us, event | category | flops | bytes accessed | tf_op | source)
XLA Modules:
  0.0 39.1 jit_solution(2051970920502194894)
XLA Ops:
  0.0 1.8 %pack_edges.1 = (f32[3,16,8,128]{3,2,1,0:T(8,128)}, f32[8,8,128]{2,1,0:T(8,128)}, f32[8,8,128]{2,1,0:T(8,128)}) custom-call(f32[128,128]{1,0:T(8,128)} %bitcast.4, f32[128,128]{1,0:T(8,128)} %bitcast.5, s32[128,128]{1,0:T(8,128)} %bitcast.6), custom_call_target="tpu_custom_call" | custom-call | tf_op jit(solution)/shard_map/pack_edges/pallas_call | solution.py:286
  1.8 0.0 copy-start
  1.8 0.7 %collective-permute-start = (f32[8,8,128]{2,1,0:T(8,128)}, f32[8,8,128]{2,1,0:T(8,128)S(1)}, u32[]{:S(2)}, u32[]{:S(2)}) collective-permute-start(f32[8,8,128]{2,1,0:T(8,128)} %get-tuple-element.12), channel_id=1, source_target_pairs={{8,0},{16,8},{24,16},{0,24},{9,1},{17,9},{25,17},{1,25},{10,2},{18... | collective-permute-start | bytes 98312 | tf_op jit(solution)/shard_map/ppermute | solution.py:291
  2.4 1.1 %collective-permute-start.1 = (f32[8,8,128]{2,1,0:T(8,128)}, f32[8,8,128]{2,1,0:T(8,128)S(1)}, u32[]{:S(2)}, u32[]{:S(2)}) collective-permute-start(f32[8,8,128]{2,1,0:T(8,128)} %get-tuple-element.13), channel_id=1, source_target_pairs={{0,8},{8,16},{16,24},{24,0},{1,9},{9,17},{17,25},{25,1},{2,10},{10... | collective-permute-start | bytes 98312 | tf_op jit(solution)/shard_map/ppermute | solution.py:290
  3.5 2.4 %collective-permute-done.from_right = f32[8,8,128]{2,1,0:T(8,128)S(1)} collective-permute-done((f32[8,8,128]{2,1,0:T(8,128)}, f32[8,8,128]{2,1,0:T(8,128)S(1)}, u32[]{:S(2)}, u32[]{:S(2)}) %collective-permute-start) | collective-permute-done | bytes 32800 | tf_op jit(solution)/shard_map/ppermute | solution.py:291
  5.9 0.0 copy-start.2
  5.9 0.0 collective-permute-done.1.from_left
  5.9 0.0 copy-start.3
  5.9 0.6 %copy-done.2 = f32[8,8,128]{2,1,0:T(8,128)} copy-done((f32[8,8,128]{2,1,0:T(8,128)}, f32[8,8,128]{2,1,0:T(8,128)S(1)}, u32[]{:S(2)}) %copy-start.2) | copy-done | bytes 32792
  6.5 0.0 copy-done.3
  6.6 1.8 %pack_rows.1 = (f32[16,8,128]{2,1,0:T(8,128)}, f32[54,8,128]{2,1,0:T(8,128)}, f32[54,8,128]{2,1,0:T(8,128)}) custom-call(f32[3,16,8,128]{3,2,1,0:T(8,128)} %get-tuple-element.11.main, f32[8,8,128]{2,1,0:T(8,128)} %copy-done.2, f32[8,8,128]{2,1,0:T(8,128)} %copy-done.3), custom_call_target="tpu_custom_call" | custom-call | tf_op jit(solution)/shard_map/pack_rows/pallas_call | solution.py:292
  8.4 3.0 %collective-permute-start.2 = (f32[54,8,128]{2,1,0:T(8,128)}, f32[54,8,128]{2,1,0:T(8,128)S(1)}, u32[]{:S(2)}, u32[]{:S(2)}) collective-permute-start(f32[54,8,128]{2,1,0:T(8,128)} %get-tuple-element.15), channel_id=1, source_target_pairs={{1,2},{3,4},{5,6},{2,1},{4,3},{6,5},{9,10},{11,12},{13,14},{10,9},... | collective-permute-start | bytes 663560 | tf_op jit(solution)/shard_map/ppermute | solution.py:296
  11.4 1.4 %collective-permute-start.3 = (f32[54,8,128]{2,1,0:T(8,128)}, f32[54,8,128]{2,1,0:T(8,128)S(1)}, u32[]{:S(2)}, u32[]{:S(2)}) collective-permute-start(f32[54,8,128]{2,1,0:T(8,128)} %get-tuple-element.16), channel_id=1, source_target_pairs={{0,1},{1,0},{2,3},{3,2},{4,5},{5,4},{6,7},{7,6},{8,9},{9,8},{10,11... | collective-permute-start | bytes 663560 | tf_op jit(solution)/shard_map/ppermute | solution.py:297
  12.8 5.2 %collective-permute-done.2.far = f32[54,8,128]{2,1,0:T(8,128)S(1)} collective-permute-done((f32[54,8,128]{2,1,0:T(8,128)}, f32[54,8,128]{2,1,0:T(8,128)S(1)}, u32[]{:S(2)}, u32[]{:S(2)}) %collective-permute-start.2) | collective-permute-done | bytes 221216 | tf_op jit(solution)/shard_map/ppermute | solution.py:296
  18.0 5.4 %collective-permute-done.3.near = f32[54,8,128]{2,1,0:T(8,128)S(1)} collective-permute-done((f32[54,8,128]{2,1,0:T(8,128)}, f32[54,8,128]{2,1,0:T(8,128)S(1)}, u32[]{:S(2)}, u32[]{:S(2)}) %collective-permute-start.3) | collective-permute-done | bytes 221216 | tf_op jit(solution)/shard_map/ppermute | solution.py:297
  23.4 0.0 copy-done
  23.4 0.0 copy-start.1
  23.5 0.8 %copy-done.1 = f32[16,8,128]{2,1,0:T(8,128)S(1)} copy-done((f32[16,8,128]{2,1,0:T(8,128)S(1)}, f32[16,8,128]{2,1,0:T(8,128)}, u32[]{:S(2)}) %copy-start.1) | copy-done | bytes 65560
  24.3 14.8 %solve_all.1 = f32[128,128]{1,0:T(8,128)} custom-call(f32[3,16,8,128]{3,2,1,0:T(8,128)S(1)} %copy-done, f32[16,8,128]{2,1,0:T(8,128)S(1)} %copy-done.1, f32[54,8,128]{2,1,0:T(8,128)S(1)} %collective-permute-done.2.far, f32[54,8,128]{2,1,0:T(8,128)S(1)} %collective-permute-done.3.near), custom_call_target="tpu_custom_call" | custom-call | tf_op jit(solution)/shard_map/solve_all/pallas_call | solution.py:299
Async XLA Ops:
  1.8 21.7 %copy-start = (f32[3,16,8,128]{3,2,1,0:T(8,128)S(1)}, f32[3,16,8,128]{3,2,1,0:T(8,128)}, u32[]{:S(2)}) copy-start(f32[3,16,8,128]{3,2,1,0:T(8,128)} %get-tuple-element.11.main) | copy-start | bytes 589828
  1.8 4.2 %collective-permute-start = (f32[8,8,128]{2,1,0:T(8,128)}, f32[8,8,128]{2,1,0:T(8,128)S(1)}, u32[]{:S(2)}, u32[]{:S(2)}) collective-permute-start(f32[8,8,128]{2,1,0:T(8,128)} %get-tuple-element.12), channel_id=1, source_target_pairs={{8,0},{16,8},{24,16},{0,24},{9,1},{17,9},{25,17},{1,25},{10,2},{18... | collective-permute-start | bytes 98312 | tf_op jit(solution)/shard_map/ppermute | solution.py:291
  2.4 3.5 %collective-permute-start.1 = (f32[8,8,128]{2,1,0:T(8,128)}, f32[8,8,128]{2,1,0:T(8,128)S(1)}, u32[]{:S(2)}, u32[]{:S(2)}) collective-permute-start(f32[8,8,128]{2,1,0:T(8,128)} %get-tuple-element.13), channel_id=1, source_target_pairs={{0,8},{8,16},{16,24},{24,0},{1,9},{9,17},{17,25},{25,1},{2,10},{10... | collective-permute-start | bytes 98312 | tf_op jit(solution)/shard_map/ppermute | solution.py:290
  5.9 0.6 %copy-start.2 = (f32[8,8,128]{2,1,0:T(8,128)}, f32[8,8,128]{2,1,0:T(8,128)S(1)}, u32[]{:S(2)}) copy-start(f32[8,8,128]{2,1,0:T(8,128)S(1)} %collective-permute-done.from_right) | copy-start | bytes 98308
  5.9 0.6 %copy-start.3 = (f32[8,8,128]{2,1,0:T(8,128)}, f32[8,8,128]{2,1,0:T(8,128)S(1)}, u32[]{:S(2)}) copy-start(f32[8,8,128]{2,1,0:T(8,128)S(1)} %collective-permute-done.1.from_left) | copy-start | bytes 98308
  8.4 9.7 %collective-permute-start.2 = (f32[54,8,128]{2,1,0:T(8,128)}, f32[54,8,128]{2,1,0:T(8,128)S(1)}, u32[]{:S(2)}, u32[]{:S(2)}) collective-permute-start(f32[54,8,128]{2,1,0:T(8,128)} %get-tuple-element.15), channel_id=1, source_target_pairs={{1,2},{3,4},{5,6},{2,1},{4,3},{6,5},{9,10},{11,12},{13,14},{10,9},... | collective-permute-start | bytes 663560 | tf_op jit(solution)/shard_map/ppermute | solution.py:296
  11.4 12.1 %collective-permute-start.3 = (f32[54,8,128]{2,1,0:T(8,128)}, f32[54,8,128]{2,1,0:T(8,128)S(1)}, u32[]{:S(2)}, u32[]{:S(2)}) collective-permute-start(f32[54,8,128]{2,1,0:T(8,128)} %get-tuple-element.16), channel_id=1, source_target_pairs={{0,1},{1,0},{2,3},{3,2},{4,5},{5,4},{6,7},{7,6},{8,9},{9,8},{10,11... | collective-permute-start | bytes 663560 | tf_op jit(solution)/shard_map/ppermute | solution.py:297
  23.4 0.8 %copy-start.1 = (f32[16,8,128]{2,1,0:T(8,128)S(1)}, f32[16,8,128]{2,1,0:T(8,128)}, u32[]{:S(2)}) copy-start(f32[16,8,128]{2,1,0:T(8,128)} %get-tuple-element.14.strips) | copy-start | bytes 196612

commit v2 on v0

v2 whole, which is shorter than its diff:
```python
import jax
import jax.numpy as jnp
from jax import lax
from jax.experimental import pallas as pl
from jax.experimental.pallas import tpu as pltpu
from jax.sharding import PartitionSpec as P

OV = 2
SWEEPS = 6
LOWER_END = 0.2
UPPER_END = 2.0
MIDDLE = 0.5 * (UPPER_END + LOWER_END)
SPREAD = 0.5 * (UPPER_END - LOWER_END)

NZ = 8
CR = 16
CA = 128
HALF = CA // 2
MIB = 1024 * 1024
DG = 2 * SWEEPS + 1
DK = DG + 1
TILES = 2 * DG + DK
SIDE = DG + OV
OWN = CR + 2 * OV
ROWS = 2 * SIDE + OWN
REACH = SWEEPS + 1
FAR_BOX = (-DG, SIDE, 0, 1)
OWN_BOX = (-OV, OWN, SIDE, SIDE + 2)
NEAR_BOX = (CR - OV, SIDE, SIDE + OWN, SIDE + OWN + 3)
GUARDED = ROWS + 4
TWIN = 3
GROUP = 8
STRIP = 7
RIGHT0 = 67
LEFT0 = 118
SPAN = 48
LEFT_AT = LEFT0 - RIGHT0


def coefficients():
    ratio = SPREAD / MIDDLE
    update = [1.0 / MIDDLE] + [0.0] * SWEEPS
    estimate = list(update)
    for _ in range(SWEEPS):
        image = [0.0] + estimate[:-1]
        remain = [float(n == 0) - e + i for n, (e, i) in enumerate(zip(estimate, image))]
        ratio_next = 1.0 / (2.0 * MIDDLE / SPREAD - ratio)
        update = [ratio_next * ratio * u + 2.0 * ratio_next / SPREAD * r for u, r in zip(update, remain)]
        estimate = [e + u for e, u in zip(estimate, update)]
        ratio = ratio_next
    return estimate


def lanes():
    return lax.broadcasted_iota(jnp.int32, (NZ, CA), 1)


def turn(value, by, axis=1):
    return pltpu.roll(value, by % value.shape[axis], axis)


def any_of(lane, *spans):
    mask = None
    for low, high in spans:
        here = (lane >= low) & (lane < high)
        mask = here if mask is None else mask | here
    return mask


def needed(layer):
    return (max(DK - 1 - layer, OV) + 1) // 2


def block_of(ref, first, count):
    return ref[pl.ds(first, count)]


def pack_block(fields, main, to_far, to_near, to_left, to_right):
    odd = lax.rem(lax.axis_index("row"), 2)
    lane = lax.broadcasted_iota(jnp.int32, (CR * NZ, CA), 1)
    order = jnp.where(lane < HALF, 2 * lane, 2 * lane - (CA - 1))
    left = right = jnp.zeros((CR * NZ, CA), jnp.float32)
    for number in range(3):
        rows = []
        for row in range(CR):
            at = pl.ds(odd * (CR - 1 - 2 * row) + row, NZ, stride=CR)
            rows.append(fields[number, at, :])
        field = jnp.take_along_axis(jnp.concatenate(rows), order, axis=1)
        rows = field.reshape(CR, NZ, CA)
        main[number] = rows
        depth = DK if number == 1 else DG
        start = (0, DG, DG + DK)[number]
        to_far[pl.ds(start, depth)] = jnp.stack([rows[depth - 1 - n] for n in range(depth)])
        to_near[pl.ds(start, depth)] = jnp.stack([rows[CR - 1 - n] for n in range(depth)])
        base = 16 * number
        left = jnp.where(any_of(lane, (base, base + 8)), turn(field, base), left)
        left = jnp.where(any_of(lane, (base + 8, base + 16)), turn(field, base + 8 - HALF), left)
        base = base + LEFT_AT
        right = jnp.where(any_of(lane, (base, base + 8)), turn(field, base + STRIP - HALF), right)
        right = jnp.where(any_of(lane, (base + 8, base + 16)), turn(field, base + 8 + STRIP - CA), right)
    half = CR * NZ // 2
    few = lane[:half] < SPAN
    to_left[...] = jnp.where(few, left[:half], turn(left[half:], SPAN)).reshape(CR // 2, NZ, CA)
    to_right[...] = jnp.where(few, turn(right[half:], -LEFT_AT), right[:half]).reshape(CR // 2, NZ, CA)


def slots(lane):
    return lax.rem(lane, 8), lax.rem(lane + 6, 8)


def pack_strips(from_right, from_left, strips, to_far, to_near):
    lane = lanes()
    in_right = lane < SPAN
    slot_right, slot_left = slots(lane)
    half = CR // 2
    rows = []
    for row in range(half):
        rows.append(jnp.where(in_right, from_right[row], from_left[row]))
    for row in range(half):
        rows.append(jnp.where(in_right, turn(from_right[row], -SPAN), turn(from_left[row], LEFT_AT)))
    strips[...] = jnp.stack(rows)
    around_left = any_of(lane, (LEFT_AT - 1, LEFT_AT + SPAN))
    for out, place in ((to_far, lambda q: q), (to_near, lambda q: CR - 1 - q)):
        for layer in range(DK // 2):
            first, second = needed(layer), needed(DK - 1 - layer)
            deep = rows[place(DK - 1 - layer)]
            takes_right = in_right & (slot_right >= 8 - second)
            takes_left = around_left & (slot_left >= 8 - first - second) & (slot_left < 8 - first)
            value = jnp.where(takes_left, turn(deep, -first), rows[place(layer)])
            out[layer] = jnp.where(takes_right, turn(deep, 8 - second), value)


def unpack_strips(pairs, lane):
    slot_right, slot_left = slots(lane)
    half = DK // 2
    near_part = [pairs[layer] for layer in range(half)]
    deep_part = []
    for layer in reversed(range(half)):
        first, second = needed(layer), needed(DK - 1 - layer)
        right = (lane < SPAN) & (slot_right < second)
        left = any_of(lane, (LEFT_AT, LEFT_AT + SPAN)) & (slot_left >= 8 - second)
        value = jnp.where(left, turn(pairs[layer], first), 0.0)
        deep_part.append(jnp.where(right, turn(pairs[layer], second - 8), value))
    return near_part + deep_part


def expand(block, strip, number, fill):
    lane = lax.broadcasted_iota(jnp.int32, block.shape, 2)
    beside = any_of(lane, (RIGHT0, RIGHT0 + STRIP), (LEFT0, LEFT0 + STRIP))
    tiles = []
    for colour in range(2):
        part = turn(block, HALF, 2) if colour else block
        value = jnp.where(beside, turn(strip, RIGHT0 - 16 * number - 8 * colour, 2), 0.0)
        tiles.append(jnp.where(lane < HALF, part, value))
    if fill:
        low = any_of(lane, (64, 65), (125, 126))
        high = any_of(lane, (66, 67), (127, 128))
        tiles = [jnp.where(low, turn(v, -TWIN, 2), jnp.where(high, turn(v, TWIN, 2), v)) for v in tiles]
    return jnp.stack(tiles, axis=1)


def spread(here, shift):
    level = lax.broadcasted_iota(jnp.int32, here.shape, 2)
    even, uneven = here[:, 0], here[:, 1]
    after, before = turn(even, -1, 2), turn(uneven, 1, 2)
    x_up = jnp.stack([uneven, after], axis=1)
    x_both = jnp.stack([uneven + before, even + after], axis=1)
    z_up = turn(here, -1, 2)
    z_both = jnp.where(level == NZ - 1, 0.0, z_up) + jnp.where(level == 0, 0.0, turn(here, 1, 2))
    part = shift + 3.0 * here + 0.5 * (z_both + x_both)
    return 0.5 * (here + x_up), jnp.where(level == NZ - 1, 0.0, 0.5 * (here + z_up)), part


def prepare_own(main, strips, rhs, cond, face_x, face_z, part):
    for first in range(0, CR, 8):
        at = pl.ds(first, 8)
        strip = strips[at]
        rhs[at] = expand(main[0, at], strip, 0, False)
        cond[at] = expand(main[1, at], strip, 1, True)
        shift = expand(main[2, at], strip, 2, True)
        face_x[at], face_z[at], part[at] = spread(cond[at], shift)


def solve_all(own_rhs, own_cond, own_x, own_z, own_part, far, near, far_strips, near_strips, out,
              cond, face_x, face_z, face_r, part, inverse, rhs, est_a, est_b, total):
    row_at = lax.axis_index("row")
    odd = lax.rem(row_at, 2)
    far_there = jnp.where(odd == 0, row_at > 0, row_at < lax.axis_size("row") - 1)
    far_level = far_there.astype(jnp.float32)
    far_tile = jnp.full((NZ, CA), far_level) > 0.5
    lane = lanes()

    own = pl.ds(DK, CR)
    cond[own] = own_cond[...]
    face_x[own] = own_x[...]
    face_z[own] = own_z[...]
    part[own] = own_part[...]
    p0, count, at, guarded = OWN_BOX
    zeros = jnp.zeros((1, 2, NZ, CA), jnp.float32)
    rhs[pl.ds(at + OV, CR)] = own_rhs[...]
    for row in (SIDE - 2, SIDE - 1, SIDE, SIDE + 1, SIDE + OWN - 2, SIDE + OWN - 1, SIDE + OWN, SIDE + OWN + 1):
        rhs[pl.ds(row, 1)] = zeros
    for est in (est_a, est_b):
        for row in (0, SIDE + 1, SIDE + OWN + 2, GUARDED - 1):
            est[pl.ds(row, 1)] = zeros

    for block, pairs, is_far in ((far, far_strips, True), (near, near_strips, False)):
        strip = unpack_strips(pairs, lane)
        strip = strip[::-1] if is_far else strip
        for low, high in ((0, 7), (7, DK)):
            at = pl.ds((0 if is_far else DK + CR) + low, high - low)
            cond[at] = expand(block[pl.ds(DG + low, high - low)], jnp.stack(strip[low:high]), 1, True)
        strip = strip[1:] if is_far else strip[:DG]
        for low, high in ((0, 7), (7, DG)):
            beside = jnp.stack(strip[low:high])
            at = pl.ds((0 if is_far else NEAR_BOX[2] + OV) + low, high - low)
            rhs[at] = expand(block[pl.ds(low, high - low)], beside, 0, False)
            shift = expand(block[pl.ds(DG + DK + low, high - low)], beside, 2, True)
            if is_far:
                shift = jnp.where(far_tile, shift, 1.0)
            at = pl.ds((1 if is_far else DK + CR) + low, high - low)
            face_x[at], face_z[at], part[at] = spread(cond[at], shift)

    for low in range(1, 2 * DG + CR + 2, 7):
        count = min(7, 2 * DG + CR + 2 - low)
        face_r[pl.ds(low, count)] = 0.5 * (cond[pl.ds(low - 1, count)] + cond[pl.ds(low, count)])

    both = lax.broadcasted_iota(jnp.int32, (2, NZ, CA), 2)
    in_box = any_of(both, (0, 65), (66, 74), (118, 126), (127, 128))
    core = any_of(both, (0, 64), (67, 74), (118, 125))

    def invert(box, first, count, has_below=True, has_above=True):
        p0, _, at, _ = box
        place = p0 + first + DK
        diagonal = part[pl.ds(place, count)]
        if has_below:
            diagonal += 0.5 * cond[pl.ds(place - 1, count)]
        if has_above:
            diagonal += 0.5 * cond[pl.ds(place + 1, count)]
        good = in_box & (diagonal > 0.0)
        inverse[pl.ds(at + first, count)] = jnp.where(good, 1.0 / jnp.where(good, diagonal, 1.0), 0.0)

    for low, high in ((0, 7), (7, SIDE - 1)):
        invert(FAR_BOX, low, high - low)
        invert(NEAR_BOX, low + 1, high - low)
    invert(FAR_BOX, SIDE - 1, 1, has_above=False)
    invert(NEAR_BOX, 0, 1, has_below=False)
    for low, high in ((1, 7), (7, 13), (13, OWN - 1)):
        invert(OWN_BOX, low, high - low)
    invert(OWN_BOX, 0, 1, has_below=False)
    invert(OWN_BOX, OWN - 1, 1, has_above=False)

    def around(p, count, here, below, above):
        at = pl.ds(p + DK, count)
        fx, fz = face_x[at], face_z[at]
        even, uneven = here[:, 0], here[:, 1]
        summed = face_r[at] * below + face_r[pl.ds(p + DK + 1, count)] * above
        summed += fz * turn(here, -1, 2) + turn(fz * here, 1, 2)
        sum_even = fx[:, 0] * uneven + turn(fx[:, 1] * uneven, 1, 2)
        sum_odd = fx[:, 0] * even + fx[:, 1] * turn(even, -1, 2)
        return summed + jnp.stack([sum_even, sum_odd], axis=1)

    powers = coefficients()

    def pieces(low, high):
        number = -(-(high - low) // GROUP)
        cuts = [low + (high - low) * n // number for n in range(number + 1)]
        return zip(cuts[:-1], cuts[1:])

    def solve(spans):
        for (p0, _, at, guarded), (low, high) in zip((FAR_BOX, OWN_BOX, NEAR_BOX), spans(0)):
            for first, last in pieces(low, high):
                here = pl.ds(at + first, last - first)
                est_a[pl.ds(guarded + first, last - first)] = powers[-1] * (inverse[here] * rhs[here])
        source, target = est_a, est_b
        for number, power in enumerate(reversed(powers[:-1])):
            for (p0, _, at, guarded), (low, high) in zip((FAR_BOX, OWN_BOX, NEAR_BOX), spans(number + 1)):
                for first, last in pieces(low, high):
                    count = last - first
                    here, below, above = [source[pl.ds(guarded + first + n, count)] for n in (0, -1, 1)]
                    summed = power * rhs[pl.ds(at + first, count)] + around(p0 + first, count, here, below, above)
                    target[pl.ds(guarded + first, count)] = inverse[pl.ds(at + first, count)] * summed
            source, target = target, source

    solve(lambda done: ((done, SIDE), (0, OWN), (0, SIDE - done)))
    est = est_a if SWEEPS % 2 == 0 else est_b

    to_low = any_of(both, (63, 65), (124, 126))
    to_high = any_of(both, (66, 68), (127, 128), (0, 1))

    def joined(value):
        other = jnp.where(to_low, turn(value, -TWIN, 3), jnp.where(to_high, turn(value, TWIN, 3), 0.0))
        return value + other

    def summed_boxes(p, count):
        value = None
        for p0, rows, _, guarded in (FAR_BOX, OWN_BOX, NEAR_BOX):
            if p0 <= p and p + count <= p0 + rows:
                share = est[pl.ds(guarded + p - p0, count)]
                value = share if value is None else value + share
        return value

    for low, high in ((-REACH, -OV), (-OV, 0), (0, OV), (OV, 8), (8, CR - OV), (CR - OV, CR + OV), (CR + OV, CR + REACH)):
        value = joined(summed_boxes(low, high - low))
        if low < 0:
            value = jnp.where(far_tile, value, 0.0)
        total[pl.ds(low + REACH, high - low)] = value

    def remainder(box, p, count):
        p0, _, at, _ = box
        here, below, above = [total[pl.ds(p + REACH + n, count)] for n in (0, -1, 1)]
        place = p + DK
        diagonal = part[pl.ds(place, count)] + 0.5 * (cond[pl.ds(place - 1, count)] + cond[pl.ds(place + 1, count)])
        summed = around(p, count, here, below, above)
        here_rhs = pl.ds(at + p - p0, count)
        value = jnp.where(core, rhs[here_rhs] - (diagonal * here - summed), 0.0)
        if p < 0:
            value = jnp.where(far_tile, value, 0.0)
        rhs[here_rhs] = value

    remainder(FAR_BOX, -SWEEPS, SWEEPS)
    for p in range(0, CR, 8):
        remainder(OWN_BOX, p, 8)
    remainder(NEAR_BOX, CR, SWEEPS)

    def second(done):
        cut = max(0, done + OV - SWEEPS)
        return (DG - SWEEPS + done, SIDE), (cut, OWN - cut), (0, SWEEPS + OV - done)

    solve(second)

    order = lax.div(lane, 2) + HALF * lax.rem(lane, 2)
    for low, high in ((0, OV), (OV, 8), (8, CR - OV), (CR - OV, CR)):
        value = joined(summed_boxes(low, high - low)) + total[pl.ds(low + REACH, high - low)]
        value = jnp.where(lane < HALF, value[:, 0], turn(value[:, 1], HALF, 2))
        value = value.reshape((high - low) * NZ, CA)
        value = jnp.take_along_axis(value, jnp.concatenate([order] * (high - low)), axis=1)
        for n in range(high - low):
            row = low + n
            out[pl.ds(odd * (CR - 1 - 2 * row) + row, NZ, stride=CR), :] = value[n * NZ : (n + 1) * NZ]


def call(kernel, outs, *args, scratch=(), limit=4):
    vmem = pl.BlockSpec(memory_space=pltpu.VMEM)
    return pl.pallas_call(
        kernel,
        out_shape=outs,
        in_specs=[vmem] * len(args),
        out_specs=jax.tree.map(lambda _: vmem, outs),
        scratch_shapes=scratch,
        compiler_params=pltpu.CompilerParams(vmem_limit_bytes=limit * MIB),
        name=kernel.__name__,
    )(*args)


def body(source, conduct, solid):
    aisles = lax.axis_size("aisle")
    rows = lax.axis_size("row")
    flat = (NZ * CR, CA)
    tile = lambda *lead: jax.ShapeDtypeStruct(lead + (NZ, CA), jnp.float32)
    fields = jnp.stack([source, conduct, 0.05 + 20.0 * solid.astype(jnp.float32)])
    main, to_far, to_near, to_left, to_right = call(
        pack_block,
        (tile(3, CR), tile(TILES), tile(TILES), tile(CR // 2), tile(CR // 2)),
        fields.reshape((3,) + flat),
    )
    up = [(i, (i + 1) % aisles) for i in range(aisles)]
    far_pairs = [(i, i + 1) for i in range(1, rows - 1, 2)]
    far_pairs += [(b, a) for a, b in far_pairs]
    near_pairs = [(i, i ^ 1) for i in range(rows)]
    from_left = lax.ppermute(to_right, "aisle", up)
    from_right = lax.ppermute(to_left, "aisle", [(b, a) for a, b in up])
    far = lax.ppermute(to_far, "row", far_pairs)
    near = lax.ppermute(to_near, "row", near_pairs)
    strips, strips_far, strips_near = call(
        pack_strips, (tile(CR), tile(DK // 2), tile(DK // 2)), from_right, from_left
    )
    far_strips = lax.ppermute(strips_far, "row", far_pairs)
    near_strips = lax.ppermute(strips_near, "row", near_pairs)
    own = call(prepare_own, (tile(CR, 2),) * 5, main, strips)
    pair_rows = lambda count: pltpu.VMEM((count, 2, NZ, CA), jnp.float32)
    around = CR + 2 * DK
    result = call(
        solve_all,
        jax.ShapeDtypeStruct(flat, jnp.float32),
        *own, far, near, far_strips, near_strips,
        scratch=[
            pair_rows(around), pair_rows(around), pair_rows(around), pair_rows(around), pair_rows(around),
            pair_rows(ROWS), pair_rows(ROWS), pair_rows(GUARDED), pair_rows(GUARDED), pair_rows(CR + 2 * REACH),
        ],
        limit=16,
    )
    return result.reshape(NZ, CR, CA)


def solution(mesh):
    spec = P(None, "row", "aisle")
    return jax.shard_map(body, mesh=mesh, in_specs=(spec, spec, spec), out_specs=spec, check_vma=False)
```

time: 66.5 us -> 23 us (0.35)
  the two profiles are of different devices: /device:TPU:8 before, /device:TPU:0 now
where the time goes in v2:
time: 23 us; the launch traced here: 22.8 us
  starting transfers between devices  12 us (52%)
  Pallas kernels  5.32 us (23%)
  waiting for transfers between devices  4.51 us (20%)
  other arithmetic  0.9 us (4%)
    ppermute x1, starting transfers between devices, body(): near = lax.ppermute(to_near, 'row', near_pairs)  5.79 us
    pallas_call x4, Pallas kernels, call(): pl.pallas_call(kernel, out_shape=outs, in_specs=[vmem] * len(args), out_s...  5.32 us
    ppermute x1, starting transfers between devices, body(): near_strips = lax.ppermute(strips_near, 'row', near_pairs)  4.35 us
    ppermute x1, waiting for transfers between devices, body(): from_left = lax.ppermute(to_right, 'aisle', up)  1.76 us
    ppermute x1, waiting for transfers between devices, body(): from_right = lax.ppermute(to_left, 'aisle', [(b, a) for a, b in up])  1.46 us
    ppermute x1, waiting for transfers between devices, body(): near_strips = lax.ppermute(strips_near, 'row', near_pairs)  1.28 us
    add x1, other arithmetic, body(): 0.05 + 20.0 * solid.astype(jnp.float32)  0.88 us
    ppermute x1, starting transfers between devices, body(): far = lax.ppermute(to_far, 'row', far_pairs)  0.67 us
  transfers between devices with their start and end apart: 6, of which 3 were waited for; matrix products, arithmetic and copies ran while one was open for 0% of the time, Pallas kernels for 3%

profile of v2, /device:TPU:0, one launch (start us, length us, event | category | flops | bytes accessed | tf_op | source)
XLA Modules:
  0.0 22.8 jit_solution(14362516016068479651)
XLA Ops:
  0.0 0.0 copy-start
  0.0 0.0 copy-start.1
  0.0 0.9 %multiply_add_fusion = f32[8,16,128]{2,1,0:T(8,128)S(1)} fusion(s32[8,16,128]{2,1,0:T(8,128)} %param.5), kind=kLoop, calls=%fused_computation.1 | loop fusion | flops 49152 | bytes 131072 | tf_op jit(solution)/shard_map/add | solution.py:361
  0.9 0.0 copy-done
  0.9 0.0 copy-done.1
  0.9 0.5 %pack_block.1 = (f32[3,16,8,128]{3,2,1,0:T(8,128)S(1)}, f32[40,8,128]{2,1,0:T(8,128)S(1)}, f32[40,8,128]{2,1,0:T(8,128)S(1)}, f32[8,8,128]{2,1,0:T(8,128)S(1)}, f32[8,8,128]{2,1,0:T(8,128)S(1)}) custom-call(f32[3,128,128]{2,1,0:T(8,128)S(1)} %pad_maximum_fusion.fields), custom_call_target="tpu_custom_call" | custom-call | tf_op jit(solution)/shard_map/pack_block/pallas_call | solution.py:345
  1.4 0.7 %collective-permute-start.2 = (f32[40,8,128]{2,1,0:T(8,128)S(1)}, f32[40,8,128]{2,1,0:T(8,128)S(1)}, u32[]{:S(2)}, u32[]{:S(2)}) collective-permute-start(f32[40,8,128]{2,1,0:T(8,128)S(1)} %get-tuple-element.27), channel_id=1, source_target_pairs={{1,2},{3,4},{5,6},{2,1},{4,3},{6,5},{9,10},{11,12},{13,14},{10,9},... | collective-permute-start | bytes 491528 | tf_op jit(solution)/shard_map/ppermute | solution.py:373
  2.1 5.8 %collective-permute-start.3 = (f32[40,8,128]{2,1,0:T(8,128)S(1)}, f32[40,8,128]{2,1,0:T(8,128)S(1)}, u32[]{:S(2)}, u32[]{:S(2)}) collective-permute-start(f32[40,8,128]{2,1,0:T(8,128)S(1)} %get-tuple-element.28), channel_id=1, source_target_pairs={{0,1},{1,0},{2,3},{3,2},{4,5},{5,4},{6,7},{7,6},{8,9},{9,8},{10,11... | collective-permute-start | bytes 491528 | tf_op jit(solution)/shard_map/ppermute | solution.py:374
  7.9 0.4 %collective-permute-start = (f32[8,8,128]{2,1,0:T(8,128)S(1)}, f32[8,8,128]{2,1,0:T(8,128)S(1)}, u32[]{:S(2)}, u32[]{:S(2)}) collective-permute-start(f32[8,8,128]{2,1,0:T(8,128)S(1)} %get-tuple-element.19), channel_id=1, source_target_pairs={{8,0},{16,8},{24,16},{0,24},{9,1},{17,9},{25,17},{1,25},{10,2},{18... | collective-permute-start | bytes 98312 | tf_op jit(solution)/shard_map/ppermute | solution.py:372
  8.2 0.1 collective-permute-start.1
  8.4 1.5 %collective-permute-done.from_right = f32[8,8,128]{2,1,0:T(8,128)S(1)} collective-permute-done((f32[8,8,128]{2,1,0:T(8,128)S(1)}, f32[8,8,128]{2,1,0:T(8,128)S(1)}, u32[]{:S(2)}, u32[]{:S(2)}) %collective-permute-start) | collective-permute-done | bytes 32800 | tf_op jit(solution)/shard_map/ppermute | solution.py:372
  9.8 1.8 %collective-permute-done.1.from_left = f32[8,8,128]{2,1,0:T(8,128)S(1)} collective-permute-done((f32[8,8,128]{2,1,0:T(8,128)S(1)}, f32[8,8,128]{2,1,0:T(8,128)S(1)}, u32[]{:S(2)}, u32[]{:S(2)}) %collective-permute-start.1) | collective-permute-done | bytes 32800 | tf_op jit(solution)/shard_map/ppermute | solution.py:371
  11.6 0.2 pack_strips.1
  11.8 0.7 %collective-permute-start.4 = (f32[7,8,128]{2,1,0:T(8,128)S(1)}, f32[7,8,128]{2,1,0:T(8,128)S(1)}, u32[]{:S(2)}, u32[]{:S(2)}) collective-permute-start(f32[7,8,128]{2,1,0:T(8,128)S(1)} %get-tuple-element.29), channel_id=1, source_target_pairs={{1,2},{3,4},{5,6},{2,1},{4,3},{6,5},{9,10},{11,12},{13,14},{10,9},... | collective-permute-start | bytes 86024 | tf_op jit(solution)/shard_map/ppermute | solution.py:378
  12.4 4.3 %collective-permute-start.5 = (f32[7,8,128]{2,1,0:T(8,128)S(1)}, f32[7,8,128]{2,1,0:T(8,128)S(1)}, u32[]{:S(2)}, u32[]{:S(2)}) collective-permute-start(f32[7,8,128]{2,1,0:T(8,128)S(1)} %get-tuple-element.30), channel_id=1, source_target_pairs={{0,1},{1,0},{2,3},{3,2},{4,5},{5,4},{6,7},{7,6},{8,9},{9,8},{10,11... | collective-permute-start | bytes 86024 | tf_op jit(solution)/shard_map/ppermute | solution.py:379
  16.8 0.6 %prepare_own.1 = (f32[16,2,8,128]{3,2,1,0:T(8,128)S(1)}, f32[16,2,8,128]{3,2,1,0:T(8,128)S(1)}, f32[16,2,8,128]{3,2,1,0:T(8,128)S(1)}, f32[16,2,8,128]{3,2,1,0:T(8,128)S(1)}, f32[16,2,8,128]{3,2,1,0:T(8,128)S(1)}) custom-call(f32[3,16,8,128]{3,2,1,0:T(8,128)S(1)} %get-tuple-element.18.main, f32[16,8,128]{2,1,0:T(8,128)S(1)} %get-tuple-element.21.strips), custom_call_target="tpu_custom_call" | custom-call | tf_op jit(solution)/shard_map/prepare_own/pallas_call | solution.py:345
  17.3 0.0 collective-permute-done.4.far_strips
  17.4 1.3 %collective-permute-done.5.near_strips = f32[7,8,128]{2,1,0:T(8,128)S(1)} collective-permute-done((f32[7,8,128]{2,1,0:T(8,128)S(1)}, f32[7,8,128]{2,1,0:T(8,128)S(1)}, u32[]{:S(2)}, u32[]{:S(2)}) %collective-permute-start.5) | collective-permute-done | bytes 28704 | tf_op jit(solution)/shard_map/ppermute | solution.py:379
  18.6 0.0 collective-permute-done.2.far
  18.6 0.0 collective-permute-done.3.near
  18.6 4.2 %solve_all.1 = f32[128,128]{1,0:T(8,128)} custom-call(f32[16,2,8,128]{3,2,1,0:T(8,128)S(1)} %get-tuple-element.22.own_rhs, f32[16,2,8,128]{3,2,1,0:T(8,128)S(1)} %get-tuple-element.23.own_cond, f32[16,2,8,128]{3,2,1,0:T(8,128)S(1)} %get-tuple-element.24.own_x, f32[16,2,8,128]{3,2,1,0:T(8,128)S(1)} %get-tuple-element.25.own_z, ...), custom_call_target="tpu_custom_call" | custom-call | tf_op jit(solution)/shard_map/solve_all/pallas_call | solution.py:345
  (1 shorter events, 0.0 us)
Async XLA Ops:
  0.0 0.9 %copy-start = (f32[8,16,128]{2,1,0:T(8,128)S(1)}, f32[8,16,128]{2,1,0:T(8,128)}, u32[]{:S(2)}) copy-start(f32[8,16,128]{2,1,0:T(8,128)} %param.4) | copy-start | bytes 196612
  0.0 0.9 %copy-start.1 = (f32[8,16,128]{2,1,0:T(8,128)S(1)}, f32[8,16,128]{2,1,0:T(8,128)}, u32[]{:S(2)}) copy-start(f32[8,16,128]{2,1,0:T(8,128)} %param.3) | copy-start | bytes 196612
  1.4 17.2 %collective-permute-start.2 = (f32[40,8,128]{2,1,0:T(8,128)S(1)}, f32[40,8,128]{2,1,0:T(8,128)S(1)}, u32[]{:S(2)}, u32[]{:S(2)}) collective-permute-start(f32[40,8,128]{2,1,0:T(8,128)S(1)} %get-tuple-element.27), channel_id=1, source_target_pairs={{1,2},{3,4},{5,6},{2,1},{4,3},{6,5},{9,10},{11,12},{13,14},{10,9},... | collective-permute-start | bytes 491528 | tf_op jit(solution)/shard_map/ppermute | solution.py:373
  2.1 16.6 %collective-permute-start.3 = (f32[40,8,128]{2,1,0:T(8,128)S(1)}, f32[40,8,128]{2,1,0:T(8,128)S(1)}, u32[]{:S(2)}, u32[]{:S(2)}) collective-permute-start(f32[40,8,128]{2,1,0:T(8,128)S(1)} %get-tuple-element.28), channel_id=1, source_target_pairs={{0,1},{1,0},{2,3},{3,2},{4,5},{5,4},{6,7},{7,6},{8,9},{9,8},{10,11... | collective-permute-start | bytes 491528 | tf_op jit(solution)/shard_map/ppermute | solution.py:374
  7.9 2.0 %collective-permute-start = (f32[8,8,128]{2,1,0:T(8,128)S(1)}, f32[8,8,128]{2,1,0:T(8,128)S(1)}, u32[]{:S(2)}, u32[]{:S(2)}) collective-permute-start(f32[8,8,128]{2,1,0:T(8,128)S(1)} %get-tuple-element.19), channel_id=1, source_target_pairs={{8,0},{16,8},{24,16},{0,24},{9,1},{17,9},{25,17},{1,25},{10,2},{18... | collective-permute-start | bytes 98312 | tf_op jit(solution)/shard_map/ppermute | solution.py:372
  8.2 3.4 %collective-permute-start.1 = (f32[8,8,128]{2,1,0:T(8,128)S(1)}, f32[8,8,128]{2,1,0:T(8,128)S(1)}, u32[]{:S(2)}, u32[]{:S(2)}) collective-permute-start(f32[8,8,128]{2,1,0:T(8,128)S(1)} %get-tuple-element.20), channel_id=1, source_target_pairs={{0,8},{8,16},{16,24},{24,0},{1,9},{9,17},{17,25},{25,1},{2,10},{10... | collective-permute-start | bytes 98312 | tf_op jit(solution)/shard_map/ppermute | solution.py:371
  11.8 5.6 %collective-permute-start.4 = (f32[7,8,128]{2,1,0:T(8,128)S(1)}, f32[7,8,128]{2,1,0:T(8,128)S(1)}, u32[]{:S(2)}, u32[]{:S(2)}) collective-permute-start(f32[7,8,128]{2,1,0:T(8,128)S(1)} %get-tuple-element.29), channel_id=1, source_target_pairs={{1,2},{3,4},{5,6},{2,1},{4,3},{6,5},{9,10},{11,12},{13,14},{10,9},... | collective-permute-start | bytes 86024 | tf_op jit(solution)/shard_map/ppermute | solution.py:378
  12.4 6.2 %collective-permute-start.5 = (f32[7,8,128]{2,1,0:T(8,128)S(1)}, f32[7,8,128]{2,1,0:T(8,128)S(1)}, u32[]{:S(2)}, u32[]{:S(2)}) collective-permute-start(f32[7,8,128]{2,1,0:T(8,128)S(1)} %get-tuple-element.30), channel_id=1, source_target_pairs={{0,1},{1,0},{2,3},{3,2},{4,5},{5,4},{6,7},{7,6},{8,9},{9,8},{10,11... | collective-permute-start | bytes 86024 | tf_op jit(solution)/shard_map/ppermute | solution.py:379

commit v3 on v2

--- a/solution.py
+++ b/solution.py
@@ -51,6 +51,10 @@
     return estimate
 
 
+LEAD = coefficients()[-1]
+POWERS = [power / LEAD for power in coefficients()[:-1]]
+
+
 def lanes():
     return lax.broadcasted_iota(jnp.int32, (NZ, CA), 1)
 
@@ -75,23 +79,18 @@
     return ref[pl.ds(first, count)]
 
 
-def pack_block(fields, main, to_far, to_near, to_left, to_right):
+def pack_edges(source, conduct, shift, main, to_other, to_pair):
     odd = lax.rem(lax.axis_index("row"), 2)
     lane = lax.broadcasted_iota(jnp.int32, (CR * NZ, CA), 1)
     order = jnp.where(lane < HALF, 2 * lane, 2 * lane - (CA - 1))
     left = right = jnp.zeros((CR * NZ, CA), jnp.float32)
-    for number in range(3):
+    for number, (field, scale) in enumerate(((source, 2.0 * LEAD), (conduct, 1.0), (shift, 1.0))):
         rows = []
         for row in range(CR):
             at = pl.ds(odd * (CR - 1 - 2 * row) + row, NZ, stride=CR)
-            rows.append(fields[number, at, :])
-        field = jnp.take_along_axis(jnp.concatenate(rows), order, axis=1)
-        rows = field.reshape(CR, NZ, CA)
-        main[number] = rows
-        depth = DK if number == 1 else DG
-        start = (0, DG, DG + DK)[number]
-        to_far[pl.ds(start, depth)] = jnp.stack([rows[depth - 1 - n] for n in range(depth)])
-        to_near[pl.ds(start, depth)] = jnp.stack([rows[CR - 1 - n] for n in range(depth)])
+            rows.append(field[at, :])
+        field = scale * jnp.take_along_axis(jnp.concatenate(rows), order, axis=1)
+        main[number] = field.reshape(CR, NZ, CA)
         base = 16 * number
         left = jnp.where(any_of(lane, (base, base + 8)), turn(field, base), left)
         left = jnp.where(any_of(lane, (base + 8, base + 16)), turn(field, base + 8 - HALF), left)
@@ -100,18 +99,36 @@
         right = jnp.where(any_of(lane, (base + 8, base + 16)), turn(field, base + 8 + STRIP - CA), right)
     half = CR * NZ // 2
     few = lane[:half] < SPAN
-    to_left[...] = jnp.where(few, left[:half], turn(left[half:], SPAN)).reshape(CR // 2, NZ, CA)
-    to_right[...] = jnp.where(few, turn(right[half:], -LEFT_AT), right[:half]).reshape(CR // 2, NZ, CA)
+    left = jnp.where(few, left[:half], turn(left[half:], SPAN)).reshape(CR // 2, NZ, CA)
+    right = jnp.where(few, turn(right[half:], -LEFT_AT), right[:half]).reshape(CR // 2, NZ, CA)
+    uneven = odd_aisle()
+    to_pair[...] = jnp.where(uneven, left, right)
+    to_other[...] = jnp.where(uneven, right, left)
+
+
+def odd_aisle():
+    return jnp.full((NZ, CA), lax.rem(lax.axis_index("aisle"), 2)) > 0
+
+
+def pack_rows(main, to_far, to_near):
+    start = 0
+    for number, depth in enumerate((DG, DK, DG)):
+        to_far[pl.ds(start, depth)] = jnp.stack([main[number, depth - 1 - n] for n in range(depth)])
+        to_near[pl.ds(start, depth)] = jnp.stack([main[number, CR - 1 - n] for n in range(depth)])
+        start += depth
 
 
 def slots(lane):
     return lax.rem(lane, 8), lax.rem(lane + 6, 8)
 
 
-def pack_strips(from_right, from_left, strips, to_far, to_near):
+def pack_strips(from_other, from_pair, strips, to_far, to_near):
     lane = lanes()
     in_right = lane < SPAN
     slot_right, slot_left = slots(lane)
+    uneven = odd_aisle()
+    from_right = jnp.where(uneven, from_other[...], from_pair[...])
+    from_left = jnp.where(uneven, from_pair[...], from_other[...])
     half = CR // 2
     rows = []
     for row in range(half):
@@ -167,8 +184,8 @@
     x_both = jnp.stack([uneven + before, even + after], axis=1)
     z_up = turn(here, -1, 2)
     z_both = jnp.where(level == NZ - 1, 0.0, z_up) + jnp.where(level == 0, 0.0, turn(here, 1, 2))
-    part = shift + 3.0 * here + 0.5 * (z_both + x_both)
-    return 0.5 * (here + x_up), jnp.where(level == NZ - 1, 0.0, 0.5 * (here + z_up)), part
+    part = shift + 6.0 * here + (z_both + x_both)
+    return here + x_up, jnp.where(level == NZ - 1, 0.0, here + z_up), part
 
 
 def prepare_own(main, strips, rhs, cond, face_x, face_z, part):
@@ -181,7 +198,7 @@
         face_x[at], face_z[at], part[at] = spread(cond[at], shift)
 
 
-def solve_all(own_rhs, own_cond, own_x, own_z, own_part, far, near, far_strips, near_strips, out,
+def solve_all(own_rhs, own_cond, own_x, own_z, own_part, near, far, far_strips, near_strips, out,
               cond, face_x, face_z, face_r, part, inverse, rhs, est_a, est_b, total):
     row_at = lax.axis_index("row")
     odd = lax.rem(row_at, 2)
@@ -217,13 +234,13 @@
             rhs[at] = expand(block[pl.ds(low, high - low)], beside, 0, False)
             shift = expand(block[pl.ds(DG + DK + low, high - low)], beside, 2, True)
             if is_far:
-                shift = jnp.where(far_tile, shift, 1.0)
+                shift = jnp.where(far_tile, shift, 2.0)
             at = pl.ds((1 if is_far else DK + CR) + low, high - low)
             face_x[at], face_z[at], part[at] = spread(cond[at], shift)
 
     for low in range(1, 2 * DG + CR + 2, 7):
         count = min(7, 2 * DG + CR + 2 - low)
-        face_r[pl.ds(low, count)] = 0.5 * (cond[pl.ds(low - 1, count)] + cond[pl.ds(low, count)])
+        face_r[pl.ds(low, count)] = cond[pl.ds(low - 1, count)] + cond[pl.ds(low, count)]
 
     both = lax.broadcasted_iota(jnp.int32, (2, NZ, CA), 2)
     in_box = any_of(both, (0, 65), (66, 74), (118, 126), (127, 128))
@@ -234,9 +251,9 @@
         place = p0 + first + DK
         diagonal = part[pl.ds(place, count)]
         if has_below:
-            diagonal += 0.5 * cond[pl.ds(place - 1, count)]
+            diagonal += cond[pl.ds(place - 1, count)]
         if has_above:
-            diagonal += 0.5 * cond[pl.ds(place + 1, count)]
+            diagonal += cond[pl.ds(place + 1, count)]
         good = in_box & (diagonal > 0.0)
         inverse[pl.ds(at + first, count)] = jnp.where(good, 1.0 / jnp.where(good, diagonal, 1.0), 0.0)
 
@@ -260,7 +277,6 @@
         sum_odd = fx[:, 0] * even + fx[:, 1] * turn(even, -1, 2)
         return summed + jnp.stack([sum_even, sum_odd], axis=1)
 
-    powers = coefficients()
 
     def pieces(low, high):
         number = -(-(high - low) // GROUP)
@@ -271,9 +287,9 @@
         for (p0, _, at, guarded), (low, high) in zip((FAR_BOX, OWN_BOX, NEAR_BOX), spans(0)):
             for first, last in pieces(low, high):
                 here = pl.ds(at + first, last - first)
-                est_a[pl.ds(guarded + first, last - first)] = powers[-1] * (inverse[here] * rhs[here])
+                est_a[pl.ds(guarded + first, last - first)] = inverse[here] * rhs[here]
         source, target = est_a, est_b
-        for number, power in enumerate(reversed(powers[:-1])):
+        for number, power in enumerate(reversed(POWERS)):
             for (p0, _, at, guarded), (low, high) in zip((FAR_BOX, OWN_BOX, NEAR_BOX), spans(number + 1)):
                 for first, last in pieces(low, high):
                     count = last - first
@@ -310,10 +326,10 @@
         p0, _, at, _ = box
         here, below, above = [total[pl.ds(p + REACH + n, count)] for n in (0, -1, 1)]
         place = p + DK
-        diagonal = part[pl.ds(place, count)] + 0.5 * (cond[pl.ds(place - 1, count)] + cond[pl.ds(place + 1, count)])
+        diagonal = part[pl.ds(place, count)] + (cond[pl.ds(place - 1, count)] + cond[pl.ds(place + 1, count)])
         summed = around(p, count, here, below, above)
         here_rhs = pl.ds(at + p - p0, count)
-        value = jnp.where(core, rhs[here_rhs] - (diagonal * here - summed), 0.0)
+        value = jnp.where(core, rhs[here_rhs] - LEAD * (diagonal * here - summed), 0.0)
         if p < 0:
             value = jnp.where(far_tile, value, 0.0)
         rhs[here_rhs] = value
@@ -340,7 +356,7 @@
             out[pl.ds(odd * (CR - 1 - 2 * row) + row, NZ, stride=CR), :] = value[n * NZ : (n + 1) * NZ]
 
 
-def call(kernel, outs, *args, scratch=(), limit=4):
+def call(kernel, outs, *args, scratch=(), limit=4, cost=None):
     vmem = pl.BlockSpec(memory_space=pltpu.VMEM)
     return pl.pallas_call(
         kernel,
@@ -349,6 +365,7 @@
         out_specs=jax.tree.map(lambda _: vmem, outs),
         scratch_shapes=scratch,
         compiler_params=pltpu.CompilerParams(vmem_limit_bytes=limit * MIB),
+        cost_estimate=cost,
         name=kernel.__name__,
     )(*args)
 
@@ -358,32 +375,37 @@
     rows = lax.axis_size("row")
     flat = (NZ * CR, CA)
     tile = lambda *lead: jax.ShapeDtypeStruct(lead + (NZ, CA), jnp.float32)
-    fields = jnp.stack([source, conduct, 0.05 + 20.0 * solid.astype(jnp.float32)])
-    main, to_far, to_near, to_left, to_right = call(
-        pack_block,
-        (tile(3, CR), tile(TILES), tile(TILES), tile(CR // 2), tile(CR // 2)),
-        fields.reshape((3,) + flat),
+    busy = pl.CostEstimate(flops=10**11, bytes_accessed=1024 * MIB, transcendentals=0)
+    shift = 0.1 + 40.0 * solid.astype(jnp.float32)
+    main, to_other, to_pair = call(
+        pack_edges, (tile(3, CR), tile(CR // 2), tile(CR // 2)),
+        source.reshape(flat), conduct.reshape(flat), shift.reshape(flat),
     )
-    up = [(i, (i + 1) % aisles) for i in range(aisles)]
+    pair = [(i, i ^ 1) for i in range(aisles)]
+    other = [(i, (i - 1 + 2 * (i % 2)) % aisles) for i in range(aisles)]
     far_pairs = [(i, i + 1) for i in range(1, rows - 1, 2)]
     far_pairs += [(b, a) for a, b in far_pairs]
     near_pairs = [(i, i ^ 1) for i in range(rows)]
-    from_left = lax.ppermute(to_right, "aisle", up)
-    from_right = lax.ppermute(to_left, "aisle", [(b, a) for a, b in up])
+    from_other = lax.ppermute(to_other, "aisle", other)
+    from_pair = lax.ppermute(to_pair, "aisle", pair)
+    to_far, to_near = call(
+        pack_rows, (tile(TILES), tile(TILES)), main,
+        cost=busy,
+    )
+    near = lax.ppermute(to_near, "row", near_pairs)
     far = lax.ppermute(to_far, "row", far_pairs)
-    near = lax.ppermute(to_near, "row", near_pairs)
     strips, strips_far, strips_near = call(
-        pack_strips, (tile(CR), tile(DK // 2), tile(DK // 2)), from_right, from_left
+        pack_strips, (tile(CR), tile(DK // 2), tile(DK // 2)), from_other, from_pair
     )
     far_strips = lax.ppermute(strips_far, "row", far_pairs)
     near_strips = lax.ppermute(strips_near, "row", near_pairs)
-    own = call(prepare_own, (tile(CR, 2),) * 5, main, strips)
+    own = call(prepare_own, (tile(CR, 2),) * 5, main, strips, cost=busy)
     pair_rows = lambda count: pltpu.VMEM((count, 2, NZ, CA), jnp.float32)
     around = CR + 2 * DK
     result = call(
         solve_all,
         jax.ShapeDtypeStruct(flat, jnp.float32),
-        *own, far, near, far_strips, near_strips,
+        *own, near, far, far_strips, near_strips,
         scratch=[
             pair_rows(around), pair_rows(around), pair_rows(around), pair_rows(around), pair_rows(around),
             pair_rows(ROWS), pair_rows(ROWS), pair_rows(GUARDED), pair_rows(GUARDED), pair_rows(CR + 2 * REACH),

time: 23 us -> 19.5 us (0.85)
  the two profiles are of different devices: /device:TPU:0 before, /device:TPU:8 now
where the time goes in v3:
time: 19.5 us; the launch traced here: 19.3 us
  starting transfers between devices  10.6 us (54%)
  Pallas kernels  5 us (26%)
  waiting for transfers between devices  2.81 us (14%)
  other arithmetic  0.88 us (5%)
    pallas_call x5, Pallas kernels, call(): pl.pallas_call(kernel, out_shape=outs, in_specs=[vmem] * len(args), out_s...  5 us
    ppermute x1, starting transfers between devices, body(): far_strips = lax.ppermute(strips_far, 'row', far_pairs)  4.44 us
    ppermute x1, starting transfers between devices, body(): far = lax.ppermute(to_far, 'row', far_pairs)  2.29 us
    ppermute x1, waiting for transfers between devices, body(): near_strips = lax.ppermute(strips_near, 'row', near_pairs)  1.6 us
    ppermute x1, starting transfers between devices, body(): near = lax.ppermute(to_near, 'row', near_pairs)  1.58 us
    ppermute x1, waiting for transfers between devices, body(): far_strips = lax.ppermute(strips_far, 'row', far_pairs)  1.19 us
    ppermute x1, starting transfers between devices, body(): from_other = lax.ppermute(to_other, 'aisle', other)  1 us
    add x1, other arithmetic, body(): shift = 0.1 + 40.0 * solid.astype(jnp.float32)  0.88 us
  transfers between devices with their start and end apart: 6, of which 2 were waited for; matrix products, arithmetic and copies ran while one was open for 0% of the time, Pallas kernels for 4%

profile of v3, /device:TPU:8, one launch (start us, length us, event | category | flops | bytes accessed | tf_op | source)
XLA Modules:
  0.0 19.3 jit_solution(12414603121578133498)
XLA Ops:
  0.0 0.0 copy-start
  0.0 0.0 copy-start.1
  0.0 0.9 %multiply_add_fusion = f32[8,16,128]{2,1,0:T(8,128)S(1)} fusion(s32[8,16,128]{2,1,0:T(8,128)} %param.5), kind=kLoop, calls=%fused_computation | loop fusion | flops 49152 | bytes 131072 | tf_op jit(solution)/shard_map/add | solution.py:379
  0.9 0.0 copy-done
  0.9 0.0 copy-done.1
  0.9 0.5 %pack_edges.1 = (f32[3,16,8,128]{3,2,1,0:T(8,128)S(1)}, f32[8,8,128]{2,1,0:T(8,128)S(1)}, f32[8,8,128]{2,1,0:T(8,128)S(1)}) custom-call(f32[128,128]{1,0:T(8,128)S(1)} %bitcast.5, f32[128,128]{1,0:T(8,128)S(1)} %bitcast.6, f32[128,128]{1,0:T(8,128)S(1)} %bitcast.4), custom_call_target="tpu_custom_call" | custom-call | tf_op jit(solution)/shard_map/pack_edges/pallas_call | solution.py:361
  1.4 1.0 %collective-permute-start = (f32[8,8,128]{2,1,0:T(8,128)S(1)}, f32[8,8,128]{2,1,0:T(8,128)S(1)}, u32[]{:S(2)}, u32[]{:S(2)}) collective-permute-start(f32[8,8,128]{2,1,0:T(8,128)S(1)} %get-tuple-element.19), channel_id=1, source_target_pairs={{0,24},{8,16},{16,8},{24,0},{1,25},{9,17},{17,9},{25,1},{2,26},{10... | collective-permute-start | bytes 98312 | tf_op jit(solution)/shard_map/ppermute | solution.py:389
  2.4 0.7 %collective-permute-start.1 = (f32[8,8,128]{2,1,0:T(8,128)S(1)}, f32[8,8,128]{2,1,0:T(8,128)S(1)}, u32[]{:S(2)}, u32[]{:S(2)}) collective-permute-start(f32[8,8,128]{2,1,0:T(8,128)S(1)} %get-tuple-element.20), channel_id=1, source_target_pairs={{0,8},{8,0},{16,24},{24,16},{1,9},{9,1},{17,25},{25,17},{2,10},{10... | collective-permute-start | bytes 98312 | tf_op jit(solution)/shard_map/ppermute | solution.py:390
  3.1 1.6 %collective-permute-start.2 = (f32[40,8,128]{2,1,0:T(8,128)S(1)}, f32[40,8,128]{2,1,0:T(8,128)S(1)}, u32[]{:S(2)}, u32[]{:S(2)}) collective-permute-start(f32[40,8,128]{2,1,0:T(8,128)S(1)} %get-tuple-element.27), channel_id=1, source_target_pairs={{0,1},{1,0},{2,3},{3,2},{4,5},{5,4},{6,7},{7,6},{8,9},{9,8},{10,11... | collective-permute-start | bytes 491528 | tf_op jit(solution)/shard_map/ppermute | solution.py:395
  4.7 2.3 %collective-permute-start.3 = (f32[40,8,128]{2,1,0:T(8,128)S(1)}, f32[40,8,128]{2,1,0:T(8,128)S(1)}, u32[]{:S(2)}, u32[]{:S(2)}) collective-permute-start(f32[40,8,128]{2,1,0:T(8,128)S(1)} %get-tuple-element.28), channel_id=1, source_target_pairs={{1,2},{3,4},{5,6},{2,1},{4,3},{6,5},{9,10},{11,12},{13,14},{10,9},... | collective-permute-start | bytes 491528 | tf_op jit(solution)/shard_map/ppermute | solution.py:396
  7.0 0.0 collective-permute-done.from_other
  7.0 0.0 collective-permute-done.1.from_pair
  7.0 0.2 pack_strips.1
  7.2 4.4 %collective-permute-start.4 = (f32[7,8,128]{2,1,0:T(8,128)S(1)}, f32[7,8,128]{2,1,0:T(8,128)S(1)}, u32[]{:S(2)}, u32[]{:S(2)}) collective-permute-start(f32[7,8,128]{2,1,0:T(8,128)S(1)} %get-tuple-element.29), channel_id=1, source_target_pairs={{1,2},{3,4},{5,6},{2,1},{4,3},{6,5},{9,10},{11,12},{13,14},{10,9},... | collective-permute-start | bytes 86024 | tf_op jit(solution)/shard_map/ppermute | solution.py:400
  11.6 0.6 %collective-permute-start.5 = (f32[7,8,128]{2,1,0:T(8,128)S(1)}, f32[7,8,128]{2,1,0:T(8,128)S(1)}, u32[]{:S(2)}, u32[]{:S(2)}) collective-permute-start(f32[7,8,128]{2,1,0:T(8,128)S(1)} %get-tuple-element.30), channel_id=1, source_target_pairs={{0,1},{1,0},{2,3},{3,2},{4,5},{5,4},{6,7},{7,6},{8,9},{9,8},{10,11... | collective-permute-start | bytes 86024 | tf_op jit(solution)/shard_map/ppermute | solution.py:401
  12.2 0.6 %prepare_own.1 = (f32[16,2,8,128]{3,2,1,0:T(8,128)S(1)}, f32[16,2,8,128]{3,2,1,0:T(8,128)S(1)}, f32[16,2,8,128]{3,2,1,0:T(8,128)S(1)}, f32[16,2,8,128]{3,2,1,0:T(8,128)S(1)}, f32[16,2,8,128]{3,2,1,0:T(8,128)S(1)}) custom-call(f32[3,16,8,128]{3,2,1,0:T(8,128)S(1)} %get-tuple-element.18.main, f32[16,8,128]{2,1,0:T(8,128)S(1)} %get-tuple-element.21.strips), custom_call_target="tpu_custom_call" | custom-call | flops 99999997952 | bytes 1073741824 | tf_op jit(solution)/shard_map/prepare_own/pallas_call | solution.py:361
  12.7 1.2 %collective-permute-done.4.far_strips = f32[7,8,128]{2,1,0:T(8,128)S(1)} collective-permute-done((f32[7,8,128]{2,1,0:T(8,128)S(1)}, f32[7,8,128]{2,1,0:T(8,128)S(1)}, u32[]{:S(2)}, u32[]{:S(2)}) %collective-permute-start.4) | collective-permute-done | bytes 28704 | tf_op jit(solution)/shard_map/ppermute | solution.py:400
  13.9 1.6 %collective-permute-done.5.near_strips = f32[7,8,128]{2,1,0:T(8,128)S(1)} collective-permute-done((f32[7,8,128]{2,1,0:T(8,128)S(1)}, f32[7,8,128]{2,1,0:T(8,128)S(1)}, u32[]{:S(2)}, u32[]{:S(2)}) %collective-permute-start.5) | collective-permute-done | bytes 28704 | tf_op jit(solution)/shard_map/ppermute | solution.py:401
  15.5 0.0 collective-permute-done.2.near
  15.5 0.0 collective-permute-done.3.far
  15.6 3.8 %solve_all.1 = f32[128,128]{1,0:T(8,128)} custom-call(f32[16,2,8,128]{3,2,1,0:T(8,128)S(1)} %get-tuple-element.22.own_rhs, f32[16,2,8,128]{3,2,1,0:T(8,128)S(1)} %get-tuple-element.23.own_cond, f32[16,2,8,128]{3,2,1,0:T(8,128)S(1)} %get-tuple-element.24.own_x, f32[16,2,8,128]{3,2,1,0:T(8,128)S(1)} %get-tuple-element.25.own_z, ...), custom_call_target="tpu_custom_call" | custom-call | tf_op jit(solution)/shard_map/solve_all/pallas_call | solution.py:361
  (1 shorter events, 0.0 us)
Async XLA Ops:
  0.0 0.9 %copy-start = (f32[8,16,128]{2,1,0:T(8,128)S(1)}, f32[8,16,128]{2,1,0:T(8,128)}, u32[]{:S(2)}) copy-start(f32[8,16,128]{2,1,0:T(8,128)} %param.3) | copy-start | bytes 196612
  0.0 0.9 %copy-start.1 = (f32[8,16,128]{2,1,0:T(8,128)S(1)}, f32[8,16,128]{2,1,0:T(8,128)}, u32[]{:S(2)}) copy-start(f32[8,16,128]{2,1,0:T(8,128)} %param.4) | copy-start | bytes 196612
  1.4 5.6 %collective-permute-start = (f32[8,8,128]{2,1,0:T(8,128)S(1)}, f32[8,8,128]{2,1,0:T(8,128)S(1)}, u32[]{:S(2)}, u32[]{:S(2)}) collective-permute-start(f32[8,8,128]{2,1,0:T(8,128)S(1)} %get-tuple-element.19), channel_id=1, source_target_pairs={{0,24},{8,16},{16,8},{24,0},{1,25},{9,17},{17,9},{25,1},{2,26},{10... | collective-permute-start | bytes 98312 | tf_op jit(solution)/shard_map/ppermute | solution.py:389
  2.4 4.6 %collective-permute-start.1 = (f32[8,8,128]{2,1,0:T(8,128)S(1)}, f32[8,8,128]{2,1,0:T(8,128)S(1)}, u32[]{:S(2)}, u32[]{:S(2)}) collective-permute-start(f32[8,8,128]{2,1,0:T(8,128)S(1)} %get-tuple-element.20), channel_id=1, source_target_pairs={{0,8},{8,0},{16,24},{24,16},{1,9},{9,1},{17,25},{25,17},{2,10},{10... | collective-permute-start | bytes 98312 | tf_op jit(solution)/shard_map/ppermute | solution.py:390
  3.1 12.5 %collective-permute-start.2 = (f32[40,8,128]{2,1,0:T(8,128)S(1)}, f32[40,8,128]{2,1,0:T(8,128)S(1)}, u32[]{:S(2)}, u32[]{:S(2)}) collective-permute-start(f32[40,8,128]{2,1,0:T(8,128)S(1)} %get-tuple-element.27), channel_id=1, source_target_pairs={{0,1},{1,0},{2,3},{3,2},{4,5},{5,4},{6,7},{7,6},{8,9},{9,8},{10,11... | collective-permute-start | bytes 491528 | tf_op jit(solution)/shard_map/ppermute | solution.py:395
  4.7 10.9 %collective-permute-start.3 = (f32[40,8,128]{2,1,0:T(8,128)S(1)}, f32[40,8,128]{2,1,0:T(8,128)S(1)}, u32[]{:S(2)}, u32[]{:S(2)}) collective-permute-start(f32[40,8,128]{2,1,0:T(8,128)S(1)} %get-tuple-element.28), channel_id=1, source_target_pairs={{1,2},{3,4},{5,6},{2,1},{4,3},{6,5},{9,10},{11,12},{13,14},{10,9},... | collective-permute-start | bytes 491528 | tf_op jit(solution)/shard_map/ppermute | solution.py:396
  7.2 6.8 %collective-permute-start.4 = (f32[7,8,128]{2,1,0:T(8,128)S(1)}, f32[7,8,128]{2,1,0:T(8,128)S(1)}, u32[]{:S(2)}, u32[]{:S(2)}) collective-permute-start(f32[7,8,128]{2,1,0:T(8,128)S(1)} %get-tuple-element.29), channel_id=1, source_target_pairs={{1,2},{3,4},{5,6},{2,1},{4,3},{6,5},{9,10},{11,12},{13,14},{10,9},... | collective-permute-start | bytes 86024 | tf_op jit(solution)/shard_map/ppermute | solution.py:400
  11.6 3.9 %collective-permute-start.5 = (f32[7,8,128]{2,1,0:T(8,128)S(1)}, f32[7,8,128]{2,1,0:T(8,128)S(1)}, u32[]{:S(2)}, u32[]{:S(2)}) collective-permute-start(f32[7,8,128]{2,1,0:T(8,128)S(1)} %get-tuple-element.30), channel_id=1, source_target_pairs={{0,1},{1,0},{2,3},{3,2},{4,5},{5,4},{6,7},{7,6},{8,9},{9,8},{10,11... | collective-permute-start | bytes 86024 | tf_op jit(solution)/shard_map/ppermute | solution.py:401

commit v4 on v3

--- a/solution.py
+++ b/solution.py
@@ -81,26 +81,33 @@
 
 def pack_edges(source, conduct, shift, main, to_other, to_pair):
     odd = lax.rem(lax.axis_index("row"), 2)
-    lane = lax.broadcasted_iota(jnp.int32, (CR * NZ, CA), 1)
+    half = CR // 2
+    shape = (half * NZ, CA)
+    lane = lax.broadcasted_iota(jnp.int32, shape, 1)
     order = jnp.where(lane < HALF, 2 * lane, 2 * lane - (CA - 1))
-    left = right = jnp.zeros((CR * NZ, CA), jnp.float32)
+
+    def edge(slot, first):
+        return first + 2 * lax.rem(slot, 8) + lax.rem(lax.div(slot, 8), 2)
+
+    end = CA - 2 * STRIP
+    left_order = edge(lane, 0)
+    right_order = jnp.where(lane < SPAN, edge(lane, end), edge(lane + (16 * 4 - LEFT_AT), end))
+    right_order = jnp.minimum(right_order, CA - 1)
+    pick = lambda value, index: jnp.take_along_axis(value, index, axis=1)
+    left = right = jnp.zeros(shape, jnp.float32)
     for number, (field, scale) in enumerate(((source, 2.0 * LEAD), (conduct, 1.0), (shift, 1.0))):
-        rows = []
-        for row in range(CR):
-            at = pl.ds(odd * (CR - 1 - 2 * row) + row, NZ, stride=CR)
-            rows.append(field[at, :])
-        field = scale * jnp.take_along_axis(jnp.concatenate(rows), order, axis=1)
-        main[number] = field.reshape(CR, NZ, CA)
-        base = 16 * number
-        left = jnp.where(any_of(lane, (base, base + 8)), turn(field, base), left)
-        left = jnp.where(any_of(lane, (base + 8, base + 16)), turn(field, base + 8 - HALF), left)
-        base = base + LEFT_AT
-        right = jnp.where(any_of(lane, (base, base + 8)), turn(field, base + STRIP - HALF), right)
-        right = jnp.where(any_of(lane, (base + 8, base + 16)), turn(field, base + 8 + STRIP - CA), right)
-    half = CR * NZ // 2
-    few = lane[:half] < SPAN
-    left = jnp.where(few, left[:half], turn(left[half:], SPAN)).reshape(CR // 2, NZ, CA)
-    right = jnp.where(few, turn(right[half:], -LEFT_AT), right[:half]).reshape(CR // 2, NZ, CA)
+        for part in range(2):
+            rows = []
+            for row in range(part * half, (part + 1) * half):
+                rows.append(field[pl.ds(odd * (CR - 1 - 2 * row) + row, NZ, stride=CR), :])
+            rows = scale * jnp.concatenate(rows)
+            main[number, pl.ds(part * half, half)] = pick(rows, order).reshape(half, NZ, CA)
+            base = part * SPAN + 16 * number
+            left = jnp.where(any_of(lane, (base, base + 16)), pick(rows, left_order), left)
+            base = (1 - part) * LEFT_AT + 16 * number
+            right = jnp.where(any_of(lane, (base, base + 16)), pick(rows, right_order), right)
+    left = left.reshape(half, NZ, CA)
+    right = right.reshape(half, NZ, CA)
     uneven = odd_aisle()
     to_pair[...] = jnp.where(uneven, left, right)
     to_other[...] = jnp.where(uneven, right, left)
@@ -161,7 +168,7 @@
     return near_part + deep_part
 
 
-def expand(block, strip, number, fill):
+def merge(block, strip, number):
     lane = lax.broadcasted_iota(jnp.int32, block.shape, 2)
     beside = any_of(lane, (RIGHT0, RIGHT0 + STRIP), (LEFT0, LEFT0 + STRIP))
     tiles = []
@@ -169,11 +176,14 @@
         part = turn(block, HALF, 2) if colour else block
         value = jnp.where(beside, turn(strip, RIGHT0 - 16 * number - 8 * colour, 2), 0.0)
         tiles.append(jnp.where(lane < HALF, part, value))
-    if fill:
-        low = any_of(lane, (64, 65), (125, 126))
-        high = any_of(lane, (66, 67), (127, 128))
-        tiles = [jnp.where(low, turn(v, -TWIN, 2), jnp.where(high, turn(v, TWIN, 2), v)) for v in tiles]
     return jnp.stack(tiles, axis=1)
+
+
+def fill(tiles):
+    lane = lax.broadcasted_iota(jnp.int32, tiles.shape, 3)
+    low = any_of(lane, (64, 65), (125, 126))
+    high = any_of(lane, (66, 67), (127, 128))
+    return jnp.where(low, turn(tiles, -TWIN, 3), jnp.where(high, turn(tiles, TWIN, 3), tiles))
 
 
 def spread(here, shift):
@@ -188,17 +198,58 @@
     return here + x_up, jnp.where(level == NZ - 1, 0.0, here + z_up), part
 
 
-def prepare_own(main, strips, rhs, cond, face_x, face_z, part):
-    for first in range(0, CR, 8):
-        at = pl.ds(first, 8)
+def pieces(low, high):
+    number = -(-(high - low) // GROUP)
+    cuts = [low + (high - low) * n // number for n in range(number + 1)]
+    return [(first, last - first) for first, last in zip(cuts[:-1], cuts[1:])]
+
+
+def inverted(diagonal):
+    both = lax.broadcasted_iota(jnp.int32, (2, NZ, CA), 2)
+    good = any_of(both, (0, 65), (66, 74), (118, 126), (127, 128)) & (diagonal > 0.0)
+    return jnp.where(good, 1.0 / jnp.where(good, diagonal, 1.0), 0.0)
+
+
+def around(weights, row, count, here, below, above):
+    face_x, face_z, face_r = weights
+    at = pl.ds(row, count)
+    fx, fz = face_x[at], face_z[at]
+    even, uneven = here[:, 0], here[:, 1]
+    summed = face_r[at] * below + face_r[pl.ds(row + 1, count)] * above
+    summed += fz * turn(here, -1, 2) + turn(fz * here, 1, 2)
+    sum_even = fx[:, 0] * uneven + turn(fx[:, 1] * uneven, 1, 2)
+    sum_odd = fx[:, 0] * even + fx[:, 1] * turn(even, -1, 2)
+    return summed + jnp.stack([sum_even, sum_odd], axis=1)
+
+
+def prepare_own(main, strips, rhs, cond, face_x, face_z, face_r, part, inverse, levels):
+    halves = [pl.ds(first, 8) for first in range(0, CR, 8)]
+    for at in halves:
         strip = strips[at]
-        rhs[at] = expand(main[0, at], strip, 0, False)
-        cond[at] = expand(main[1, at], strip, 1, True)
-        shift = expand(main[2, at], strip, 2, True)
-        face_x[at], face_z[at], part[at] = spread(cond[at], shift)
-
-
-def solve_all(own_rhs, own_cond, own_x, own_z, own_part, near, far, far_strips, near_strips, out,
+        cond[at] = merge(main[1, at], strip, 1)
+        part[at] = merge(main[2, at], strip, 2)
+        rhs[at] = merge(main[0, at], strip, 0)
+    for at in halves:
+        cond[at] = fill(cond[at])
+        part[at] = fill(part[at])
+    for at in halves:
+        face_x[at], face_z[at], part[at] = spread(cond[at], part[at])
+    face_r[pl.ds(0, 1)] = jnp.zeros((1, 2, NZ, CA), jnp.float32)
+    for first, count in pieces(1, CR):
+        face_r[pl.ds(first, count)] = cond[pl.ds(first - 1, count)] + cond[pl.ds(first, count)]
+    for first, count in pieces(1, CR - 1):
+        at = pl.ds(first, count)
+        inverse[at] = inverted(part[at] + (cond[pl.ds(first - 1, count)] + cond[pl.ds(first + 1, count)]))
+        levels[0, at] = inverse[at] * rhs[at]
+    weights = face_x, face_z, face_r
+    for done, power in enumerate(reversed(POWERS)):
+        for first, count in pieces(2 + done, CR - 2 - done):
+            here, below, above = [levels[done, pl.ds(first + n, count)] for n in (0, -1, 1)]
+            at = pl.ds(first, count)
+            levels[done + 1, at] = inverse[at] * (power * rhs[at] + around(weights, first, count, here, below, above))
+
+
+def solve_all(own_rhs, own_cond, own_x, own_z, own_r, own_part, own_inverse, levels, near, far, far_strips, near_strips, out,
               cond, face_x, face_z, face_r, part, inverse, rhs, est_a, est_b, total):
     row_at = lax.axis_index("row")
     odd = lax.rem(row_at, 2)
@@ -221,29 +272,39 @@
         for row in (0, SIDE + 1, SIDE + OWN + 2, GUARDED - 1):
             est[pl.ds(row, 1)] = zeros
 
-    for block, pairs, is_far in ((far, far_strips, True), (near, near_strips, False)):
-        strip = unpack_strips(pairs, lane)
-        strip = strip[::-1] if is_far else strip
+    sides = [(far, unpack_strips(far_strips, lane)[::-1], True), (near, unpack_strips(near_strips, lane), False)]
+    for block, strip, is_far in sides:
         for low, high in ((0, 7), (7, DK)):
             at = pl.ds((0 if is_far else DK + CR) + low, high - low)
-            cond[at] = expand(block[pl.ds(DG + low, high - low)], jnp.stack(strip[low:high]), 1, True)
+            cond[at] = merge(block[pl.ds(DG + low, high - low)], jnp.stack(strip[low:high]), 1)
         strip = strip[1:] if is_far else strip[:DG]
         for low, high in ((0, 7), (7, DG)):
             beside = jnp.stack(strip[low:high])
+            at = pl.ds((1 if is_far else DK + CR) + low, high - low)
+            part[at] = merge(block[pl.ds(DG + DK + low, high - low)], beside, 2)
             at = pl.ds((0 if is_far else NEAR_BOX[2] + OV) + low, high - low)
-            rhs[at] = expand(block[pl.ds(low, high - low)], beside, 0, False)
-            shift = expand(block[pl.ds(DG + DK + low, high - low)], beside, 2, True)
-            if is_far:
+            rhs[at] = merge(block[pl.ds(low, high - low)], beside, 0)
+    for first in (0, DK + CR):
+        for low, high in ((0, 7), (7, DK)):
+            at = pl.ds(first + low, high - low)
+            cond[at] = fill(cond[at])
+        for low, high in ((0, 7), (7, DG)):
+            at = pl.ds((first or 1) + low, high - low)
+            part[at] = fill(part[at])
+    for first in (1, DK + CR):
+        for low, high in ((0, 7), (7, DG)):
+            at = pl.ds(first + low, high - low)
+            shift = part[at]
+            if first == 1:
                 shift = jnp.where(far_tile, shift, 2.0)
-            at = pl.ds((1 if is_far else DK + CR) + low, high - low)
             face_x[at], face_z[at], part[at] = spread(cond[at], shift)
 
-    for low in range(1, 2 * DG + CR + 2, 7):
-        count = min(7, 2 * DG + CR + 2 - low)
-        face_r[pl.ds(low, count)] = cond[pl.ds(low - 1, count)] + cond[pl.ds(low, count)]
+    face_r[pl.ds(DK + 1, CR - 1)] = own_r[pl.ds(1, CR - 1)]
+    for first, last in ((1, DK + 1), (DK + CR, 2 * DG + CR + 2)):
+        for low, count in pieces(first, last):
+            face_r[pl.ds(low, count)] = cond[pl.ds(low - 1, count)] + cond[pl.ds(low, count)]
 
     both = lax.broadcasted_iota(jnp.int32, (2, NZ, CA), 2)
-    in_box = any_of(both, (0, 65), (66, 74), (118, 126), (127, 128))
     core = any_of(both, (0, 64), (67, 74), (118, 125))
 
     def invert(box, first, count, has_below=True, has_above=True):
@@ -254,51 +315,49 @@
             diagonal += cond[pl.ds(place - 1, count)]
         if has_above:
             diagonal += cond[pl.ds(place + 1, count)]
-        good = in_box & (diagonal > 0.0)
-        inverse[pl.ds(at + first, count)] = jnp.where(good, 1.0 / jnp.where(good, diagonal, 1.0), 0.0)
+        inverse[pl.ds(at + first, count)] = inverted(diagonal)
 
     for low, high in ((0, 7), (7, SIDE - 1)):
         invert(FAR_BOX, low, high - low)
         invert(NEAR_BOX, low + 1, high - low)
     invert(FAR_BOX, SIDE - 1, 1, has_above=False)
     invert(NEAR_BOX, 0, 1, has_below=False)
-    for low, high in ((1, 7), (7, 13), (13, OWN - 1)):
-        invert(OWN_BOX, low, high - low)
+    inverse[pl.ds(OWN_BOX[2] + OV + 1, CR - 2)] = own_inverse[pl.ds(1, CR - 2)]
+    for low in (1, OV + CR - 1):
+        invert(OWN_BOX, low, OV)
     invert(OWN_BOX, 0, 1, has_below=False)
     invert(OWN_BOX, OWN - 1, 1, has_above=False)
 
-    def around(p, count, here, below, above):
-        at = pl.ds(p + DK, count)
-        fx, fz = face_x[at], face_z[at]
-        even, uneven = here[:, 0], here[:, 1]
-        summed = face_r[at] * below + face_r[pl.ds(p + DK + 1, count)] * above
-        summed += fz * turn(here, -1, 2) + turn(fz * here, 1, 2)
-        sum_even = fx[:, 0] * uneven + turn(fx[:, 1] * uneven, 1, 2)
-        sum_odd = fx[:, 0] * even + fx[:, 1] * turn(even, -1, 2)
-        return summed + jnp.stack([sum_even, sum_odd], axis=1)
-
-
-    def pieces(low, high):
-        number = -(-(high - low) // GROUP)
-        cuts = [low + (high - low) * n // number for n in range(number + 1)]
-        return zip(cuts[:-1], cuts[1:])
-
-    def solve(spans):
-        for (p0, _, at, guarded), (low, high) in zip((FAR_BOX, OWN_BOX, NEAR_BOX), spans(0)):
-            for first, last in pieces(low, high):
-                here = pl.ds(at + first, last - first)
-                est_a[pl.ds(guarded + first, last - first)] = inverse[here] * rhs[here]
+    weights = face_x, face_z, face_r
+
+    def solve(spans, borrow):
+        for p0, _, at, guarded, low, high in spans(0):
+            for first, count in pieces(low, high):
+                here = pl.ds(at + first, count)
+                est_a[pl.ds(guarded + first, count)] = inverse[here] * rhs[here]
         source, target = est_a, est_b
-        for number, power in enumerate(reversed(POWERS)):
-            for (p0, _, at, guarded), (low, high) in zip((FAR_BOX, OWN_BOX, NEAR_BOX), spans(number + 1)):
-                for first, last in pieces(low, high):
-                    count = last - first
+        for done, power in enumerate(reversed(POWERS)):
+            borrow(done, source)
+            for p0, _, at, guarded, low, high in spans(done + 1):
+                for first, count in pieces(low, high):
                     here, below, above = [source[pl.ds(guarded + first + n, count)] for n in (0, -1, 1)]
-                    summed = power * rhs[pl.ds(at + first, count)] + around(p0 + first, count, here, below, above)
+                    summed = power * rhs[pl.ds(at + first, count)]
+                    summed += around(weights, p0 + first + DK, count, here, below, above)
                     target[pl.ds(guarded + first, count)] = inverse[pl.ds(at + first, count)] * summed
             source, target = target, source
-
-    solve(lambda done: ((done, SIDE), (0, OWN), (0, SIDE - done)))
+        borrow(SWEEPS, source)
+
+    def first_spans(done):
+        low = (0, OV + 1 + done)
+        high = (OWN - OV - 1 - done, OWN)
+        return (FAR_BOX + (done, SIDE), NEAR_BOX + (0, SIDE - done), OWN_BOX + low, OWN_BOX + high)
+
+    def from_own(done, est):
+        rows = (7, 8) if done == SWEEPS else (done + 1, done + 2, CR - 3 - done, CR - 2 - done)
+        for p in rows:
+            est[pl.ds(OWN_BOX[3] + OV + p, 1)] = levels[done, pl.ds(p, 1)]
+
+    solve(first_spans, from_own)
     est = est_a if SWEEPS % 2 == 0 else est_b
 
     to_low = any_of(both, (63, 65), (124, 126))
@@ -327,7 +386,7 @@
         here, below, above = [total[pl.ds(p + REACH + n, count)] for n in (0, -1, 1)]
         place = p + DK
         diagonal = part[pl.ds(place, count)] + (cond[pl.ds(place - 1, count)] + cond[pl.ds(place + 1, count)])
-        summed = around(p, count, here, below, above)
+        summed = around(weights, p + DK, count, here, below, above)
         here_rhs = pl.ds(at + p - p0, count)
         value = jnp.where(core, rhs[here_rhs] - LEAD * (diagonal * here - summed), 0.0)
         if p < 0:
@@ -339,11 +398,13 @@
         remainder(OWN_BOX, p, 8)
     remainder(NEAR_BOX, CR, SWEEPS)
 
-    def second(done):
+    def second_spans(done):
         cut = max(0, done + OV - SWEEPS)
-        return (DG - SWEEPS + done, SIDE), (cut, OWN - cut), (0, SWEEPS + OV - done)
-
-    solve(second)
+        return (
+            FAR_BOX + (DG - SWEEPS + done, SIDE), OWN_BOX + (cut, OWN - cut), NEAR_BOX + (0, SWEEPS + OV - done)
+        )
+
+    solve(second_spans, lambda done, est: None)
 
     order = lax.div(lane, 2) + HALF * lax.rem(lane, 2)
     for low, high in ((0, OV), (OV, 8), (8, CR - OV), (CR - OV, CR)):
@@ -399,7 +460,8 @@
     )
     far_strips = lax.ppermute(strips_far, "row", far_pairs)
     near_strips = lax.ppermute(strips_near, "row", near_pairs)
-    own = call(prepare_own, (tile(CR, 2),) * 5, main, strips, cost=busy)
+    own_rows = (tile(CR, 2),) * 7 + (tile(SWEEPS + 1, CR, 2),)
+    own = call(prepare_own, own_rows, main, strips, limit=8, cost=busy)
     pair_rows = lambda count: pltpu.VMEM((count, 2, NZ, CA), jnp.float32)
     around = CR + 2 * DK
     result = call(

time: 19.5 us -> 18.9 us (0.969)
  Pallas kernels: 5 us -> 4.62 us
  waiting for transfers between devices: 2.81 us -> 2.61 us
    pallas_call x5, Pallas kernels: 5 us -> 4.62 us  [call(): pl.pallas_call(kernel, out_shape=outs, in_specs=[vmem] * len(args), out_s...]
  transfers between devices with their start and end apart: 6 -> 6, of which waited for: 2 -> 2; matrix products, arithmetic and copies ran while one was open for 0% -> 0% of each run, Pallas kernels for 4% -> 5%
where the time goes in v4:
time: 18.9 us; the launch traced here: 18.8 us
  starting transfers between devices  10.6 us (56%)
  Pallas kernels  4.62 us (24%)
  waiting for transfers between devices  2.61 us (14%)
  other arithmetic  0.88 us (5%)
    pallas_call x5, Pallas kernels, call(): pl.pallas_call(kernel, out_shape=outs, in_specs=[vmem] * len(args), out_s...  4.62 us
    ppermute x1, starting transfers between devices, body(): far_strips = lax.ppermute(strips_far, 'row', far_pairs)  4.44 us
    ppermute x1, starting transfers between devices, body(): far = lax.ppermute(to_far, 'row', far_pairs)  2.29 us
    ppermute x1, waiting for transfers between devices, body(): near_strips = lax.ppermute(strips_near, 'row', near_pairs)  1.6 us
    ppermute x1, starting transfers between devices, body(): near = lax.ppermute(to_near, 'row', near_pairs)  1.58 us
    ppermute x1, waiting for transfers between devices, body(): far_strips = lax.ppermute(strips_far, 'row', far_pairs)  1 us
    ppermute x1, starting transfers between devices, body(): from_other = lax.ppermute(to_other, 'aisle', other)  1 us
    add x1, other arithmetic, body(): shift = 0.1 + 40.0 * solid.astype(jnp.float32)  0.88 us
  transfers between devices with their start and end apart: 6, of which 2 were waited for; matrix products, arithmetic and copies ran while one was open for 0% of the time, Pallas kernels for 5%

profile of v4, /device:TPU:8, one launch (start us, length us, event | category | flops | bytes accessed | tf_op | source)
XLA Modules:
  0.0 18.8 jit_solution(654591756580654505)
XLA Ops:
  0.0 0.0 copy-start
  0.0 0.0 copy-start.1
  0.0 0.9 %multiply_add_fusion = f32[8,16,128]{2,1,0:T(8,128)S(1)} fusion(s32[8,16,128]{2,1,0:T(8,128)} %param.5), kind=kLoop, calls=%fused_computation | loop fusion | flops 49152 | bytes 131072 | tf_op jit(solution)/shard_map/add | solution.py:440
  0.9 0.0 copy-done
  0.9 0.0 copy-done.1
  0.9 0.3 %pack_edges.1 = (f32[3,16,8,128]{3,2,1,0:T(8,128)S(1)}, f32[8,8,128]{2,1,0:T(8,128)S(1)}, f32[8,8,128]{2,1,0:T(8,128)S(1)}) custom-call(f32[128,128]{1,0:T(8,128)S(1)} %bitcast.5, f32[128,128]{1,0:T(8,128)S(1)} %bitcast.6, f32[128,128]{1,0:T(8,128)S(1)} %bitcast.4), custom_call_target="tpu_custom_call" | custom-call | tf_op jit(solution)/shard_map/pack_edges/pallas_call | solution.py:422
  1.2 1.0 %collective-permute-start = (f32[8,8,128]{2,1,0:T(8,128)S(1)}, f32[8,8,128]{2,1,0:T(8,128)S(1)}, u32[]{:S(2)}, u32[]{:S(2)}) collective-permute-start(f32[8,8,128]{2,1,0:T(8,128)S(1)} %get-tuple-element.22), channel_id=1, source_target_pairs={{0,24},{8,16},{16,8},{24,0},{1,25},{9,17},{17,9},{25,1},{2,26},{10... | collective-permute-start | bytes 98312 | tf_op jit(solution)/shard_map/ppermute | solution.py:450
  2.2 0.7 %collective-permute-start.1 = (f32[8,8,128]{2,1,0:T(8,128)S(1)}, f32[8,8,128]{2,1,0:T(8,128)S(1)}, u32[]{:S(2)}, u32[]{:S(2)}) collective-permute-start(f32[8,8,128]{2,1,0:T(8,128)S(1)} %get-tuple-element.23), channel_id=1, source_target_pairs={{0,8},{8,0},{16,24},{24,16},{1,9},{9,1},{17,25},{25,17},{2,10},{10... | collective-permute-start | bytes 98312 | tf_op jit(solution)/shard_map/ppermute | solution.py:451
  2.9 1.6 %collective-permute-start.2 = (f32[40,8,128]{2,1,0:T(8,128)S(1)}, f32[40,8,128]{2,1,0:T(8,128)S(1)}, u32[]{:S(2)}, u32[]{:S(2)}) collective-permute-start(f32[40,8,128]{2,1,0:T(8,128)S(1)} %get-tuple-element.33), channel_id=1, source_target_pairs={{0,1},{1,0},{2,3},{3,2},{4,5},{5,4},{6,7},{7,6},{8,9},{9,8},{10,11... | collective-permute-start | bytes 491528 | tf_op jit(solution)/shard_map/ppermute | solution.py:456
  4.5 2.3 %collective-permute-start.3 = (f32[40,8,128]{2,1,0:T(8,128)S(1)}, f32[40,8,128]{2,1,0:T(8,128)S(1)}, u32[]{:S(2)}, u32[]{:S(2)}) collective-permute-start(f32[40,8,128]{2,1,0:T(8,128)S(1)} %get-tuple-element.34), channel_id=1, source_target_pairs={{1,2},{3,4},{5,6},{2,1},{4,3},{6,5},{9,10},{11,12},{13,14},{10,9},... | collective-permute-start | bytes 491528 | tf_op jit(solution)/shard_map/ppermute | solution.py:457
  6.8 0.0 collective-permute-done.from_other
  6.8 0.0 collective-permute-done.1.from_pair
  6.8 0.2 pack_strips.1
  7.0 4.4 %collective-permute-start.4 = (f32[7,8,128]{2,1,0:T(8,128)S(1)}, f32[7,8,128]{2,1,0:T(8,128)S(1)}, u32[]{:S(2)}, u32[]{:S(2)}) collective-permute-start(f32[7,8,128]{2,1,0:T(8,128)S(1)} %get-tuple-element.35), channel_id=1, source_target_pairs={{1,2},{3,4},{5,6},{2,1},{4,3},{6,5},{9,10},{11,12},{13,14},{10,9},... | collective-permute-start | bytes 86024 | tf_op jit(solution)/shard_map/ppermute | solution.py:461
  11.4 0.6 %collective-permute-start.5 = (f32[7,8,128]{2,1,0:T(8,128)S(1)}, f32[7,8,128]{2,1,0:T(8,128)S(1)}, u32[]{:S(2)}, u32[]{:S(2)}) collective-permute-start(f32[7,8,128]{2,1,0:T(8,128)S(1)} %get-tuple-element.36), channel_id=1, source_target_pairs={{0,1},{1,0},{2,3},{3,2},{4,5},{5,4},{6,7},{7,6},{8,9},{9,8},{10,11... | collective-permute-start | bytes 86024 | tf_op jit(solution)/shard_map/ppermute | solution.py:462
  12.0 0.8 %prepare_own.1 = (f32[16,2,8,128]{3,2,1,0:T(8,128)S(1)}, f32[16,2,8,128]{3,2,1,0:T(8,128)S(1)}, f32[16,2,8,128]{3,2,1,0:T(8,128)S(1)}, f32[16,2,8,128]{3,2,1,0:T...) custom-call(f32[3,16,8,128]{3,2,1,0:T(8,128)S(1)} %get-tuple-element, ...), custom_call_target="tpu_custom_call" | custom-call | flops 99999997952 | bytes 1073741824 | tf_op jit(solution)/shard_map/prepare_own/pallas_call | solution.py:422
  12.8 1.0 %collective-permute-done.4.far_strips = f32[7,8,128]{2,1,0:T(8,128)S(1)} collective-permute-done((f32[7,8,128]{2,1,0:T(8,128)S(1)}, f32[7,8,128]{2,1,0:T(8,128)S(1)}, u32[]{:S(2)}, u32[]{:S(2)}) %collective-permute-start.4) | collective-permute-done | bytes 28704 | tf_op jit(solution)/shard_map/ppermute | solution.py:461
  13.8 1.6 %collective-permute-done.5.near_strips = f32[7,8,128]{2,1,0:T(8,128)S(1)} collective-permute-done((f32[7,8,128]{2,1,0:T(8,128)S(1)}, f32[7,8,128]{2,1,0:T(8,128)S(1)}, u32[]{:S(2)}, u32[]{:S(2)}) %collective-permute-start.5) | collective-permute-done | bytes 28704 | tf_op jit(solution)/shard_map/ppermute | solution.py:462
  15.4 0.0 collective-permute-done.2.near
  15.4 0.0 collective-permute-done.3.far
  15.4 3.4 %solve_all.1 = f32[128,128]{1,0:T(8,128)} custom-call(f32[16,2,8,128]{3,2,1,0:T(8,128)S(1)} %get-tuple-element.25.own_rhs, f32[16,2,8,128]{3,2,1,0:T(8,128)S(1)} %get-tuple-element.26.own_cond, f32[16,2,8,128]{3,2,1,0:T(8,128)S(1)} %get-tuple-element.27.own_x, f32[16,2,8,128]{3,2,1,0:T(8,128)S(1)} %get-tuple-element.28.own_z, ...), custom_call_target="tpu_custom_call" | custom-call | tf_op jit(solution)/shard_map/solve_all/pallas_call | solution.py:422
  (1 shorter events, 0.0 us)
Async XLA Ops:
  0.0 0.9 %copy-start = (f32[8,16,128]{2,1,0:T(8,128)S(1)}, f32[8,16,128]{2,1,0:T(8,128)}, u32[]{:S(2)}) copy-start(f32[8,16,128]{2,1,0:T(8,128)} %param.3) | copy-start | bytes 196612
  0.0 0.9 %copy-start.1 = (f32[8,16,128]{2,1,0:T(8,128)S(1)}, f32[8,16,128]{2,1,0:T(8,128)}, u32[]{:S(2)}) copy-start(f32[8,16,128]{2,1,0:T(8,128)} %param.4) | copy-start | bytes 196612
  1.2 5.6 %collective-permute-start = (f32[8,8,128]{2,1,0:T(8,128)S(1)}, f32[8,8,128]{2,1,0:T(8,128)S(1)}, u32[]{:S(2)}, u32[]{:S(2)}) collective-permute-start(f32[8,8,128]{2,1,0:T(8,128)S(1)} %get-tuple-element.22), channel_id=1, source_target_pairs={{0,24},{8,16},{16,8},{24,0},{1,25},{9,17},{17,9},{25,1},{2,26},{10... | collective-permute-start | bytes 98312 | tf_op jit(solution)/shard_map/ppermute | solution.py:450
  2.2 4.6 %collective-permute-start.1 = (f32[8,8,128]{2,1,0:T(8,128)S(1)}, f32[8,8,128]{2,1,0:T(8,128)S(1)}, u32[]{:S(2)}, u32[]{:S(2)}) collective-permute-start(f32[8,8,128]{2,1,0:T(8,128)S(1)} %get-tuple-element.23), channel_id=1, source_target_pairs={{0,8},{8,0},{16,24},{24,16},{1,9},{9,1},{17,25},{25,17},{2,10},{10... | collective-permute-start | bytes 98312 | tf_op jit(solution)/shard_map/ppermute | solution.py:451
  2.9 12.5 %collective-permute-start.2 = (f32[40,8,128]{2,1,0:T(8,128)S(1)}, f32[40,8,128]{2,1,0:T(8,128)S(1)}, u32[]{:S(2)}, u32[]{:S(2)}) collective-permute-start(f32[40,8,128]{2,1,0:T(8,128)S(1)} %get-tuple-element.33), channel_id=1, source_target_pairs={{0,1},{1,0},{2,3},{3,2},{4,5},{5,4},{6,7},{7,6},{8,9},{9,8},{10,11... | collective-permute-start | bytes 491528 | tf_op jit(solution)/shard_map/ppermute | solution.py:456
  4.5 10.9 %collective-permute-start.3 = (f32[40,8,128]{2,1,0:T(8,128)S(1)}, f32[40,8,128]{2,1,0:T(8,128)S(1)}, u32[]{:S(2)}, u32[]{:S(2)}) collective-permute-start(f32[40,8,128]{2,1,0:T(8,128)S(1)} %get-tuple-element.34), channel_id=1, source_target_pairs={{1,2},{3,4},{5,6},{2,1},{4,3},{6,5},{9,10},{11,12},{13,14},{10,9},... | collective-permute-start | bytes 491528 | tf_op jit(solution)/shard_map/ppermute | solution.py:457
  7.0 6.8 %collective-permute-start.4 = (f32[7,8,128]{2,1,0:T(8,128)S(1)}, f32[7,8,128]{2,1,0:T(8,128)S(1)}, u32[]{:S(2)}, u32[]{:S(2)}) collective-permute-start(f32[7,8,128]{2,1,0:T(8,128)S(1)} %get-tuple-element.35), channel_id=1, source_target_pairs={{1,2},{3,4},{5,6},{2,1},{4,3},{6,5},{9,10},{11,12},{13,14},{10,9},... | collective-permute-start | bytes 86024 | tf_op jit(solution)/shard_map/ppermute | solution.py:461
  11.4 3.9 %collective-permute-start.5 = (f32[7,8,128]{2,1,0:T(8,128)S(1)}, f32[7,8,128]{2,1,0:T(8,128)S(1)}, u32[]{:S(2)}, u32[]{:S(2)}) collective-permute-start(f32[7,8,128]{2,1,0:T(8,128)S(1)} %get-tuple-element.36), channel_id=1, source_target_pairs={{0,1},{1,0},{2,3},{3,2},{4,5},{5,4},{6,7},{7,6},{8,9},{9,8},{10,11... | collective-permute-start | bytes 86024 | tf_op jit(solution)/shard_map/ppermute | solution.py:462

commit v5 on v4

--- a/solution.py
+++ b/solution.py
@@ -168,22 +168,36 @@
     return near_part + deep_part
 
 
-def merge(block, strip, number):
-    lane = lax.broadcasted_iota(jnp.int32, block.shape, 2)
-    beside = any_of(lane, (RIGHT0, RIGHT0 + STRIP), (LEFT0, LEFT0 + STRIP))
+def picked(value, index):
+    rows = value.reshape(-1, CA)
+    return jnp.take_along_axis(rows, jnp.concatenate([index] * (rows.shape[0] // NZ)), axis=1).reshape(value.shape)
+
+
+def split(block, copies):
+    lane = lanes()
+    in_block = lane < HALF
+    index = lane
+    if copies:
+        in_block |= any_of(lane, (66, 67), (125, 126))
+        index = jnp.where(lane == 66, HALF - 1, jnp.where(lane == 125, 0, index))
     tiles = []
     for colour in range(2):
-        part = turn(block, HALF, 2) if colour else block
-        value = jnp.where(beside, turn(strip, RIGHT0 - 16 * number - 8 * colour, 2), 0.0)
-        tiles.append(jnp.where(lane < HALF, part, value))
+        part = block
+        if copies or colour:
+            part = picked(block, jnp.clip(index + HALF * colour, 0, CA - 1))
+        tiles.append(jnp.where(in_block, part, 0.0))
     return jnp.stack(tiles, axis=1)
 
 
-def fill(tiles):
-    lane = lax.broadcasted_iota(jnp.int32, tiles.shape, 3)
-    low = any_of(lane, (64, 65), (125, 126))
-    high = any_of(lane, (66, 67), (127, 128))
-    return jnp.where(low, turn(tiles, -TWIN, 3), jnp.where(high, turn(tiles, TWIN, 3), tiles))
+def expand(tiles, strip, number, copies):
+    lane = lanes()
+    in_strip = any_of(lane, (RIGHT0, RIGHT0 + STRIP), (LEFT0, LEFT0 + STRIP))
+    index = lane - RIGHT0
+    if copies:
+        in_strip |= any_of(lane, (64, 65), (127, 128))
+        index = jnp.where(lane == 64, 0, jnp.where(lane == 127, LEFT_AT + STRIP - 1, index))
+    beside = [picked(strip, jnp.clip(index + (16 * number + 8 * colour), 0, CA - 1)) for colour in range(2)]
+    return jnp.where(in_strip, jnp.stack(beside, axis=1), tiles)
 
 
 def spread(here, shift):
@@ -226,12 +240,9 @@
     halves = [pl.ds(first, 8) for first in range(0, CR, 8)]
     for at in halves:
         strip = strips[at]
-        cond[at] = merge(main[1, at], strip, 1)
-        part[at] = merge(main[2, at], strip, 2)
-        rhs[at] = merge(main[0, at], strip, 0)
-    for at in halves:
-        cond[at] = fill(cond[at])
-        part[at] = fill(part[at])
+        cond[at] = expand(split(main[1, at], True), strip, 1, True)
+        part[at] = expand(split(main[2, at], True), strip, 2, True)
+        rhs[at] = expand(split(main[0, at], False), strip, 0, False)
     for at in halves:
         face_x[at], face_z[at], part[at] = spread(cond[at], part[at])
     face_r[pl.ds(0, 1)] = jnp.zeros((1, 2, NZ, CA), jnp.float32)
@@ -249,6 +260,11 @@
             levels[done + 1, at] = inverse[at] * (power * rhs[at] + around(weights, first, count, here, below, above))
 
 
+def split_near(near, tiles):
+    tiles[:DG] = split(near[:DG], False)
+    tiles[DG:] = split(near[DG:], True)
+
+
 def solve_all(own_rhs, own_cond, own_x, own_z, own_r, own_part, own_inverse, levels, near, far, far_strips, near_strips, out,
               cond, face_x, face_z, face_r, part, inverse, rhs, est_a, est_b, total):
     row_at = lax.axis_index("row")
@@ -274,23 +290,17 @@
 
     sides = [(far, unpack_strips(far_strips, lane)[::-1], True), (near, unpack_strips(near_strips, lane), False)]
     for block, strip, is_far in sides:
+        part_of = (lambda at, copies: split(block[at], copies)) if is_far else (lambda at, copies: block[at])
         for low, high in ((0, 7), (7, DK)):
             at = pl.ds((0 if is_far else DK + CR) + low, high - low)
-            cond[at] = merge(block[pl.ds(DG + low, high - low)], jnp.stack(strip[low:high]), 1)
+            cond[at] = expand(part_of(pl.ds(DG + low, high - low), True), jnp.stack(strip[low:high]), 1, True)
         strip = strip[1:] if is_far else strip[:DG]
         for low, high in ((0, 7), (7, DG)):
             beside = jnp.stack(strip[low:high])
             at = pl.ds((1 if is_far else DK + CR) + low, high - low)
-            part[at] = merge(block[pl.ds(DG + DK + low, high - low)], beside, 2)
+            part[at] = expand(part_of(pl.ds(DG + DK + low, high - low), True), beside, 2, True)
             at = pl.ds((0 if is_far else NEAR_BOX[2] + OV) + low, high - low)
-            rhs[at] = merge(block[pl.ds(low, high - low)], beside, 0)
-    for first in (0, DK + CR):
-        for low, high in ((0, 7), (7, DK)):
-            at = pl.ds(first + low, high - low)
-            cond[at] = fill(cond[at])
-        for low, high in ((0, 7), (7, DG)):
-            at = pl.ds((first or 1) + low, high - low)
-            part[at] = fill(part[at])
+            rhs[at] = expand(part_of(pl.ds(low, high - low), False), beside, 0, False)
     for first in (1, DK + CR):
         for low, high in ((0, 7), (7, DG)):
             at = pl.ds(first + low, high - low)
@@ -360,12 +370,13 @@
     solve(first_spans, from_own)
     est = est_a if SWEEPS % 2 == 0 else est_b
 
-    to_low = any_of(both, (63, 65), (124, 126))
-    to_high = any_of(both, (66, 68), (127, 128), (0, 1))
+    to_low = any_of(lane, (63, 65), (124, 126))
+    to_high = any_of(lane, (66, 68), (127, 128), (0, 1))
+    twins = lax.rem(lane + jnp.where(to_low, TWIN, jnp.where(to_high, CA - TWIN, 0)), CA)
+    twice = to_low | to_high
 
     def joined(value):
-        other = jnp.where(to_low, turn(value, -TWIN, 3), jnp.where(to_high, turn(value, TWIN, 3), 0.0))
-        return value + other
+        return value + jnp.where(twice, picked(value, twins), 0.0)
 
     def summed_boxes(p, count):
         value = None
@@ -406,12 +417,12 @@
 
     solve(second_spans, lambda done, est: None)
 
-    order = lax.div(lane, 2) + HALF * lax.rem(lane, 2)
+    order = lax.div(lane, 2)
+    is_even = lax.rem(lane, 2) == 0
     for low, high in ((0, OV), (OV, 8), (8, CR - OV), (CR - OV, CR)):
         value = joined(summed_boxes(low, high - low)) + total[pl.ds(low + REACH, high - low)]
-        value = jnp.where(lane < HALF, value[:, 0], turn(value[:, 1], HALF, 2))
+        value = jnp.where(is_even, picked(value[:, 0], order), picked(value[:, 1], order))
         value = value.reshape((high - low) * NZ, CA)
-        value = jnp.take_along_axis(value, jnp.concatenate([order] * (high - low)), axis=1)
         for n in range(high - low):
             row = low + n
             out[pl.ds(odd * (CR - 1 - 2 * row) + row, NZ, stride=CR), :] = value[n * NZ : (n + 1) * NZ]
@@ -436,7 +447,7 @@
     rows = lax.axis_size("row")
     flat = (NZ * CR, CA)
     tile = lambda *lead: jax.ShapeDtypeStruct(lead + (NZ, CA), jnp.float32)
-    busy = pl.CostEstimate(flops=10**11, bytes_accessed=1024 * MIB, transcendentals=0)
+    busy = pl.CostEstimate(flops=10**11, bytes_accessed=0, transcendentals=0)
     shift = 0.1 + 40.0 * solid.astype(jnp.float32)
     main, to_other, to_pair = call(
         pack_edges, (tile(3, CR), tile(CR // 2), tile(CR // 2)),
@@ -467,7 +478,7 @@
     result = call(
         solve_all,
         jax.ShapeDtypeStruct(flat, jnp.float32),
-        *own, near, far, far_strips, near_strips,
+        *own, call(split_near, tile(TILES, 2), near, cost=None), far, far_strips, near_strips,
         scratch=[
             pair_rows(around), pair_rows(around), pair_rows(around), pair_rows(around), pair_rows(around),
             pair_rows(ROWS), pair_rows(ROWS), pair_rows(GUARDED), pair_rows(GUARDED), pair_rows(CR + 2 * REACH),

time: 18.9 us -> 18.7 us (0.989)
    pallas_call x5 -> x6, Pallas kernels: 4.62 us -> 4.51 us  [call(): pl.pallas_call(kernel, out_shape=outs, in_specs=[vmem] * len(args), out_s...]
  transfers between devices with their start and end apart: 6 -> 6, of which waited for: 2 -> 2; matrix products, arithmetic and copies ran while one was open for 0% -> 0% of each run, Pallas kernels for 5% -> 6%
where the time goes in v5:
time: 18.7 us; the launch traced here: 18.5 us
  starting transfers between devices  10.6 us (57%)
  Pallas kernels  4.51 us (24%)
  waiting for transfers between devices  2.44 us (13%)
  other arithmetic  0.88 us (5%)
    pallas_call x6, Pallas kernels, call(): pl.pallas_call(kernel, out_shape=outs, in_specs=[vmem] * len(args), out_s...  4.51 us
    ppermute x1, starting transfers between devices, body(): far_strips = lax.ppermute(strips_far, 'row', far_pairs)  4.44 us
    ppermute x1, starting transfers between devices, body(): far = lax.ppermute(to_far, 'row', far_pairs)  2.29 us
    ppermute x1, waiting for transfers between devices, body(): near_strips = lax.ppermute(strips_near, 'row', near_pairs)  1.6 us
    ppermute x1, starting transfers between devices, body(): near = lax.ppermute(to_near, 'row', near_pairs)  1.58 us
    ppermute x1, starting transfers between devices, body(): from_other = lax.ppermute(to_other, 'aisle', other)  1 us
    add x1, other arithmetic, body(): shift = 0.1 + 40.0 * solid.astype(jnp.float32)  0.88 us
    ppermute x1, waiting for transfers between devices, body(): far_strips = lax.ppermute(strips_far, 'row', far_pairs)  0.82 us
  transfers between devices with their start and end apart: 6, of which 2 were waited for; matrix products, arithmetic and copies ran while one was open for 0% of the time, Pallas kernels for 6%

profile of v5, /device:TPU:8, one launch (start us, length us, event | category | flops | bytes accessed | tf_op | source)
XLA Modules:
  0.0 18.5 jit_solution(13977015266718200498)
XLA Ops:
  0.0 0.0 copy-start
  0.0 0.0 copy-start.1
  0.0 0.9 %multiply_add_fusion = f32[8,16,128]{2,1,0:T(8,128)S(1)} fusion(s32[8,16,128]{2,1,0:T(8,128)} %param.5), kind=kLoop, calls=%fused_computation | loop fusion | flops 49152 | bytes 131072 | tf_op jit(solution)/shard_map/add | solution.py:451
  0.9 0.0 copy-done
  0.9 0.0 copy-done.1
  0.9 0.3 %pack_edges.1 = (f32[3,16,8,128]{3,2,1,0:T(8,128)S(1)}, f32[8,8,128]{2,1,0:T(8,128)S(1)}, f32[8,8,128]{2,1,0:T(8,128)S(1)}) custom-call(f32[128,128]{1,0:T(8,128)S(1)} %bitcast.5, f32[128,128]{1,0:T(8,128)S(1)} %bitcast.6, f32[128,128]{1,0:T(8,128)S(1)} %bitcast.4), custom_call_target="tpu_custom_call" | custom-call | tf_op jit(solution)/shard_map/pack_edges/pallas_call | solution.py:433
  1.2 1.0 %collective-permute-start = (f32[8,8,128]{2,1,0:T(8,128)S(1)}, f32[8,8,128]{2,1,0:T(8,128)S(1)}, u32[]{:S(2)}, u32[]{:S(2)}) collective-permute-start(f32[8,8,128]{2,1,0:T(8,128)S(1)} %get-tuple-element.22), channel_id=1, source_target_pairs={{0,24},{8,16},{16,8},{24,0},{1,25},{9,17},{17,9},{25,1},{2,26},{10... | collective-permute-start | bytes 98312 | tf_op jit(solution)/shard_map/ppermute | solution.py:461
  2.2 0.7 %collective-permute-start.1 = (f32[8,8,128]{2,1,0:T(8,128)S(1)}, f32[8,8,128]{2,1,0:T(8,128)S(1)}, u32[]{:S(2)}, u32[]{:S(2)}) collective-permute-start(f32[8,8,128]{2,1,0:T(8,128)S(1)} %get-tuple-element.23), channel_id=1, source_target_pairs={{0,8},{8,0},{16,24},{24,16},{1,9},{9,1},{17,25},{25,17},{2,10},{10... | collective-permute-start | bytes 98312 | tf_op jit(solution)/shard_map/ppermute | solution.py:462
  2.9 1.6 %collective-permute-start.2 = (f32[40,8,128]{2,1,0:T(8,128)S(1)}, f32[40,8,128]{2,1,0:T(8,128)S(1)}, u32[]{:S(2)}, u32[]{:S(2)}) collective-permute-start(f32[40,8,128]{2,1,0:T(8,128)S(1)} %get-tuple-element.33), channel_id=1, source_target_pairs={{0,1},{1,0},{2,3},{3,2},{4,5},{5,4},{6,7},{7,6},{8,9},{9,8},{10,11... | collective-permute-start | bytes 491528 | tf_op jit(solution)/shard_map/ppermute | solution.py:467
  4.5 2.3 %collective-permute-start.3 = (f32[40,8,128]{2,1,0:T(8,128)S(1)}, f32[40,8,128]{2,1,0:T(8,128)S(1)}, u32[]{:S(2)}, u32[]{:S(2)}) collective-permute-start(f32[40,8,128]{2,1,0:T(8,128)S(1)} %get-tuple-element.34), channel_id=1, source_target_pairs={{1,2},{3,4},{5,6},{2,1},{4,3},{6,5},{9,10},{11,12},{13,14},{10,9},... | collective-permute-start | bytes 491528 | tf_op jit(solution)/shard_map/ppermute | solution.py:468
  6.8 0.0 collective-permute-done.from_other
  6.8 0.0 collective-permute-done.1.from_pair
  6.8 0.2 pack_strips.1
  7.0 4.4 %collective-permute-start.4 = (f32[7,8,128]{2,1,0:T(8,128)S(1)}, f32[7,8,128]{2,1,0:T(8,128)S(1)}, u32[]{:S(2)}, u32[]{:S(2)}) collective-permute-start(f32[7,8,128]{2,1,0:T(8,128)S(1)} %get-tuple-element.35), channel_id=1, source_target_pairs={{1,2},{3,4},{5,6},{2,1},{4,3},{6,5},{9,10},{11,12},{13,14},{10,9},... | collective-permute-start | bytes 86024 | tf_op jit(solution)/shard_map/ppermute | solution.py:472
  11.4 0.6 %collective-permute-start.5 = (f32[7,8,128]{2,1,0:T(8,128)S(1)}, f32[7,8,128]{2,1,0:T(8,128)S(1)}, u32[]{:S(2)}, u32[]{:S(2)}) collective-permute-start(f32[7,8,128]{2,1,0:T(8,128)S(1)} %get-tuple-element.36), channel_id=1, source_target_pairs={{0,1},{1,0},{2,3},{3,2},{4,5},{5,4},{6,7},{7,6},{8,9},{9,8},{10,11... | collective-permute-start | bytes 86024 | tf_op jit(solution)/shard_map/ppermute | solution.py:473
  12.0 0.8 %prepare_own.1 = (f32[16,2,8,128]{3,2,1,0:T(8,128)S(1)}, f32[16,2,8,128]{3,2,1,0:T(8,128)S(1)}, f32[16,2,8,128]{3,2,1,0:T(8,128)S(1)}, f32[16,2,8,128]{3,2,1,0:T...) custom-call(f32[3,16,8,128]{3,2,1,0:T(8,128)S(1)} %get-tuple-element, ...), custom_call_target="tpu_custom_call" | custom-call | flops 99999997952 | tf_op jit(solution)/shard_map/prepare_own/pallas_call | solution.py:433
  12.8 0.0 collective-permute-done.2.near
  12.8 0.1 split_near.1.near
  12.9 0.8 %collective-permute-done.4.far_strips = f32[7,8,128]{2,1,0:T(8,128)S(1)} collective-permute-done((f32[7,8,128]{2,1,0:T(8,128)S(1)}, f32[7,8,128]{2,1,0:T(8,128)S(1)}, u32[]{:S(2)}, u32[]{:S(2)}) %collective-permute-start.4) | collective-permute-done | bytes 28704 | tf_op jit(solution)/shard_map/ppermute | solution.py:472
  13.8 1.6 %collective-permute-done.5.near_strips = f32[7,8,128]{2,1,0:T(8,128)S(1)} collective-permute-done((f32[7,8,128]{2,1,0:T(8,128)S(1)}, f32[7,8,128]{2,1,0:T(8,128)S(1)}, u32[]{:S(2)}, u32[]{:S(2)}) %collective-permute-start.5) | collective-permute-done | bytes 28704 | tf_op jit(solution)/shard_map/ppermute | solution.py:473
  15.4 0.0 collective-permute-done.3.far
  15.4 3.1 %solve_all.1 = f32[128,128]{1,0:T(8,128)} custom-call(f32[16,2,8,128]{3,2,1,0:T(8,128)S(1)} %get-tuple-element.25.own_rhs, f32[16,2,8,128]{3,2,1,0:T(8,128)S(1)} %get-tuple-element.26.own_cond, f32[16,2,8,128]{3,2,1,0:T(8,128)S(1)} %get-tuple-element.27.own_x, f32[16,2,8,128]{3,2,1,0:T(8,128)S(1)} %get-tuple-element.28.own_z, ...), custom_call_target="tpu_custom_call" | custom-call | tf_op jit(solution)/shard_map/solve_all/pallas_call | solution.py:433
  (1 shorter events, 0.0 us)
Async XLA Ops:
  0.0 0.9 %copy-start = (f32[8,16,128]{2,1,0:T(8,128)S(1)}, f32[8,16,128]{2,1,0:T(8,128)}, u32[]{:S(2)}) copy-start(f32[8,16,128]{2,1,0:T(8,128)} %param.3) | copy-start | bytes 196612
  0.0 0.9 %copy-start.1 = (f32[8,16,128]{2,1,0:T(8,128)S(1)}, f32[8,16,128]{2,1,0:T(8,128)}, u32[]{:S(2)}) copy-start(f32[8,16,128]{2,1,0:T(8,128)} %param.4) | copy-start | bytes 196612
  1.2 5.6 %collective-permute-start = (f32[8,8,128]{2,1,0:T(8,128)S(1)}, f32[8,8,128]{2,1,0:T(8,128)S(1)}, u32[]{:S(2)}, u32[]{:S(2)}) collective-permute-start(f32[8,8,128]{2,1,0:T(8,128)S(1)} %get-tuple-element.22), channel_id=1, source_target_pairs={{0,24},{8,16},{16,8},{24,0},{1,25},{9,17},{17,9},{25,1},{2,26},{10... | collective-permute-start | bytes 98312 | tf_op jit(solution)/shard_map/ppermute | solution.py:461
  2.2 4.6 %collective-permute-start.1 = (f32[8,8,128]{2,1,0:T(8,128)S(1)}, f32[8,8,128]{2,1,0:T(8,128)S(1)}, u32[]{:S(2)}, u32[]{:S(2)}) collective-permute-start(f32[8,8,128]{2,1,0:T(8,128)S(1)} %get-tuple-element.23), channel_id=1, source_target_pairs={{0,8},{8,0},{16,24},{24,16},{1,9},{9,1},{17,25},{25,17},{2,10},{10... | collective-permute-start | bytes 98312 | tf_op jit(solution)/shard_map/ppermute | solution.py:462
  2.9 9.9 %collective-permute-start.2 = (f32[40,8,128]{2,1,0:T(8,128)S(1)}, f32[40,8,128]{2,1,0:T(8,128)S(1)}, u32[]{:S(2)}, u32[]{:S(2)}) collective-permute-start(f32[40,8,128]{2,1,0:T(8,128)S(1)} %get-tuple-element.33), channel_id=1, source_target_pairs={{0,1},{1,0},{2,3},{3,2},{4,5},{5,4},{6,7},{7,6},{8,9},{9,8},{10,11... | collective-permute-start | bytes 491528 | tf_op jit(solution)/shard_map/ppermute | solution.py:467
  4.5 10.9 %collective-permute-start.3 = (f32[40,8,128]{2,1,0:T(8,128)S(1)}, f32[40,8,128]{2,1,0:T(8,128)S(1)}, u32[]{:S(2)}, u32[]{:S(2)}) collective-permute-start(f32[40,8,128]{2,1,0:T(8,128)S(1)} %get-tuple-element.34), channel_id=1, source_target_pairs={{1,2},{3,4},{5,6},{2,1},{4,3},{6,5},{9,10},{11,12},{13,14},{10,9},... | collective-permute-start | bytes 491528 | tf_op jit(solution)/shard_map/ppermute | solution.py:468
  7.0 6.8 %collective-permute-start.4 = (f32[7,8,128]{2,1,0:T(8,128)S(1)}, f32[7,8,128]{2,1,0:T(8,128)S(1)}, u32[]{:S(2)}, u32[]{:S(2)}) collective-permute-start(f32[7,8,128]{2,1,0:T(8,128)S(1)} %get-tuple-element.35), channel_id=1, source_target_pairs={{1,2},{3,4},{5,6},{2,1},{4,3},{6,5},{9,10},{11,12},{13,14},{10,9},... | collective-permute-start | bytes 86024 | tf_op jit(solution)/shard_map/ppermute | solution.py:472
  11.4 3.9 %collective-permute-start.5 = (f32[7,8,128]{2,1,0:T(8,128)S(1)}, f32[7,8,128]{2,1,0:T(8,128)S(1)}, u32[]{:S(2)}, u32[]{:S(2)}) collective-permute-start(f32[7,8,128]{2,1,0:T(8,128)S(1)} %get-tuple-element.36), channel_id=1, source_target_pairs={{0,1},{1,0},{2,3},{3,2},{4,5},{5,4},{6,7},{7,6},{8,9},{9,8},{10,11... | collective-permute-start | bytes 86024 | tf_op jit(solution)/shard_map/ppermute | solution.py:473

commit v6 on v5

--- a/solution.py
+++ b/solution.py
@@ -129,29 +129,31 @@
     return lax.rem(lane, 8), lax.rem(lane + 6, 8)
 
 
-def pack_strips(from_other, from_pair, strips, to_far, to_near):
+def right_and_left(from_other, from_pair):
+    uneven = odd_aisle()
+    return jnp.where(uneven, from_other[...], from_pair[...]), jnp.where(uneven, from_pair[...], from_other[...])
+
+
+def side_by_side(from_right, from_left):
+    in_right = lanes() < SPAN
+    first = jnp.where(in_right, from_right, from_left)
+    return jnp.concatenate([first, jnp.where(in_right, turn(from_right, -SPAN, 2), turn(from_left, LEFT_AT, 2))])
+
+
+def pack_strips(from_other, from_pair, strips, to_far):
     lane = lanes()
     in_right = lane < SPAN
     slot_right, slot_left = slots(lane)
-    uneven = odd_aisle()
-    from_right = jnp.where(uneven, from_other[...], from_pair[...])
-    from_left = jnp.where(uneven, from_pair[...], from_other[...])
-    half = CR // 2
-    rows = []
-    for row in range(half):
-        rows.append(jnp.where(in_right, from_right[row], from_left[row]))
-    for row in range(half):
-        rows.append(jnp.where(in_right, turn(from_right[row], -SPAN), turn(from_left[row], LEFT_AT)))
-    strips[...] = jnp.stack(rows)
+    rows = side_by_side(*right_and_left(from_other, from_pair))
+    strips[...] = rows
     around_left = any_of(lane, (LEFT_AT - 1, LEFT_AT + SPAN))
-    for out, place in ((to_far, lambda q: q), (to_near, lambda q: CR - 1 - q)):
-        for layer in range(DK // 2):
-            first, second = needed(layer), needed(DK - 1 - layer)
-            deep = rows[place(DK - 1 - layer)]
-            takes_right = in_right & (slot_right >= 8 - second)
-            takes_left = around_left & (slot_left >= 8 - first - second) & (slot_left < 8 - first)
-            value = jnp.where(takes_left, turn(deep, -first), rows[place(layer)])
-            out[layer] = jnp.where(takes_right, turn(deep, 8 - second), value)
+    for layer in range(DK // 2):
+        first, second = needed(layer), needed(DK - 1 - layer)
+        deep = rows[DK - 1 - layer]
+        takes_right = in_right & (slot_right >= 8 - second)
+        takes_left = around_left & (slot_left >= 8 - first - second) & (slot_left < 8 - first)
+        value = jnp.where(takes_left, turn(deep, -first), rows[layer])
+        to_far[layer] = jnp.where(takes_right, turn(deep, 8 - second), value)
 
 
 def unpack_strips(pairs, lane):
@@ -236,7 +238,9 @@
     return summed + jnp.stack([sum_even, sum_odd], axis=1)
 
 
-def prepare_own(main, strips, rhs, cond, face_x, face_z, face_r, part, inverse, levels):
+def prepare_own(main, strips, near, tiles, rhs, cond, face_x, face_z, face_r, part, inverse, levels):
+    tiles[:DG] = split(near[:DG], False)
+    tiles[DG:] = split(near[DG:], True)
     halves = [pl.ds(first, 8) for first in range(0, CR, 8)]
     for at in halves:
         strip = strips[at]
@@ -260,12 +264,31 @@
             levels[done + 1, at] = inverse[at] * (power * rhs[at] + around(weights, first, count, here, below, above))
 
 
-def split_near(near, tiles):
-    tiles[:DG] = split(near[:DG], False)
-    tiles[DG:] = split(near[DG:], True)
-
-
-def solve_all(own_rhs, own_cond, own_x, own_z, own_r, own_part, own_inverse, levels, near, far, far_strips, near_strips, out,
+def pack_near_edges(near, to_other, to_pair):
+    half = DK // 2
+    lane = lanes()
+
+    def edge(slot, first):
+        index = first + lax.rem(slot, 8) + HALF * lax.rem(lax.div(slot, 8), 2)
+        return jnp.clip(index, 0, CA - 1)
+
+    left_order = edge(lane, 0)
+    right_order = jnp.where(lane < SPAN, edge(lane, HALF - STRIP), edge(lane + (16 * 4 - LEFT_AT), HALF - STRIP))
+    left = right = jnp.zeros((half, NZ, CA), jnp.float32)
+    for number, start in enumerate((0, DG, DG + DK)):
+        for part in range(2):
+            last = DK if number == 1 else DG
+            rows = jnp.stack([near[start + min(part * half + n, last - 1)] for n in range(half)])
+            base = part * SPAN + 16 * number
+            left = jnp.where(any_of(lane, (base, base + 16)), picked(rows, left_order), left)
+            base = (1 - part) * LEFT_AT + 16 * number
+            right = jnp.where(any_of(lane, (base, base + 16)), picked(rows, right_order), right)
+    uneven = odd_aisle()
+    to_pair[...] = jnp.where(uneven, left, right)
+    to_other[...] = jnp.where(uneven, right, left)
+
+
+def solve_all(own_rhs, own_cond, own_x, own_z, own_r, own_part, own_inverse, levels, near, far, far_strips, near_other, near_pair, out,
               cond, face_x, face_z, face_r, part, inverse, rhs, est_a, est_b, total):
     row_at = lax.axis_index("row")
     odd = lax.rem(row_at, 2)
@@ -288,7 +311,7 @@
         for row in (0, SIDE + 1, SIDE + OWN + 2, GUARDED - 1):
             est[pl.ds(row, 1)] = zeros
 
-    sides = [(far, unpack_strips(far_strips, lane)[::-1], True), (near, unpack_strips(near_strips, lane), False)]
+    sides = [(far, unpack_strips(far_strips, lane)[::-1], True), (near, side_by_side(*right_and_left(near_other, near_pair)), False)]
     for block, strip, is_far in sides:
         part_of = (lambda at, copies: split(block[at], copies)) if is_far else (lambda at, copies: block[at])
         for low, high in ((0, 7), (7, DK)):
@@ -466,19 +489,21 @@
     )
     near = lax.ppermute(to_near, "row", near_pairs)
     far = lax.ppermute(to_far, "row", far_pairs)
-    strips, strips_far, strips_near = call(
-        pack_strips, (tile(CR), tile(DK // 2), tile(DK // 2)), from_other, from_pair
+    strips, strips_far = call(pack_strips, (tile(CR), tile(DK // 2)), from_other, from_pair)
+    far_strips = lax.ppermute(strips_far, "row", far_pairs)
+    near_to_other, near_to_pair = call(pack_near_edges, (tile(DK // 2), tile(DK // 2)), near, cost=None)
+    near_other = lax.ppermute(near_to_other, "aisle", other)
+    near_pair = lax.ppermute(near_to_pair, "aisle", pair)
+    own_rows = (tile(CR, 2),) * 7 + (tile(SWEEPS + 1, CR, 2),)
+    near_tiles, *own = call(
+        prepare_own, (tile(TILES, 2),) + own_rows, main, strips, near, limit=8, cost=pl.CostEstimate(flops=2000*10**6, bytes_accessed=0, transcendentals=0)
     )
-    far_strips = lax.ppermute(strips_far, "row", far_pairs)
-    near_strips = lax.ppermute(strips_near, "row", near_pairs)
-    own_rows = (tile(CR, 2),) * 7 + (tile(SWEEPS + 1, CR, 2),)
-    own = call(prepare_own, own_rows, main, strips, limit=8, cost=busy)
     pair_rows = lambda count: pltpu.VMEM((count, 2, NZ, CA), jnp.float32)
     around = CR + 2 * DK
     result = call(
         solve_all,
         jax.ShapeDtypeStruct(flat, jnp.float32),
-        *own, call(split_near, tile(TILES, 2), near, cost=None), far, far_strips, near_strips,
+        *own, near_tiles, far, far_strips, near_other, near_pair,
         scratch=[
             pair_rows(around), pair_rows(around), pair_rows(around), pair_rows(around), pair_rows(around),
             pair_rows(ROWS), pair_rows(ROWS), pair_rows(GUARDED), pair_rows(GUARDED), pair_rows(CR + 2 * REACH),

time: 18.7 us -> 18.2 us (0.973)
  waiting for transfers between devices: 2.44 us -> 1.82 us
    ppermute x1 -> x2, waiting for transfers between devices: 1.6 us -> 1.01 us  [the longest x1 1.01 us: body(): near_other = lax.ppermute(near_to_other, 'aisle', other)]
    ppermute x1, starting transfers between devices: 1 us -> 0.65 us  [body(): from_other = lax.ppermute(to_other, 'aisle', other)]
    ppermute x1, starting transfers between devices: 0.68 us -> 0.96 us  [body(): from_pair = lax.ppermute(to_pair, 'aisle', pair)]
    ppermute x1 -> x2, starting transfers between devices: 0.57 us -> 0.71 us  [the longest x1 0.64 us: body(): near_pair = lax.ppermute(near_to_pair, 'aisle', pair)]
  transfers between devices with their start and end apart: 6 -> 7, of which waited for: 2 -> 2; matrix products, arithmetic and copies ran while one was open for 0% -> 0% of each run, Pallas kernels for 6% -> 7%
where the time goes in v6:
time: 18.2 us; the launch traced here: 18.1 us
  starting transfers between devices  10.6 us (58%)
  Pallas kernels  4.62 us (25%)
  waiting for transfers between devices  1.82 us (10%)
  other arithmetic  0.88 us (5%)
    pallas_call x6, Pallas kernels, call(): pl.pallas_call(kernel, out_shape=outs, in_specs=[vmem] * len(args), out_s...  4.62 us
    ppermute x1, starting transfers between devices, body(): far_strips = lax.ppermute(strips_far, 'row', far_pairs)  4.44 us
    ppermute x1, starting transfers between devices, body(): far = lax.ppermute(to_far, 'row', far_pairs)  2.29 us
    ppermute x1, starting transfers between devices, body(): near = lax.ppermute(to_near, 'row', near_pairs)  1.58 us
    ppermute x1, waiting for transfers between devices, body(): near_other = lax.ppermute(near_to_other, 'aisle', other)  1.01 us
    ppermute x1, starting transfers between devices, body(): from_pair = lax.ppermute(to_pair, 'aisle', pair)  0.96 us
    add x1, other arithmetic, body(): shift = 0.1 + 40.0 * solid.astype(jnp.float32)  0.88 us
    ppermute x1, waiting for transfers between devices, body(): far_strips = lax.ppermute(strips_far, 'row', far_pairs)  0.8 us
  transfers between devices with their start and end apart: 7, of which 2 were waited for; matrix products, arithmetic and copies ran while one was open for 0% of the time, Pallas kernels for 7%

profile of v6, /device:TPU:8, one launch (start us, length us, event | category | flops | bytes accessed | tf_op | source)
XLA Modules:
  0.0 18.1 jit_solution(7693333836933914967)
XLA Ops:
  0.0 0.0 copy-start
  0.0 0.0 copy-start.1
  0.0 0.9 %multiply_add_fusion = f32[8,16,128]{2,1,0:T(8,128)S(1)} fusion(s32[8,16,128]{2,1,0:T(8,128)} %param.5), kind=kLoop, calls=%fused_computation | loop fusion | flops 49152 | bytes 131072 | tf_op jit(solution)/shard_map/add | solution.py:474
  0.9 0.0 copy-done
  0.9 0.0 copy-done.1
  0.9 0.3 %pack_edges.1 = (f32[3,16,8,128]{3,2,1,0:T(8,128)S(1)}, f32[8,8,128]{2,1,0:T(8,128)S(1)}, f32[8,8,128]{2,1,0:T(8,128)S(1)}) custom-call(f32[128,128]{1,0:T(8,128)S(1)} %bitcast.5, f32[128,128]{1,0:T(8,128)S(1)} %bitcast.6, f32[128,128]{1,0:T(8,128)S(1)} %bitcast.4), custom_call_target="tpu_custom_call" | custom-call | tf_op jit(solution)/shard_map/pack_edges/pallas_call | solution.py:456
  1.2 1.6 %collective-permute-start.2 = (f32[40,8,128]{2,1,0:T(8,128)S(1)}, f32[40,8,128]{2,1,0:T(8,128)S(1)}, u32[]{:S(2)}, u32[]{:S(2)}) collective-permute-start(f32[40,8,128]{2,1,0:T(8,128)S(1)} %get-tuple-element.27), channel_id=1, source_target_pairs={{0,1},{1,0},{2,3},{3,2},{4,5},{5,4},{6,7},{7,6},{8,9},{9,8},{10,11... | collective-permute-start | bytes 491528 | tf_op jit(solution)/shard_map/ppermute | solution.py:490
  2.8 0.7 %collective-permute-start = (f32[8,8,128]{2,1,0:T(8,128)S(1)}, f32[8,8,128]{2,1,0:T(8,128)S(1)}, u32[]{:S(2)}, u32[]{:S(2)}) collective-permute-start(f32[8,8,128]{2,1,0:T(8,128)S(1)} %get-tuple-element.24), channel_id=1, source_target_pairs={{0,24},{8,16},{16,8},{24,0},{1,25},{9,17},{17,9},{25,1},{2,26},{10... | collective-permute-start | bytes 98312 | tf_op jit(solution)/shard_map/ppermute | solution.py:484
  3.5 1.0 %collective-permute-start.1 = (f32[8,8,128]{2,1,0:T(8,128)S(1)}, f32[8,8,128]{2,1,0:T(8,128)S(1)}, u32[]{:S(2)}, u32[]{:S(2)}) collective-permute-start(f32[8,8,128]{2,1,0:T(8,128)S(1)} %get-tuple-element.25), channel_id=1, source_target_pairs={{0,8},{8,0},{16,24},{24,16},{1,9},{9,1},{17,25},{25,17},{2,10},{10... | collective-permute-start | bytes 98312 | tf_op jit(solution)/shard_map/ppermute | solution.py:485
  4.4 2.3 %collective-permute-start.3 = (f32[40,8,128]{2,1,0:T(8,128)S(1)}, f32[40,8,128]{2,1,0:T(8,128)S(1)}, u32[]{:S(2)}, u32[]{:S(2)}) collective-permute-start(f32[40,8,128]{2,1,0:T(8,128)S(1)} %get-tuple-element.37), channel_id=1, source_target_pairs={{1,2},{3,4},{5,6},{2,1},{4,3},{6,5},{9,10},{11,12},{13,14},{10,9},... | collective-permute-start | bytes 491528 | tf_op jit(solution)/shard_map/ppermute | solution.py:491
  6.7 0.0 collective-permute-done.from_other
  6.7 0.0 collective-permute-done.1.from_pair
  6.7 0.2 pack_strips.1
  6.9 4.4 %collective-permute-start.4 = (f32[7,8,128]{2,1,0:T(8,128)S(1)}, f32[7,8,128]{2,1,0:T(8,128)S(1)}, u32[]{:S(2)}, u32[]{:S(2)}) collective-permute-start(f32[7,8,128]{2,1,0:T(8,128)S(1)} %get-tuple-element.38), channel_id=1, source_target_pairs={{1,2},{3,4},{5,6},{2,1},{4,3},{6,5},{9,10},{11,12},{13,14},{10,9},... | collective-permute-start | bytes 86024 | tf_op jit(solution)/shard_map/ppermute | solution.py:493
  11.4 0.0 collective-permute-done.2.near
  11.4 0.2 %pack_near_edges.1 = (f32[7,8,128]{2,1,0:T(8,128)S(1)}, f32[7,8,128]{2,1,0:T(8,128)S(1)}) custom-call(f32[40,8,128]{2,1,0:T(8,128)S(1)} %collective-permute-done.2.near), custom_call_target="tpu_custom_call" | custom-call | tf_op jit(solution)/shard_map/pack_near_edges/pallas_call | solution.py:456
  11.6 0.1 collective-permute-start.5
  11.7 0.6 %collective-permute-start.6 = (f32[7,8,128]{2,1,0:T(8,128)S(1)}, f32[7,8,128]{2,1,0:T(8,128)S(1)}, u32[]{:S(2)}, u32[]{:S(2)}) collective-permute-start(f32[7,8,128]{2,1,0:T(8,128)S(1)} %get-tuple-element.40), channel_id=1, source_target_pairs={{0,8},{8,0},{16,24},{24,16},{1,9},{9,1},{17,25},{25,17},{2,10},{10... | collective-permute-start | bytes 86024 | tf_op jit(solution)/shard_map/ppermute | solution.py:496
  12.3 0.8 %prepare_own.1 = (f32[40,2,8,128]{3,2,1,0:T(8,128)S(1)}, f32[16,2,8,128]{3,2,1,0:T(8,128)S(1)}, f32[16,2,8,128]{3,2,1,0:T(8,128)S(1)}, f32[16,2,8,128]{3,2,1,0:T...) custom-call(f32[3,16,8,128]{3,2,1,0:T(8,128)S(1)} %get-tuple-element, ...), custom_call_target="tpu_custom_call" | custom-call | flops 2000000000 | tf_op jit(solution)/shard_map/prepare_own/pallas_call | solution.py:456
  13.1 0.8 %collective-permute-done.4.far_strips = f32[7,8,128]{2,1,0:T(8,128)S(1)} collective-permute-done((f32[7,8,128]{2,1,0:T(8,128)S(1)}, f32[7,8,128]{2,1,0:T(8,128)S(1)}, u32[]{:S(2)}, u32[]{:S(2)}) %collective-permute-start.4) | collective-permute-done | bytes 28704 | tf_op jit(solution)/shard_map/ppermute | solution.py:493
  13.9 0.0 collective-permute-done.3.far
  13.9 1.0 %collective-permute-done.5.near_other = f32[7,8,128]{2,1,0:T(8,128)S(1)} collective-permute-done((f32[7,8,128]{2,1,0:T(8,128)S(1)}, f32[7,8,128]{2,1,0:T(8,128)S(1)}, u32[]{:S(2)}, u32[]{:S(2)}) %collective-permute-start.5) | collective-permute-done | bytes 28704 | tf_op jit(solution)/shard_map/ppermute | solution.py:495
  14.9 0.0 collective-permute-done.6.near_pair
  14.9 3.1 %solve_all.1 = f32[128,128]{1,0:T(8,128)} custom-call(f32[16,2,8,128]{3,2,1,0:T(8,128)S(1)} %get-tuple-element.28.own_rhs, f32[16,2,8,128]{3,2,1,0:T(8,128)S(1)} %get-tuple-element.29.own_cond, f32[16,2,8,128]{3,2,1,0:T(8,128)S(1)} %get-tuple-element.30.own_x, f32[16,2,8,128]{3,2,1,0:T(8,128)S(1)} %get-tuple-element.31.own_z, ...), custom_call_target="tpu_custom_call" | custom-call | tf_op jit(solution)/shard_map/solve_all/pallas_call | solution.py:456
  (1 shorter events, 0.0 us)
Async XLA Ops:
  0.0 0.9 %copy-start = (f32[8,16,128]{2,1,0:T(8,128)S(1)}, f32[8,16,128]{2,1,0:T(8,128)}, u32[]{:S(2)}) copy-start(f32[8,16,128]{2,1,0:T(8,128)} %param.3) | copy-start | bytes 196612
  0.0 0.9 %copy-start.1 = (f32[8,16,128]{2,1,0:T(8,128)S(1)}, f32[8,16,128]{2,1,0:T(8,128)}, u32[]{:S(2)}) copy-start(f32[8,16,128]{2,1,0:T(8,128)} %param.4) | copy-start | bytes 196612
  1.2 10.1 %collective-permute-start.2 = (f32[40,8,128]{2,1,0:T(8,128)S(1)}, f32[40,8,128]{2,1,0:T(8,128)S(1)}, u32[]{:S(2)}, u32[]{:S(2)}) collective-permute-start(f32[40,8,128]{2,1,0:T(8,128)S(1)} %get-tuple-element.27), channel_id=1, source_target_pairs={{0,1},{1,0},{2,3},{3,2},{4,5},{5,4},{6,7},{7,6},{8,9},{9,8},{10,11... | collective-permute-start | bytes 491528 | tf_op jit(solution)/shard_map/ppermute | solution.py:490
  2.8 3.9 %collective-permute-start = (f32[8,8,128]{2,1,0:T(8,128)S(1)}, f32[8,8,128]{2,1,0:T(8,128)S(1)}, u32[]{:S(2)}, u32[]{:S(2)}) collective-permute-start(f32[8,8,128]{2,1,0:T(8,128)S(1)} %get-tuple-element.24), channel_id=1, source_target_pairs={{0,24},{8,16},{16,8},{24,0},{1,25},{9,17},{17,9},{25,1},{2,26},{10... | collective-permute-start | bytes 98312 | tf_op jit(solution)/shard_map/ppermute | solution.py:484
  3.5 3.3 %collective-permute-start.1 = (f32[8,8,128]{2,1,0:T(8,128)S(1)}, f32[8,8,128]{2,1,0:T(8,128)S(1)}, u32[]{:S(2)}, u32[]{:S(2)}) collective-permute-start(f32[8,8,128]{2,1,0:T(8,128)S(1)} %get-tuple-element.25), channel_id=1, source_target_pairs={{0,8},{8,0},{16,24},{24,16},{1,9},{9,1},{17,25},{25,17},{2,10},{10... | collective-permute-start | bytes 98312 | tf_op jit(solution)/shard_map/ppermute | solution.py:485
  4.4 9.5 %collective-permute-start.3 = (f32[40,8,128]{2,1,0:T(8,128)S(1)}, f32[40,8,128]{2,1,0:T(8,128)S(1)}, u32[]{:S(2)}, u32[]{:S(2)}) collective-permute-start(f32[40,8,128]{2,1,0:T(8,128)S(1)} %get-tuple-element.37), channel_id=1, source_target_pairs={{1,2},{3,4},{5,6},{2,1},{4,3},{6,5},{9,10},{11,12},{13,14},{10,9},... | collective-permute-start | bytes 491528 | tf_op jit(solution)/shard_map/ppermute | solution.py:491
  6.9 7.0 %collective-permute-start.4 = (f32[7,8,128]{2,1,0:T(8,128)S(1)}, f32[7,8,128]{2,1,0:T(8,128)S(1)}, u32[]{:S(2)}, u32[]{:S(2)}) collective-permute-start(f32[7,8,128]{2,1,0:T(8,128)S(1)} %get-tuple-element.38), channel_id=1, source_target_pairs={{1,2},{3,4},{5,6},{2,1},{4,3},{6,5},{9,10},{11,12},{13,14},{10,9},... | collective-permute-start | bytes 86024 | tf_op jit(solution)/shard_map/ppermute | solution.py:493
  11.6 3.4 %collective-permute-start.5 = (f32[7,8,128]{2,1,0:T(8,128)S(1)}, f32[7,8,128]{2,1,0:T(8,128)S(1)}, u32[]{:S(2)}, u32[]{:S(2)}) collective-permute-start(f32[7,8,128]{2,1,0:T(8,128)S(1)} %get-tuple-element.39), channel_id=1, source_target_pairs={{0,24},{8,16},{16,8},{24,0},{1,25},{9,17},{17,9},{25,1},{2,26},{10... | collective-permute-start | bytes 86024 | tf_op jit(solution)/shard_map/ppermute | solution.py:495
  11.7 3.3 %collective-permute-start.6 = (f32[7,8,128]{2,1,0:T(8,128)S(1)}, f32[7,8,128]{2,1,0:T(8,128)S(1)}, u32[]{:S(2)}, u32[]{:S(2)}) collective-permute-start(f32[7,8,128]{2,1,0:T(8,128)S(1)} %get-tuple-element.40), channel_id=1, source_target_pairs={{0,8},{8,0},{16,24},{24,16},{1,9},{9,1},{17,25},{25,17},{2,10},{10... | collective-permute-start | bytes 86024 | tf_op jit(solution)/shard_map/ppermute | solution.py:496

commit v7 on v6

--- a/solution.py
+++ b/solution.py
@@ -140,7 +140,7 @@
     return jnp.concatenate([first, jnp.where(in_right, turn(from_right, -SPAN, 2), turn(from_left, LEFT_AT, 2))])
 
 
-def pack_strips(from_other, from_pair, strips, to_far):
+def pack_strips(from_pair, from_other, near, strips, to_far, near_other, near_pair):
     lane = lanes()
     in_right = lane < SPAN
     slot_right, slot_left = slots(lane)
@@ -154,6 +154,26 @@
         takes_left = around_left & (slot_left >= 8 - first - second) & (slot_left < 8 - first)
         value = jnp.where(takes_left, turn(deep, -first), rows[layer])
         to_far[layer] = jnp.where(takes_right, turn(deep, 8 - second), value)
+    half = DK // 2
+
+    def edge(slot, first):
+        index = first + lax.rem(slot, 8) + HALF * lax.rem(lax.div(slot, 8), 2)
+        return jnp.clip(index, 0, CA - 1)
+
+    left_order = edge(lane, 0)
+    right_order = jnp.where(lane < SPAN, edge(lane, HALF - STRIP), edge(lane + (16 * 4 - LEFT_AT), HALF - STRIP))
+    left = right = jnp.zeros((half, NZ, CA), jnp.float32)
+    for number, start in enumerate((0, DG, DG + DK)):
+        for part in range(2):
+            last = DK if number == 1 else DG
+            edges = jnp.stack([near[start + min(part * half + n, last - 1)] for n in range(half)])
+            base = part * SPAN + 16 * number
+            left = jnp.where(any_of(lane, (base, base + 16)), picked(edges, left_order), left)
+            base = (1 - part) * LEFT_AT + 16 * number
+            right = jnp.where(any_of(lane, (base, base + 16)), picked(edges, right_order), right)
+    uneven = odd_aisle()
+    near_pair[...] = jnp.where(uneven, left, right)
+    near_other[...] = jnp.where(uneven, right, left)
 
 
 def unpack_strips(pairs, lane):
@@ -264,28 +284,9 @@
             levels[done + 1, at] = inverse[at] * (power * rhs[at] + around(weights, first, count, here, below, above))
 
 
-def pack_near_edges(near, to_other, to_pair):
-    half = DK // 2
-    lane = lanes()
-
-    def edge(slot, first):
-        index = first + lax.rem(slot, 8) + HALF * lax.rem(lax.div(slot, 8), 2)
-        return jnp.clip(index, 0, CA - 1)
-
-    left_order = edge(lane, 0)
-    right_order = jnp.where(lane < SPAN, edge(lane, HALF - STRIP), edge(lane + (16 * 4 - LEFT_AT), HALF - STRIP))
-    left = right = jnp.zeros((half, NZ, CA), jnp.float32)
-    for number, start in enumerate((0, DG, DG + DK)):
-        for part in range(2):
-            last = DK if number == 1 else DG
-            rows = jnp.stack([near[start + min(part * half + n, last - 1)] for n in range(half)])
-            base = part * SPAN + 16 * number
-            left = jnp.where(any_of(lane, (base, base + 16)), picked(rows, left_order), left)
-            base = (1 - part) * LEFT_AT + 16 * number
-            right = jnp.where(any_of(lane, (base, base + 16)), picked(rows, right_order), right)
-    uneven = odd_aisle()
-    to_pair[...] = jnp.where(uneven, left, right)
-    to_other[...] = jnp.where(uneven, right, left)
+def split_far(far, tiles):
+    tiles[:DG] = split(far[:DG], False)
+    tiles[DG:] = split(far[DG:], True)
 
 
 def solve_all(own_rhs, own_cond, own_x, own_z, own_r, own_part, own_inverse, levels, near, far, far_strips, near_other, near_pair, out,
@@ -313,17 +314,16 @@
 
     sides = [(far, unpack_strips(far_strips, lane)[::-1], True), (near, side_by_side(*right_and_left(near_other, near_pair)), False)]
     for block, strip, is_far in sides:
-        part_of = (lambda at, copies: split(block[at], copies)) if is_far else (lambda at, copies: block[at])
         for low, high in ((0, 7), (7, DK)):
             at = pl.ds((0 if is_far else DK + CR) + low, high - low)
-            cond[at] = expand(part_of(pl.ds(DG + low, high - low), True), jnp.stack(strip[low:high]), 1, True)
+            cond[at] = expand(block[pl.ds(DG + low, high - low)], jnp.stack(strip[low:high]), 1, True)
         strip = strip[1:] if is_far else strip[:DG]
         for low, high in ((0, 7), (7, DG)):
             beside = jnp.stack(strip[low:high])
             at = pl.ds((1 if is_far else DK + CR) + low, high - low)
-            part[at] = expand(part_of(pl.ds(DG + DK + low, high - low), True), beside, 2, True)
+            part[at] = expand(block[pl.ds(DG + DK + low, high - low)], beside, 2, True)
             at = pl.ds((0 if is_far else NEAR_BOX[2] + OV) + low, high - low)
-            rhs[at] = expand(part_of(pl.ds(low, high - low), False), beside, 0, False)
+            rhs[at] = expand(block[pl.ds(low, high - low)], beside, 0, False)
     for first in (1, DK + CR):
         for low, high in ((0, 7), (7, DG)):
             at = pl.ds(first + low, high - low)
@@ -481,17 +481,17 @@
     far_pairs = [(i, i + 1) for i in range(1, rows - 1, 2)]
     far_pairs += [(b, a) for a, b in far_pairs]
     near_pairs = [(i, i ^ 1) for i in range(rows)]
+    from_pair = lax.ppermute(to_pair, "aisle", pair)
     from_other = lax.ppermute(to_other, "aisle", other)
-    from_pair = lax.ppermute(to_pair, "aisle", pair)
     to_far, to_near = call(
         pack_rows, (tile(TILES), tile(TILES)), main,
         cost=busy,
     )
     near = lax.ppermute(to_near, "row", near_pairs)
     far = lax.ppermute(to_far, "row", far_pairs)
-    strips, strips_far = call(pack_strips, (tile(CR), tile(DK // 2)), from_other, from_pair)
+    half = tile(DK // 2)
+    strips, strips_far, near_to_other, near_to_pair = call(pack_strips, (tile(CR), half, half, half), from_pair, from_other, near)
     far_strips = lax.ppermute(strips_far, "row", far_pairs)
-    near_to_other, near_to_pair = call(pack_near_edges, (tile(DK // 2), tile(DK // 2)), near, cost=None)
     near_other = lax.ppermute(near_to_other, "aisle", other)
     near_pair = lax.ppermute(near_to_pair, "aisle", pair)
     own_rows = (tile(CR, 2),) * 7 + (tile(SWEEPS + 1, CR, 2),)
@@ -503,7 +503,7 @@
     result = call(
         solve_all,
         jax.ShapeDtypeStruct(flat, jnp.float32),
-        *own, near_tiles, far, far_strips, near_other, near_pair,
+        *own, near_tiles, call(split_far, tile(TILES, 2), far), far_strips, near_other, near_pair,
         scratch=[
             pair_rows(around), pair_rows(around), pair_rows(around), pair_rows(around), pair_rows(around),
             pair_rows(ROWS), pair_rows(ROWS), pair_rows(GUARDED), pair_rows(GUARDED), pair_rows(CR + 2 * REACH),

time: 18.2 us -> 18.1 us (level)
    ppermute x1, starting transfers between devices: 0.96 us -> 0.01 us  [body(): from_pair = lax.ppermute(to_pair, 'aisle', pair)]
    ppermute x1, starting transfers between devices: 0.65 us -> 1.6 us  [body(): from_other = lax.ppermute(to_other, 'aisle', other)]
    ppermute x1, waiting for transfers between devices: 0.01 us -> 0.5 us  [body(): near = lax.ppermute(to_near, 'row', near_pairs)]
    ppermute x1, starting transfers between devices: 4.44 us -> 3.96 us  [body(): far_strips = lax.ppermute(strips_far, 'row', far_pairs)]
    ppermute x1, waiting for transfers between devices: 0.8 us -> 0.37 us  [body(): far_strips = lax.ppermute(strips_far, 'row', far_pairs)]
    ppermute x1, waiting for transfers between devices: 1.01 us -> 0.66 us  [body(): near_other = lax.ppermute(near_to_other, 'aisle', other)]
    ppermute x1, waiting for transfers between devices: 0.01 us -> 0.32 us  [body(): far = lax.ppermute(to_far, 'row', far_pairs)]
    ppermute x1, starting transfers between devices: 0.64 us -> 0.95 us  [body(): near_pair = lax.ppermute(near_to_pair, 'aisle', pair)]
  transfers between devices with their start and end apart: 7 -> 7, of which waited for: 2 -> 4; matrix products, arithmetic and copies ran while one was open for 0% -> 0% of each run, Pallas kernels for 7% -> 7%
where the time goes in v7:
time: 18.1 us; the launch traced here: 17.9 us
  starting transfers between devices  10.5 us (58%)
  Pallas kernels  4.57 us (25%)
  waiting for transfers between devices  1.85 us (10%)
  other arithmetic  0.88 us (5%)
    pallas_call x6, Pallas kernels, call(): pl.pallas_call(kernel, out_shape=outs, in_specs=[vmem] * len(args), out_s...  4.57 us
    ppermute x1, starting transfers between devices, body(): far_strips = lax.ppermute(strips_far, 'row', far_pairs)  3.96 us
    ppermute x1, starting transfers between devices, body(): far = lax.ppermute(to_far, 'row', far_pairs)  2.29 us
    ppermute x1, starting transfers between devices, body(): from_other = lax.ppermute(to_other, 'aisle', other)  1.6 us
    ppermute x1, starting transfers between devices, body(): near = lax.ppermute(to_near, 'row', near_pairs)  1.58 us
    ppermute x1, starting transfers between devices, body(): near_pair = lax.ppermute(near_to_pair, 'aisle', pair)  0.95 us
    add x1, other arithmetic, body(): shift = 0.1 + 40.0 * solid.astype(jnp.float32)  0.88 us
    ppermute x1, waiting for transfers between devices, body(): near_other = lax.ppermute(near_to_other, 'aisle', other)  0.66 us
  transfers between devices with their start and end apart: 7, of which 4 were waited for; matrix products, arithmetic and copies ran while one was open for 0% of the time, Pallas kernels for 7%

profile of v7, /device:TPU:8, one launch (start us, length us, event | category | flops | bytes accessed | tf_op | source)
XLA Modules:
  0.0 17.9 jit_solution(4214278267166940736)
XLA Ops:
  0.0 0.0 copy-start
  0.0 0.0 copy-start.1
  0.0 0.9 %multiply_add_fusion = f32[8,16,128]{2,1,0:T(8,128)S(1)} fusion(s32[8,16,128]{2,1,0:T(8,128)} %param.5), kind=kLoop, calls=%fused_computation | loop fusion | flops 49152 | bytes 131072 | tf_op jit(solution)/shard_map/add | solution.py:474
  0.9 0.0 copy-done
  0.9 0.0 copy-done.1
  0.9 0.3 %pack_edges.1 = (f32[3,16,8,128]{3,2,1,0:T(8,128)S(1)}, f32[8,8,128]{2,1,0:T(8,128)S(1)}, f32[8,8,128]{2,1,0:T(8,128)S(1)}) custom-call(f32[128,128]{1,0:T(8,128)S(1)} %bitcast.5, f32[128,128]{1,0:T(8,128)S(1)} %bitcast.6, f32[128,128]{1,0:T(8,128)S(1)} %bitcast.4), custom_call_target="tpu_custom_call" | custom-call | tf_op jit(solution)/shard_map/pack_edges/pallas_call | solution.py:456
  1.2 1.6 %collective-permute-start.2 = (f32[40,8,128]{2,1,0:T(8,128)S(1)}, f32[40,8,128]{2,1,0:T(8,128)S(1)}, u32[]{:S(2)}, u32[]{:S(2)}) collective-permute-start(f32[40,8,128]{2,1,0:T(8,128)S(1)} %get-tuple-element.26), channel_id=1, source_target_pairs={{0,1},{1,0},{2,3},{3,2},{4,5},{5,4},{6,7},{7,6},{8,9},{9,8},{10,11... | collective-permute-start | bytes 491528 | tf_op jit(solution)/shard_map/ppermute | solution.py:490
  2.8 0.0 collective-permute-start
  2.8 1.6 %collective-permute-start.1 = (f32[8,8,128]{2,1,0:T(8,128)S(1)}, f32[8,8,128]{2,1,0:T(8,128)S(1)}, u32[]{:S(2)}, u32[]{:S(2)}) collective-permute-start(f32[8,8,128]{2,1,0:T(8,128)S(1)} %get-tuple-element.25), channel_id=1, source_target_pairs={{0,24},{8,16},{16,8},{24,0},{1,25},{9,17},{17,9},{25,1},{2,26},{10... | collective-permute-start | bytes 98312 | tf_op jit(solution)/shard_map/ppermute | solution.py:485
  4.4 2.3 %collective-permute-start.3 = (f32[40,8,128]{2,1,0:T(8,128)S(1)}, f32[40,8,128]{2,1,0:T(8,128)S(1)}, u32[]{:S(2)}, u32[]{:S(2)}) collective-permute-start(f32[40,8,128]{2,1,0:T(8,128)S(1)} %get-tuple-element.37), channel_id=1, source_target_pairs={{1,2},{3,4},{5,6},{2,1},{4,3},{6,5},{9,10},{11,12},{13,14},{10,9},... | collective-permute-start | bytes 491528 | tf_op jit(solution)/shard_map/ppermute | solution.py:491
  6.7 0.0 collective-permute-done.from_pair
  6.7 0.0 collective-permute-done.1.from_other
  6.7 0.5 %collective-permute-done.2.near = f32[40,8,128]{2,1,0:T(8,128)S(1)} collective-permute-done((f32[40,8,128]{2,1,0:T(8,128)S(1)}, f32[40,8,128]{2,1,0:T(8,128)S(1)}, u32[]{:S(2)}, u32[]{:S(2)}) %collective-permute-start.2) | collective-permute-done | bytes 163872 | tf_op jit(solution)/shard_map/ppermute | solution.py:490
  7.2 0.2 %pack_strips.1 = (f32[16,8,128]{2,1,0:T(8,128)S(1)}, f32[7,8,128]{2,1,0:T(8,128)S(1)}, f32[7,8,128]{2,1,0:T(8,128)S(1)}, f32[7,8,128]{2,1,0:T(8,128)S(1)}) custom-call(f32[8,8,128]{2,1,0:T(8,128)S(1)} %collective-permute-done.from_pair, f32[8,8,128]{2,1,0:T(8,128)S(1)} %collective-permute-done.1.from_other, f32[40,8,128]{2,1,0:T(8,128)S(1)} %collective-permute-done.2.near), custom_call_target="tpu_custom_call" | custom-call | tf_op jit(solution)/shard_map/pack_strips/pallas_call | solution.py:456
  7.5 4.0 %collective-permute-start.4 = (f32[7,8,128]{2,1,0:T(8,128)S(1)}, f32[7,8,128]{2,1,0:T(8,128)S(1)}, u32[]{:S(2)}, u32[]{:S(2)}) collective-permute-start(f32[7,8,128]{2,1,0:T(8,128)S(1)} %get-tuple-element.38), channel_id=1, source_target_pairs={{1,2},{3,4},{5,6},{2,1},{4,3},{6,5},{9,10},{11,12},{13,14},{10,9},... | collective-permute-start | bytes 86024 | tf_op jit(solution)/shard_map/ppermute | solution.py:494
  11.4 0.1 collective-permute-start.5
  11.5 0.9 %collective-permute-start.6 = (f32[7,8,128]{2,1,0:T(8,128)S(1)}, f32[7,8,128]{2,1,0:T(8,128)S(1)}, u32[]{:S(2)}, u32[]{:S(2)}) collective-permute-start(f32[7,8,128]{2,1,0:T(8,128)S(1)} %get-tuple-element.40), channel_id=1, source_target_pairs={{0,8},{8,0},{16,24},{24,16},{1,9},{9,1},{17,25},{25,17},{2,10},{10... | collective-permute-start | bytes 86024 | tf_op jit(solution)/shard_map/ppermute | solution.py:496
  12.5 0.8 %prepare_own.1 = (f32[40,2,8,128]{3,2,1,0:T(8,128)S(1)}, f32[16,2,8,128]{3,2,1,0:T(8,128)S(1)}, f32[16,2,8,128]{3,2,1,0:T(8,128)S(1)}, f32[16,2,8,128]{3,2,1,0:T...) custom-call(f32[3,16,8,128]{3,2,1,0:T(8,128)S(1)} %get-tuple-element, ...), custom_call_target="tpu_custom_call" | custom-call | flops 2000000000 | tf_op jit(solution)/shard_map/prepare_own/pallas_call | solution.py:456
  13.3 0.3 %collective-permute-done.3.far = f32[40,8,128]{2,1,0:T(8,128)S(1)} collective-permute-done((f32[40,8,128]{2,1,0:T(8,128)S(1)}, f32[40,8,128]{2,1,0:T(8,128)S(1)}, u32[]{:S(2)}, u32[]{:S(2)}) %collective-permute-start.3) | collective-permute-done | bytes 163872 | tf_op jit(solution)/shard_map/ppermute | solution.py:491
  13.6 0.1 split_far.1.far
  13.8 0.4 %collective-permute-done.4.far_strips = f32[7,8,128]{2,1,0:T(8,128)S(1)} collective-permute-done((f32[7,8,128]{2,1,0:T(8,128)S(1)}, f32[7,8,128]{2,1,0:T(8,128)S(1)}, u32[]{:S(2)}, u32[]{:S(2)}) %collective-permute-start.4) | collective-permute-done | bytes 28704 | tf_op jit(solution)/shard_map/ppermute | solution.py:494
  14.1 0.7 %collective-permute-done.5.near_other = f32[7,8,128]{2,1,0:T(8,128)S(1)} collective-permute-done((f32[7,8,128]{2,1,0:T(8,128)S(1)}, f32[7,8,128]{2,1,0:T(8,128)S(1)}, u32[]{:S(2)}, u32[]{:S(2)}) %collective-permute-start.5) | collective-permute-done | bytes 28704 | tf_op jit(solution)/shard_map/ppermute | solution.py:495
  14.8 0.0 collective-permute-done.6.near_pair
  14.8 3.1 %solve_all.1 = f32[128,128]{1,0:T(8,128)} custom-call(f32[16,2,8,128]{3,2,1,0:T(8,128)S(1)} %get-tuple-element.28.own_rhs, f32[16,2,8,128]{3,2,1,0:T(8,128)S(1)} %get-tuple-element.29.own_cond, f32[16,2,8,128]{3,2,1,0:T(8,128)S(1)} %get-tuple-element.30.own_x, f32[16,2,8,128]{3,2,1,0:T(8,128)S(1)} %get-tuple-element.31.own_z, ...), custom_call_target="tpu_custom_call" | custom-call | tf_op jit(solution)/shard_map/solve_all/pallas_call | solution.py:456
  (1 shorter events, 0.0 us)
Async XLA Ops:
  0.0 0.9 %copy-start = (f32[8,16,128]{2,1,0:T(8,128)S(1)}, f32[8,16,128]{2,1,0:T(8,128)}, u32[]{:S(2)}) copy-start(f32[8,16,128]{2,1,0:T(8,128)} %param.3) | copy-start | bytes 196612
  0.0 0.9 %copy-start.1 = (f32[8,16,128]{2,1,0:T(8,128)S(1)}, f32[8,16,128]{2,1,0:T(8,128)}, u32[]{:S(2)}) copy-start(f32[8,16,128]{2,1,0:T(8,128)} %param.4) | copy-start | bytes 196612
  1.2 6.0 %collective-permute-start.2 = (f32[40,8,128]{2,1,0:T(8,128)S(1)}, f32[40,8,128]{2,1,0:T(8,128)S(1)}, u32[]{:S(2)}, u32[]{:S(2)}) collective-permute-start(f32[40,8,128]{2,1,0:T(8,128)S(1)} %get-tuple-element.26), channel_id=1, source_target_pairs={{0,1},{1,0},{2,3},{3,2},{4,5},{5,4},{6,7},{7,6},{8,9},{9,8},{10,11... | collective-permute-start | bytes 491528 | tf_op jit(solution)/shard_map/ppermute | solution.py:490
  2.8 3.9 %collective-permute-start = (f32[8,8,128]{2,1,0:T(8,128)S(1)}, f32[8,8,128]{2,1,0:T(8,128)S(1)}, u32[]{:S(2)}, u32[]{:S(2)}) collective-permute-start(f32[8,8,128]{2,1,0:T(8,128)S(1)} %get-tuple-element.24), channel_id=1, source_target_pairs={{0,8},{8,0},{16,24},{24,16},{1,9},{9,1},{17,25},{25,17},{2,10},{10... | collective-permute-start | bytes 98312 | tf_op jit(solution)/shard_map/ppermute | solution.py:484
  2.8 3.9 %collective-permute-start.1 = (f32[8,8,128]{2,1,0:T(8,128)S(1)}, f32[8,8,128]{2,1,0:T(8,128)S(1)}, u32[]{:S(2)}, u32[]{:S(2)}) collective-permute-start(f32[8,8,128]{2,1,0:T(8,128)S(1)} %get-tuple-element.25), channel_id=1, source_target_pairs={{0,24},{8,16},{16,8},{24,0},{1,25},{9,17},{17,9},{25,1},{2,26},{10... | collective-permute-start | bytes 98312 | tf_op jit(solution)/shard_map/ppermute | solution.py:485
  4.4 9.2 %collective-permute-start.3 = (f32[40,8,128]{2,1,0:T(8,128)S(1)}, f32[40,8,128]{2,1,0:T(8,128)S(1)}, u32[]{:S(2)}, u32[]{:S(2)}) collective-permute-start(f32[40,8,128]{2,1,0:T(8,128)S(1)} %get-tuple-element.37), channel_id=1, source_target_pairs={{1,2},{3,4},{5,6},{2,1},{4,3},{6,5},{9,10},{11,12},{13,14},{10,9},... | collective-permute-start | bytes 491528 | tf_op jit(solution)/shard_map/ppermute | solution.py:491
  7.5 6.7 %collective-permute-start.4 = (f32[7,8,128]{2,1,0:T(8,128)S(1)}, f32[7,8,128]{2,1,0:T(8,128)S(1)}, u32[]{:S(2)}, u32[]{:S(2)}) collective-permute-start(f32[7,8,128]{2,1,0:T(8,128)S(1)} %get-tuple-element.38), channel_id=1, source_target_pairs={{1,2},{3,4},{5,6},{2,1},{4,3},{6,5},{9,10},{11,12},{13,14},{10,9},... | collective-permute-start | bytes 86024 | tf_op jit(solution)/shard_map/ppermute | solution.py:494
  11.4 3.4 %collective-permute-start.5 = (f32[7,8,128]{2,1,0:T(8,128)S(1)}, f32[7,8,128]{2,1,0:T(8,128)S(1)}, u32[]{:S(2)}, u32[]{:S(2)}) collective-permute-start(f32[7,8,128]{2,1,0:T(8,128)S(1)} %get-tuple-element.39), channel_id=1, source_target_pairs={{0,24},{8,16},{16,8},{24,0},{1,25},{9,17},{17,9},{25,1},{2,26},{10... | collective-permute-start | bytes 86024 | tf_op jit(solution)/shard_map/ppermute | solution.py:495
  11.5 3.3 %collective-permute-start.6 = (f32[7,8,128]{2,1,0:T(8,128)S(1)}, f32[7,8,128]{2,1,0:T(8,128)S(1)}, u32[]{:S(2)}, u32[]{:S(2)}) collective-permute-start(f32[7,8,128]{2,1,0:T(8,128)S(1)} %get-tuple-element.40), channel_id=1, source_target_pairs={{0,8},{8,0},{16,24},{24,16},{1,9},{9,1},{17,25},{25,17},{2,10},{10... | collective-permute-start | bytes 86024 | tf_op jit(solution)/shard_map/ppermute | solution.py:496

commit v8 on v7

--- a/solution.py
+++ b/solution.py
@@ -79,7 +79,7 @@
     return ref[pl.ds(first, count)]
 
 
-def pack_edges(source, conduct, shift, main, to_other, to_pair):
+def pack_edges(source, conduct, shift, main, to_other, to_pair, to_far, to_near):
     odd = lax.rem(lax.axis_index("row"), 2)
     half = CR // 2
     shape = (half * NZ, CA)
@@ -108,21 +108,18 @@
             right = jnp.where(any_of(lane, (base, base + 16)), pick(rows, right_order), right)
     left = left.reshape(half, NZ, CA)
     right = right.reshape(half, NZ, CA)
-    uneven = odd_aisle()
-    to_pair[...] = jnp.where(uneven, left, right)
-    to_other[...] = jnp.where(uneven, right, left)
-
-
-def odd_aisle():
-    return jnp.full((NZ, CA), lax.rem(lax.axis_index("aisle"), 2)) > 0
-
-
-def pack_rows(main, to_far, to_near):
     start = 0
     for number, depth in enumerate((DG, DK, DG)):
         to_far[pl.ds(start, depth)] = jnp.stack([main[number, depth - 1 - n] for n in range(depth)])
         to_near[pl.ds(start, depth)] = jnp.stack([main[number, CR - 1 - n] for n in range(depth)])
         start += depth
+    uneven = odd_aisle()
+    to_pair[...] = jnp.where(uneven, left, right)
+    to_other[...] = jnp.where(uneven, right, left)
+
+
+def odd_aisle():
+    return jnp.full((NZ, CA), lax.rem(lax.axis_index("aisle"), 2)) > 0
 
 
 def slots(lane):
@@ -289,6 +286,11 @@
     tiles[DG:] = split(far[DG:], True)
 
 
+def in_core(p0, row):
+    p = p0 + row
+    return {FAR_BOX[0]: p < 0, OWN_BOX[0]: 0 <= p < CR, NEAR_BOX[0]: p >= CR}[p0]
+
+
 def solve_all(own_rhs, own_cond, own_x, own_z, own_r, own_part, own_inverse, levels, near, far, far_strips, near_other, near_pair, out,
               cond, face_x, face_z, face_r, part, inverse, rhs, est_a, est_b, total):
     row_at = lax.axis_index("row")
@@ -374,8 +376,14 @@
             for p0, _, at, guarded, low, high in spans(done + 1):
                 for first, count in pieces(low, high):
                     here, below, above = [source[pl.ds(guarded + first + n, count)] for n in (0, -1, 1)]
-                    summed = power * rhs[pl.ds(at + first, count)]
-                    summed += around(weights, p0 + first + DK, count, here, below, above)
+                    summed = around(weights, p0 + first + DK, count, here, below, above)
+                    given = [row for row in range(first, first + count) if in_core(p0, row)]
+                    if len(given) == count:
+                        summed += power * rhs[pl.ds(at + first, count)]
+                    elif given:
+                        skip, end = given[0] - first, given[-1] + 1 - first
+                        more = summed[skip:end] + power * rhs[pl.ds(at + given[0], len(given))]
+                        summed = jnp.concatenate([v for v in (summed[:skip], more, summed[end:]) if v.shape[0]])
                     target[pl.ds(guarded + first, count)] = inverse[pl.ds(at + first, count)] * summed
             source, target = target, source
         borrow(SWEEPS, source)
@@ -472,8 +480,8 @@
     tile = lambda *lead: jax.ShapeDtypeStruct(lead + (NZ, CA), jnp.float32)
     busy = pl.CostEstimate(flops=10**11, bytes_accessed=0, transcendentals=0)
     shift = 0.1 + 40.0 * solid.astype(jnp.float32)
-    main, to_other, to_pair = call(
-        pack_edges, (tile(3, CR), tile(CR // 2), tile(CR // 2)),
+    main, to_other, to_pair, to_far, to_near = call(
+        pack_edges, (tile(3, CR), tile(CR // 2), tile(CR // 2), tile(TILES), tile(TILES)),
         source.reshape(flat), conduct.reshape(flat), shift.reshape(flat),
     )
     pair = [(i, i ^ 1) for i in range(aisles)]
@@ -483,10 +491,6 @@
     near_pairs = [(i, i ^ 1) for i in range(rows)]
     from_pair = lax.ppermute(to_pair, "aisle", pair)
     from_other = lax.ppermute(to_other, "aisle", other)
-    to_far, to_near = call(
-        pack_rows, (tile(TILES), tile(TILES)), main,
-        cost=busy,
-    )
     near = lax.ppermute(to_near, "row", near_pairs)
     far = lax.ppermute(to_far, "row", far_pairs)
     half = tile(DK // 2)

time: 18.1 us -> 18.1 us (level)
    pallas_call x6 -> x5, Pallas kernels: 4.57 us -> 4.55 us  [call(): pl.pallas_call(kernel, out_shape=outs, in_specs=[vmem] * len(args), out_s...]
where the time goes in v8:
time: 18.1 us; the launch traced here: 17.8 us
  starting transfers between devices  10.5 us (58%)
  Pallas kernels  4.55 us (25%)
  waiting for transfers between devices  1.85 us (10%)
  other arithmetic  0.88 us (5%)
    pallas_call x5, Pallas kernels, call(): pl.pallas_call(kernel, out_shape=outs, in_specs=[vmem] * len(args), out_s...  4.55 us
    ppermute x1, starting transfers between devices, body(): far_strips = lax.ppermute(strips_far, 'row', far_pairs)  3.96 us
    ppermute x1, starting transfers between devices, body(): far = lax.ppermute(to_far, 'row', far_pairs)  2.29 us
    ppermute x1, starting transfers between devices, body(): from_other = lax.ppermute(to_other, 'aisle', other)  1.6 us
    ppermute x1, starting transfers between devices, body(): near = lax.ppermute(to_near, 'row', near_pairs)  1.58 us
    ppermute x1, starting transfers between devices, body(): near_pair = lax.ppermute(near_to_pair, 'aisle', pair)  0.95 us
    add x1, other arithmetic, body(): shift = 0.1 + 40.0 * solid.astype(jnp.float32)  0.88 us
    ppermute x1, waiting for transfers between devices, body(): near_other = lax.ppermute(near_to_other, 'aisle', other)  0.66 us
  transfers between devices with their start and end apart: 7, of which 4 were waited for; matrix products, arithmetic and copies ran while one was open for 0% of the time, Pallas kernels for 7%

profile of v8, /device:TPU:8, one launch (start us, length us, event | category | flops | bytes accessed | tf_op | source)
XLA Modules:
  0.0 17.8 jit_solution(15429351408832953977)
XLA Ops:
  0.0 0.0 copy-start
  0.0 0.0 copy-start.1
  0.0 0.9 %multiply_add_fusion = f32[8,16,128]{2,1,0:T(8,128)S(1)} fusion(s32[8,16,128]{2,1,0:T(8,128)} %param.5), kind=kLoop, calls=%fused_computation | loop fusion | flops 49152 | bytes 131072 | tf_op jit(solution)/shard_map/add | solution.py:482
  0.9 0.0 copy-done
  0.9 0.0 copy-done.1
  0.9 0.3 %pack_edges.1 = (f32[3,16,8,128]{3,2,1,0:T(8,128)S(1)}, f32[8,8,128]{2,1,0:T(8,128)S(1)}, f32[8,8,128]{2,1,0:T(8,128)S(1)}, f32[40,8,128]{2,1,0:T(8,128)S(1)}, f32[40,8,128]{2,1,0:T(8,128)S(1)}) custom-call(f32[128,128]{1,0:T(8,128)S(1)} %bitcast.5, f32[128,128]{1,0:T(8,128)S(1)} %bitcast.6, f32[128,128]{1,0:T(8,128)S(1)} %bitcast.4), custom_call_target="tpu_custom_call" | custom-call | tf_op jit(solution)/shard_map/pack_edges/pallas_call | solution.py:464
  1.2 1.6 %collective-permute-start.2 = (f32[40,8,128]{2,1,0:T(8,128)S(1)}, f32[40,8,128]{2,1,0:T(8,128)S(1)}, u32[]{:S(2)}, u32[]{:S(2)}) collective-permute-start(f32[40,8,128]{2,1,0:T(8,128)S(1)} %get-tuple-element.26), channel_id=1, source_target_pairs={{0,1},{1,0},{2,3},{3,2},{4,5},{5,4},{6,7},{7,6},{8,9},{9,8},{10,11... | collective-permute-start | bytes 491528 | tf_op jit(solution)/shard_map/ppermute | solution.py:494
  2.8 0.0 collective-permute-start
  2.8 1.6 %collective-permute-start.1 = (f32[8,8,128]{2,1,0:T(8,128)S(1)}, f32[8,8,128]{2,1,0:T(8,128)S(1)}, u32[]{:S(2)}, u32[]{:S(2)}) collective-permute-start(f32[8,8,128]{2,1,0:T(8,128)S(1)} %get-tuple-element.25), channel_id=1, source_target_pairs={{0,24},{8,16},{16,8},{24,0},{1,25},{9,17},{17,9},{25,1},{2,26},{10... | collective-permute-start | bytes 98312 | tf_op jit(solution)/shard_map/ppermute | solution.py:493
  4.4 2.3 %collective-permute-start.3 = (f32[40,8,128]{2,1,0:T(8,128)S(1)}, f32[40,8,128]{2,1,0:T(8,128)S(1)}, u32[]{:S(2)}, u32[]{:S(2)}) collective-permute-start(f32[40,8,128]{2,1,0:T(8,128)S(1)} %get-tuple-element.37), channel_id=1, source_target_pairs={{1,2},{3,4},{5,6},{2,1},{4,3},{6,5},{9,10},{11,12},{13,14},{10,9},... | collective-permute-start | bytes 491528 | tf_op jit(solution)/shard_map/ppermute | solution.py:495
  6.7 0.0 collective-permute-done.from_pair
  6.7 0.0 collective-permute-done.1.from_other
  6.7 0.5 %collective-permute-done.2.near = f32[40,8,128]{2,1,0:T(8,128)S(1)} collective-permute-done((f32[40,8,128]{2,1,0:T(8,128)S(1)}, f32[40,8,128]{2,1,0:T(8,128)S(1)}, u32[]{:S(2)}, u32[]{:S(2)}) %collective-permute-start.2) | collective-permute-done | bytes 163872 | tf_op jit(solution)/shard_map/ppermute | solution.py:494
  7.2 0.2 %pack_strips.1 = (f32[16,8,128]{2,1,0:T(8,128)S(1)}, f32[7,8,128]{2,1,0:T(8,128)S(1)}, f32[7,8,128]{2,1,0:T(8,128)S(1)}, f32[7,8,128]{2,1,0:T(8,128)S(1)}) custom-call(f32[8,8,128]{2,1,0:T(8,128)S(1)} %collective-permute-done.from_pair, f32[8,8,128]{2,1,0:T(8,128)S(1)} %collective-permute-done.1.from_other, f32[40,8,128]{2,1,0:T(8,128)S(1)} %collective-permute-done.2.near), custom_call_target="tpu_custom_call" | custom-call | tf_op jit(solution)/shard_map/pack_strips/pallas_call | solution.py:464
  7.4 4.0 %collective-permute-start.4 = (f32[7,8,128]{2,1,0:T(8,128)S(1)}, f32[7,8,128]{2,1,0:T(8,128)S(1)}, u32[]{:S(2)}, u32[]{:S(2)}) collective-permute-start(f32[7,8,128]{2,1,0:T(8,128)S(1)} %get-tuple-element.38), channel_id=1, source_target_pairs={{1,2},{3,4},{5,6},{2,1},{4,3},{6,5},{9,10},{11,12},{13,14},{10,9},... | collective-permute-start | bytes 86024 | tf_op jit(solution)/shard_map/ppermute | solution.py:498
  11.4 0.1 collective-permute-start.5
  11.5 0.9 %collective-permute-start.6 = (f32[7,8,128]{2,1,0:T(8,128)S(1)}, f32[7,8,128]{2,1,0:T(8,128)S(1)}, u32[]{:S(2)}, u32[]{:S(2)}) collective-permute-start(f32[7,8,128]{2,1,0:T(8,128)S(1)} %get-tuple-element.40), channel_id=1, source_target_pairs={{0,8},{8,0},{16,24},{24,16},{1,9},{9,1},{17,25},{25,17},{2,10},{10... | collective-permute-start | bytes 86024 | tf_op jit(solution)/shard_map/ppermute | solution.py:500
  12.4 0.8 %prepare_own.1 = (f32[40,2,8,128]{3,2,1,0:T(8,128)S(1)}, f32[16,2,8,128]{3,2,1,0:T(8,128)S(1)}, f32[16,2,8,128]{3,2,1,0:T(8,128)S(1)}, f32[16,2,8,128]{3,2,1,0:T...) custom-call(f32[3,16,8,128]{3,2,1,0:T(8,128)S(1)} %get-tuple-element, ...), custom_call_target="tpu_custom_call" | custom-call | flops 2000000000 | tf_op jit(solution)/shard_map/prepare_own/pallas_call | solution.py:464
  13.3 0.3 %collective-permute-done.3.far = f32[40,8,128]{2,1,0:T(8,128)S(1)} collective-permute-done((f32[40,8,128]{2,1,0:T(8,128)S(1)}, f32[40,8,128]{2,1,0:T(8,128)S(1)}, u32[]{:S(2)}, u32[]{:S(2)}) %collective-permute-start.3) | collective-permute-done | bytes 163872 | tf_op jit(solution)/shard_map/ppermute | solution.py:495
  13.6 0.1 split_far.1.far
  13.7 0.4 %collective-permute-done.4.far_strips = f32[7,8,128]{2,1,0:T(8,128)S(1)} collective-permute-done((f32[7,8,128]{2,1,0:T(8,128)S(1)}, f32[7,8,128]{2,1,0:T(8,128)S(1)}, u32[]{:S(2)}, u32[]{:S(2)}) %collective-permute-start.4) | collective-permute-done | bytes 28704 | tf_op jit(solution)/shard_map/ppermute | solution.py:498
  14.1 0.7 %collective-permute-done.5.near_other = f32[7,8,128]{2,1,0:T(8,128)S(1)} collective-permute-done((f32[7,8,128]{2,1,0:T(8,128)S(1)}, f32[7,8,128]{2,1,0:T(8,128)S(1)}, u32[]{:S(2)}, u32[]{:S(2)}) %collective-permute-start.5) | collective-permute-done | bytes 28704 | tf_op jit(solution)/shard_map/ppermute | solution.py:499
  14.8 0.0 collective-permute-done.6.near_pair
  14.8 3.1 %solve_all.1 = f32[128,128]{1,0:T(8,128)} custom-call(f32[16,2,8,128]{3,2,1,0:T(8,128)S(1)} %get-tuple-element.28.own_rhs, f32[16,2,8,128]{3,2,1,0:T(8,128)S(1)} %get-tuple-element.29.own_cond, f32[16,2,8,128]{3,2,1,0:T(8,128)S(1)} %get-tuple-element.30.own_x, f32[16,2,8,128]{3,2,1,0:T(8,128)S(1)} %get-tuple-element.31.own_z, ...), custom_call_target="tpu_custom_call" | custom-call | tf_op jit(solution)/shard_map/solve_all/pallas_call | solution.py:464
Async XLA Ops:
  0.0 0.9 %copy-start = (f32[8,16,128]{2,1,0:T(8,128)S(1)}, f32[8,16,128]{2,1,0:T(8,128)}, u32[]{:S(2)}) copy-start(f32[8,16,128]{2,1,0:T(8,128)} %param.3) | copy-start | bytes 196612
  0.0 0.9 %copy-start.1 = (f32[8,16,128]{2,1,0:T(8,128)S(1)}, f32[8,16,128]{2,1,0:T(8,128)}, u32[]{:S(2)}) copy-start(f32[8,16,128]{2,1,0:T(8,128)} %param.4) | copy-start | bytes 196612
  1.2 6.0 %collective-permute-start.2 = (f32[40,8,128]{2,1,0:T(8,128)S(1)}, f32[40,8,128]{2,1,0:T(8,128)S(1)}, u32[]{:S(2)}, u32[]{:S(2)}) collective-permute-start(f32[40,8,128]{2,1,0:T(8,128)S(1)} %get-tuple-element.26), channel_id=1, source_target_pairs={{0,1},{1,0},{2,3},{3,2},{4,5},{5,4},{6,7},{7,6},{8,9},{9,8},{10,11... | collective-permute-start | bytes 491528 | tf_op jit(solution)/shard_map/ppermute | solution.py:494
  2.8 3.9 %collective-permute-start = (f32[8,8,128]{2,1,0:T(8,128)S(1)}, f32[8,8,128]{2,1,0:T(8,128)S(1)}, u32[]{:S(2)}, u32[]{:S(2)}) collective-permute-start(f32[8,8,128]{2,1,0:T(8,128)S(1)} %get-tuple-element.24), channel_id=1, source_target_pairs={{0,8},{8,0},{16,24},{24,16},{1,9},{9,1},{17,25},{25,17},{2,10},{10... | collective-permute-start | bytes 98312 | tf_op jit(solution)/shard_map/ppermute | solution.py:492
  2.8 3.9 %collective-permute-start.1 = (f32[8,8,128]{2,1,0:T(8,128)S(1)}, f32[8,8,128]{2,1,0:T(8,128)S(1)}, u32[]{:S(2)}, u32[]{:S(2)}) collective-permute-start(f32[8,8,128]{2,1,0:T(8,128)S(1)} %get-tuple-element.25), channel_id=1, source_target_pairs={{0,24},{8,16},{16,8},{24,0},{1,25},{9,17},{17,9},{25,1},{2,26},{10... | collective-permute-start | bytes 98312 | tf_op jit(solution)/shard_map/ppermute | solution.py:493
  4.4 9.2 %collective-permute-start.3 = (f32[40,8,128]{2,1,0:T(8,128)S(1)}, f32[40,8,128]{2,1,0:T(8,128)S(1)}, u32[]{:S(2)}, u32[]{:S(2)}) collective-permute-start(f32[40,8,128]{2,1,0:T(8,128)S(1)} %get-tuple-element.37), channel_id=1, source_target_pairs={{1,2},{3,4},{5,6},{2,1},{4,3},{6,5},{9,10},{11,12},{13,14},{10,9},... | collective-permute-start | bytes 491528 | tf_op jit(solution)/shard_map/ppermute | solution.py:495
  7.4 6.7 %collective-permute-start.4 = (f32[7,8,128]{2,1,0:T(8,128)S(1)}, f32[7,8,128]{2,1,0:T(8,128)S(1)}, u32[]{:S(2)}, u32[]{:S(2)}) collective-permute-start(f32[7,8,128]{2,1,0:T(8,128)S(1)} %get-tuple-element.38), channel_id=1, source_target_pairs={{1,2},{3,4},{5,6},{2,1},{4,3},{6,5},{9,10},{11,12},{13,14},{10,9},... | collective-permute-start | bytes 86024 | tf_op jit(solution)/shard_map/ppermute | solution.py:498
  11.4 3.4 %collective-permute-start.5 = (f32[7,8,128]{2,1,0:T(8,128)S(1)}, f32[7,8,128]{2,1,0:T(8,128)S(1)}, u32[]{:S(2)}, u32[]{:S(2)}) collective-permute-start(f32[7,8,128]{2,1,0:T(8,128)S(1)} %get-tuple-element.39), channel_id=1, source_target_pairs={{0,24},{8,16},{16,8},{24,0},{1,25},{9,17},{17,9},{25,1},{2,26},{10... | collective-permute-start | bytes 86024 | tf_op jit(solution)/shard_map/ppermute | solution.py:499
  11.5 3.3 %collective-permute-start.6 = (f32[7,8,128]{2,1,0:T(8,128)S(1)}, f32[7,8,128]{2,1,0:T(8,128)S(1)}, u32[]{:S(2)}, u32[]{:S(2)}) collective-permute-start(f32[7,8,128]{2,1,0:T(8,128)S(1)} %get-tuple-element.40), channel_id=1, source_target_pairs={{0,8},{8,0},{16,24},{24,16},{1,9},{9,1},{17,25},{25,17},{2,10},{10... | collective-permute-start | bytes 86024 | tf_op jit(solution)/shard_map/ppermute | solution.py:500

commit v9 on v8

--- a/solution.py
+++ b/solution.py
@@ -450,9 +450,16 @@
 
     order = lax.div(lane, 2)
     is_even = lax.rem(lane, 2) == 0
+    at_edge = (order == 0) | (order == HALF - 1)
+    other = jnp.where(order == 0, CA - TWIN, order + TWIN)
+
+    def in_order(value, index):
+        return jnp.where(is_even, picked(value[:, 0], index), picked(value[:, 1], index))
+
     for low, high in ((0, OV), (OV, 8), (8, CR - OV), (CR - OV, CR)):
-        value = joined(summed_boxes(low, high - low)) + total[pl.ds(low + REACH, high - low)]
-        value = jnp.where(is_even, picked(value[:, 0], order), picked(value[:, 1], order))
+        value = summed_boxes(low, high - low)
+        first = in_order(total[pl.ds(low + REACH, high - low)], order)
+        value = first + (in_order(value, order) + jnp.where(at_edge, in_order(value, other), 0.0))
         value = value.reshape((high - low) * NZ, CA)
         for n in range(high - low):
             row = low + n

time: 18.1 us -> 17.9 us (0.989)
  no operation moved by 1% of the time
where the time goes in v9:
time: 17.9 us; the launch traced here: 17.7 us
  starting transfers between devices  10.5 us (59%)
  Pallas kernels  4.4 us (25%)
  waiting for transfers between devices  1.85 us (10%)
  other arithmetic  0.88 us (5%)
    pallas_call x5, Pallas kernels, call(): pl.pallas_call(kernel, out_shape=outs, in_specs=[vmem] * len(args), out_s...  4.4 us
    ppermute x1, starting transfers between devices, body(): far_strips = lax.ppermute(strips_far, 'row', far_pairs)  3.96 us
    ppermute x1, starting transfers between devices, body(): far = lax.ppermute(to_far, 'row', far_pairs)  2.29 us
    ppermute x1, starting transfers between devices, body(): from_other = lax.ppermute(to_other, 'aisle', other)  1.6 us
    ppermute x1, starting transfers between devices, body(): near = lax.ppermute(to_near, 'row', near_pairs)  1.58 us
    ppermute x1, starting transfers between devices, body(): near_pair = lax.ppermute(near_to_pair, 'aisle', pair)  0.95 us
    add x1, other arithmetic, body(): shift = 0.1 + 40.0 * solid.astype(jnp.float32)  0.88 us
    ppermute x1, waiting for transfers between devices, body(): near_other = lax.ppermute(near_to_other, 'aisle', other)  0.66 us
  transfers between devices with their start and end apart: 7, of which 4 were waited for; matrix products, arithmetic and copies ran while one was open for 0% of the time, Pallas kernels for 7%

profile of v9, /device:TPU:8, one launch (start us, length us, event | category | flops | bytes accessed | tf_op | source)
XLA Modules:
  0.0 17.7 jit_solution(407033430568401327)
XLA Ops:
  0.0 0.0 copy-start
  0.0 0.0 copy-start.1
  0.0 0.9 %multiply_add_fusion = f32[8,16,128]{2,1,0:T(8,128)S(1)} fusion(s32[8,16,128]{2,1,0:T(8,128)} %param.5), kind=kLoop, calls=%fused_computation | loop fusion | flops 49152 | bytes 131072 | tf_op jit(solution)/shard_map/add | solution.py:489
  0.9 0.0 copy-done
  0.9 0.0 copy-done.1
  0.9 0.3 %pack_edges.1 = (f32[3,16,8,128]{3,2,1,0:T(8,128)S(1)}, f32[8,8,128]{2,1,0:T(8,128)S(1)}, f32[8,8,128]{2,1,0:T(8,128)S(1)}, f32[40,8,128]{2,1,0:T(8,128)S(1)}, f32[40,8,128]{2,1,0:T(8,128)S(1)}) custom-call(f32[128,128]{1,0:T(8,128)S(1)} %bitcast.5, f32[128,128]{1,0:T(8,128)S(1)} %bitcast.6, f32[128,128]{1,0:T(8,128)S(1)} %bitcast.4), custom_call_target="tpu_custom_call" | custom-call | tf_op jit(solution)/shard_map/pack_edges/pallas_call | solution.py:471
  1.2 1.6 %collective-permute-start.2 = (f32[40,8,128]{2,1,0:T(8,128)S(1)}, f32[40,8,128]{2,1,0:T(8,128)S(1)}, u32[]{:S(2)}, u32[]{:S(2)}) collective-permute-start(f32[40,8,128]{2,1,0:T(8,128)S(1)} %get-tuple-element.26), channel_id=1, source_target_pairs={{0,1},{1,0},{2,3},{3,2},{4,5},{5,4},{6,7},{7,6},{8,9},{9,8},{10,11... | collective-permute-start | bytes 491528 | tf_op jit(solution)/shard_map/ppermute | solution.py:501
  2.8 0.0 collective-permute-start
  2.8 1.6 %collective-permute-start.1 = (f32[8,8,128]{2,1,0:T(8,128)S(1)}, f32[8,8,128]{2,1,0:T(8,128)S(1)}, u32[]{:S(2)}, u32[]{:S(2)}) collective-permute-start(f32[8,8,128]{2,1,0:T(8,128)S(1)} %get-tuple-element.25), channel_id=1, source_target_pairs={{0,24},{8,16},{16,8},{24,0},{1,25},{9,17},{17,9},{25,1},{2,26},{10... | collective-permute-start | bytes 98312 | tf_op jit(solution)/shard_map/ppermute | solution.py:500
  4.4 2.3 %collective-permute-start.3 = (f32[40,8,128]{2,1,0:T(8,128)S(1)}, f32[40,8,128]{2,1,0:T(8,128)S(1)}, u32[]{:S(2)}, u32[]{:S(2)}) collective-permute-start(f32[40,8,128]{2,1,0:T(8,128)S(1)} %get-tuple-element.37), channel_id=1, source_target_pairs={{1,2},{3,4},{5,6},{2,1},{4,3},{6,5},{9,10},{11,12},{13,14},{10,9},... | collective-permute-start | bytes 491528 | tf_op jit(solution)/shard_map/ppermute | solution.py:502
  6.7 0.0 collective-permute-done.from_pair
  6.7 0.0 collective-permute-done.1.from_other
  6.7 0.5 %collective-permute-done.2.near = f32[40,8,128]{2,1,0:T(8,128)S(1)} collective-permute-done((f32[40,8,128]{2,1,0:T(8,128)S(1)}, f32[40,8,128]{2,1,0:T(8,128)S(1)}, u32[]{:S(2)}, u32[]{:S(2)}) %collective-permute-start.2) | collective-permute-done | bytes 163872 | tf_op jit(solution)/shard_map/ppermute | solution.py:501
  7.2 0.2 %pack_strips.1 = (f32[16,8,128]{2,1,0:T(8,128)S(1)}, f32[7,8,128]{2,1,0:T(8,128)S(1)}, f32[7,8,128]{2,1,0:T(8,128)S(1)}, f32[7,8,128]{2,1,0:T(8,128)S(1)}) custom-call(f32[8,8,128]{2,1,0:T(8,128)S(1)} %collective-permute-done.from_pair, f32[8,8,128]{2,1,0:T(8,128)S(1)} %collective-permute-done.1.from_other, f32[40,8,128]{2,1,0:T(8,128)S(1)} %collective-permute-done.2.near), custom_call_target="tpu_custom_call" | custom-call | tf_op jit(solution)/shard_map/pack_strips/pallas_call | solution.py:471
  7.4 4.0 %collective-permute-start.4 = (f32[7,8,128]{2,1,0:T(8,128)S(1)}, f32[7,8,128]{2,1,0:T(8,128)S(1)}, u32[]{:S(2)}, u32[]{:S(2)}) collective-permute-start(f32[7,8,128]{2,1,0:T(8,128)S(1)} %get-tuple-element.38), channel_id=1, source_target_pairs={{1,2},{3,4},{5,6},{2,1},{4,3},{6,5},{9,10},{11,12},{13,14},{10,9},... | collective-permute-start | bytes 86024 | tf_op jit(solution)/shard_map/ppermute | solution.py:505
  11.4 0.1 collective-permute-start.5
  11.5 0.9 %collective-permute-start.6 = (f32[7,8,128]{2,1,0:T(8,128)S(1)}, f32[7,8,128]{2,1,0:T(8,128)S(1)}, u32[]{:S(2)}, u32[]{:S(2)}) collective-permute-start(f32[7,8,128]{2,1,0:T(8,128)S(1)} %get-tuple-element.40), channel_id=1, source_target_pairs={{0,8},{8,0},{16,24},{24,16},{1,9},{9,1},{17,25},{25,17},{2,10},{10... | collective-permute-start | bytes 86024 | tf_op jit(solution)/shard_map/ppermute | solution.py:507
  12.4 0.8 %prepare_own.1 = (f32[40,2,8,128]{3,2,1,0:T(8,128)S(1)}, f32[16,2,8,128]{3,2,1,0:T(8,128)S(1)}, f32[16,2,8,128]{3,2,1,0:T(8,128)S(1)}, f32[16,2,8,128]{3,2,1,0:T...) custom-call(f32[3,16,8,128]{3,2,1,0:T(8,128)S(1)} %get-tuple-element, ...), custom_call_target="tpu_custom_call" | custom-call | flops 2000000000 | tf_op jit(solution)/shard_map/prepare_own/pallas_call | solution.py:471
  13.3 0.3 %collective-permute-done.3.far = f32[40,8,128]{2,1,0:T(8,128)S(1)} collective-permute-done((f32[40,8,128]{2,1,0:T(8,128)S(1)}, f32[40,8,128]{2,1,0:T(8,128)S(1)}, u32[]{:S(2)}, u32[]{:S(2)}) %collective-permute-start.3) | collective-permute-done | bytes 163872 | tf_op jit(solution)/shard_map/ppermute | solution.py:502
  13.6 0.1 split_far.1.far
  13.7 0.4 %collective-permute-done.4.far_strips = f32[7,8,128]{2,1,0:T(8,128)S(1)} collective-permute-done((f32[7,8,128]{2,1,0:T(8,128)S(1)}, f32[7,8,128]{2,1,0:T(8,128)S(1)}, u32[]{:S(2)}, u32[]{:S(2)}) %collective-permute-start.4) | collective-permute-done | bytes 28704 | tf_op jit(solution)/shard_map/ppermute | solution.py:505
  14.1 0.7 %collective-permute-done.5.near_other = f32[7,8,128]{2,1,0:T(8,128)S(1)} collective-permute-done((f32[7,8,128]{2,1,0:T(8,128)S(1)}, f32[7,8,128]{2,1,0:T(8,128)S(1)}, u32[]{:S(2)}, u32[]{:S(2)}) %collective-permute-start.5) | collective-permute-done | bytes 28704 | tf_op jit(solution)/shard_map/ppermute | solution.py:506
  14.8 0.0 collective-permute-done.6.near_pair
  14.8 2.9 %solve_all.1 = f32[128,128]{1,0:T(8,128)} custom-call(f32[16,2,8,128]{3,2,1,0:T(8,128)S(1)} %get-tuple-element.28.own_rhs, f32[16,2,8,128]{3,2,1,0:T(8,128)S(1)} %get-tuple-element.29.own_cond, f32[16,2,8,128]{3,2,1,0:T(8,128)S(1)} %get-tuple-element.30.own_x, f32[16,2,8,128]{3,2,1,0:T(8,128)S(1)} %get-tuple-element.31.own_z, ...), custom_call_target="tpu_custom_call" | custom-call | tf_op jit(solution)/shard_map/solve_all/pallas_call | solution.py:471
Async XLA Ops:
  0.0 0.9 %copy-start = (f32[8,16,128]{2,1,0:T(8,128)S(1)}, f32[8,16,128]{2,1,0:T(8,128)}, u32[]{:S(2)}) copy-start(f32[8,16,128]{2,1,0:T(8,128)} %param.3) | copy-start | bytes 196612
  0.0 0.9 %copy-start.1 = (f32[8,16,128]{2,1,0:T(8,128)S(1)}, f32[8,16,128]{2,1,0:T(8,128)}, u32[]{:S(2)}) copy-start(f32[8,16,128]{2,1,0:T(8,128)} %param.4) | copy-start | bytes 196612
  1.2 6.0 %collective-permute-start.2 = (f32[40,8,128]{2,1,0:T(8,128)S(1)}, f32[40,8,128]{2,1,0:T(8,128)S(1)}, u32[]{:S(2)}, u32[]{:S(2)}) collective-permute-start(f32[40,8,128]{2,1,0:T(8,128)S(1)} %get-tuple-element.26), channel_id=1, source_target_pairs={{0,1},{1,0},{2,3},{3,2},{4,5},{5,4},{6,7},{7,6},{8,9},{9,8},{10,11... | collective-permute-start | bytes 491528 | tf_op jit(solution)/shard_map/ppermute | solution.py:501
  2.8 3.9 %collective-permute-start = (f32[8,8,128]{2,1,0:T(8,128)S(1)}, f32[8,8,128]{2,1,0:T(8,128)S(1)}, u32[]{:S(2)}, u32[]{:S(2)}) collective-permute-start(f32[8,8,128]{2,1,0:T(8,128)S(1)} %get-tuple-element.24), channel_id=1, source_target_pairs={{0,8},{8,0},{16,24},{24,16},{1,9},{9,1},{17,25},{25,17},{2,10},{10... | collective-permute-start | bytes 98312 | tf_op jit(solution)/shard_map/ppermute | solution.py:499
  2.8 3.9 %collective-permute-start.1 = (f32[8,8,128]{2,1,0:T(8,128)S(1)}, f32[8,8,128]{2,1,0:T(8,128)S(1)}, u32[]{:S(2)}, u32[]{:S(2)}) collective-permute-start(f32[8,8,128]{2,1,0:T(8,128)S(1)} %get-tuple-element.25), channel_id=1, source_target_pairs={{0,24},{8,16},{16,8},{24,0},{1,25},{9,17},{17,9},{25,1},{2,26},{10... | collective-permute-start | bytes 98312 | tf_op jit(solution)/shard_map/ppermute | solution.py:500
  4.4 9.2 %collective-permute-start.3 = (f32[40,8,128]{2,1,0:T(8,128)S(1)}, f32[40,8,128]{2,1,0:T(8,128)S(1)}, u32[]{:S(2)}, u32[]{:S(2)}) collective-permute-start(f32[40,8,128]{2,1,0:T(8,128)S(1)} %get-tuple-element.37), channel_id=1, source_target_pairs={{1,2},{3,4},{5,6},{2,1},{4,3},{6,5},{9,10},{11,12},{13,14},{10,9},... | collective-permute-start | bytes 491528 | tf_op jit(solution)/shard_map/ppermute | solution.py:502
  7.4 6.7 %collective-permute-start.4 = (f32[7,8,128]{2,1,0:T(8,128)S(1)}, f32[7,8,128]{2,1,0:T(8,128)S(1)}, u32[]{:S(2)}, u32[]{:S(2)}) collective-permute-start(f32[7,8,128]{2,1,0:T(8,128)S(1)} %get-tuple-element.38), channel_id=1, source_target_pairs={{1,2},{3,4},{5,6},{2,1},{4,3},{6,5},{9,10},{11,12},{13,14},{10,9},... | collective-permute-start | bytes 86024 | tf_op jit(solution)/shard_map/ppermute | solution.py:505
  11.4 3.4 %collective-permute-start.5 = (f32[7,8,128]{2,1,0:T(8,128)S(1)}, f32[7,8,128]{2,1,0:T(8,128)S(1)}, u32[]{:S(2)}, u32[]{:S(2)}) collective-permute-start(f32[7,8,128]{2,1,0:T(8,128)S(1)} %get-tuple-element.39), channel_id=1, source_target_pairs={{0,24},{8,16},{16,8},{24,0},{1,25},{9,17},{17,9},{25,1},{2,26},{10... | collective-permute-start | bytes 86024 | tf_op jit(solution)/shard_map/ppermute | solution.py:506
  11.5 3.3 %collective-permute-start.6 = (f32[7,8,128]{2,1,0:T(8,128)S(1)}, f32[7,8,128]{2,1,0:T(8,128)S(1)}, u32[]{:S(2)}, u32[]{:S(2)}) collective-permute-start(f32[7,8,128]{2,1,0:T(8,128)S(1)} %get-tuple-element.40), channel_id=1, source_target_pairs={{0,8},{8,0},{16,24},{24,16},{1,9},{9,1},{17,25},{25,17},{2,10},{10... | collective-permute-start | bytes 86024 | tf_op jit(solution)/shard_map/ppermute | solution.py:507
